TPU v7x, 256 devices: a whole 4x4x8 slice. The times are simulated.
256 devices in a mesh: dp: 64 (over z, y, core), mp: 4 (over x).
Axes of the slice: x: 4, y: 4, z: 8, core: 2. Of those that a mesh axis runs over, the one named last changes fastest.
Arguments:
- texts: bfloat16 [1024, 35, 768], P('dp'), may hold values from -6 to 6
- query_weight: bfloat16 [768, 768], P('mp'), may hold values from -0.21875 to 0.21875
- patch_key_value: bfloat16 [256, 12, 577, 128], P('dp', 'mp'), may hold values from -300 to 300
- grad_out: bfloat16 [1024, 4, 35, 768], P('dp'), may hold values from -6 to 6
- negatives: int32 [1024, 3], P('dp'), may hold values from 0 to 255, as said below
Outputs:
- text_grad: bfloat16 [1024, 35, 768], P(('dp', 'mp'))
- weight_grad: float32 [768, 768], P('mp')
- key_value_grad: bfloat16 [256, 12, 577, 128], P('dp', 'mp')
Inputs may be any that keep to these rules, and one draw needn't show every extreme that they name: Never an image whose index // 4 equals the text's index // 16. Among the negatives of the texts of one index of dp, at most 2 name images of any one index; some pair of indices reaches 2.
All inputs are finite; a program needn't handle non-finite values.
Results may differ from a plain program's by a relative error of at most 0.03.
The roundings to bfloat16 on the way count: a program that leaves them out, or rounds other values in their place, can miss the bound.
Values may be sent and summed in bfloat16 or wider, within the bound.
No kernel may reach another device: no remote copies, remote signals or barrier semaphores. Data moves between devices by JAX's collectives and lax.ppermute only.
A program may use at most 192 MiB of HBM per device.

v0:
```python
import math

import jax
import jax.numpy as jnp
from jax import lax
from jax.sharding import PartitionSpec as P

HEAD_SIZE = 64
NEG = 3


def pair_grads(query, cotangent, memory):
    scale = HEAD_SIZE ** (-0.5)
    q4 = query.reshape(query.shape[:-1] + (-1, HEAD_SIZE))
    g4 = cotangent.reshape(cotangent.shape[:-1] + (-1, HEAD_SIZE))
    k4 = memory[..., :HEAD_SIZE]
    v4 = memory[..., HEAD_SIZE:]
    scores = jnp.einsum("blhd,bhkd->bhlk", q4, k4, preferred_element_type=jnp.float32) * scale
    probs_f = jax.nn.softmax(scores, axis=-1)
    probs = probs_f.astype(jnp.bfloat16)
    dprobs = jnp.einsum("blhd,bhkd->bhlk", g4, v4, preferred_element_type=jnp.float32)
    center = jnp.sum(probs_f * dprobs, axis=-1, keepdims=True)
    dscores = (probs_f * (dprobs - center) * scale).astype(jnp.bfloat16)
    pair_dv = jnp.einsum("bhlk,blhd->bhkd", probs, g4, preferred_element_type=jnp.float32)
    pair_dq = jnp.einsum("bhlk,bhkd->blhd", dscores, k4, preferred_element_type=jnp.float32)
    pair_dk = jnp.einsum("bhlk,blhd->bhkd", dscores, q4, preferred_element_type=jnp.float32)
    pair_dq = pair_dq.reshape(pair_dq.shape[:2] + (-1,))
    return (pair_dq, jnp.concatenate([pair_dk, pair_dv], axis=-1))


def serve(query_rows, grad_rows, image_ids, patch_key_value):
    count, length, width = query_rows.shape
    size = math.gcd(count, 16)
    steps = count // size

    def visit(memory_acc, item):
        query_tile, g_block, ids = item
        memory = jnp.take(patch_key_value, ids, axis=0)
        pair_dq, pair_dkv = pair_grads(query_tile, g_block, memory)
        memory_acc = memory_acc.at[ids].add(pair_dkv)
        return (memory_acc, pair_dq)

    start = jnp.zeros(patch_key_value.shape, jnp.float32)
    items = (
        query_rows.reshape(steps, size, length, width),
        grad_rows.reshape(steps, size, length, width),
        image_ids.reshape(steps, size),
    )
    memory_acc, dquery = lax.scan(visit, start, items)
    return (dquery.reshape(count, length, width), memory_acc)


def per_device(texts, query_weight, patch_key_value, grad_out, negatives):
    owning_devices = lax.axis_size("dp")
    texts_here, length, _ = texts.shape
    local_images = patch_key_value.shape[0]
    captions = texts_here // local_images
    wanted = NEG * texts_here
    capacity = 2 * max(1, wanted // owning_devices)
    slots_all = owning_devices * capacity
    width = query_weight.shape[0]
    flat_text = texts.reshape(texts_here * length, -1)
    query = lax.dot_general(
        flat_text, query_weight, (((1,), (1,)), ((), ())), preferred_element_type=jnp.float32
    )
    query = query.astype(jnp.bfloat16).reshape(texts_here, length, width)
    grad_cols = lax.dynamic_slice_in_dim(grad_out, lax.axis_index("mp") * width, width, 3)
    flat_neg = negatives.reshape(-1)
    owner = flat_neg // local_images
    local_id = flat_neg % local_images
    owner_hot = (owner[:, None] == jnp.arange(owning_devices, dtype=jnp.int32)[None, :]).astype(
        jnp.int32
    )
    earlier = jnp.cumsum(owner_hot, axis=0) - owner_hot
    rank = jnp.sum(earlier * owner_hot, axis=1)
    slot = owner * capacity + rank
    placed = slot[None, :] == jnp.arange(slots_all, dtype=jnp.int32)[:, None]
    place = placed.astype(jnp.bfloat16)
    place_text = jnp.sum(placed.reshape(slots_all, texts_here, NEG), axis=2).astype(jnp.bfloat16)
    send_query = jnp.dot(
        place_text, query.reshape(texts_here, -1), preferred_element_type=jnp.float32
    )
    send_query = send_query.astype(jnp.bfloat16).reshape(owning_devices, capacity, length, width)
    send_grad = jnp.dot(
        place, grad_cols[:, 1:].reshape(wanted, -1), preferred_element_type=jnp.float32
    )
    send_grad = send_grad.astype(jnp.bfloat16).reshape(owning_devices, capacity, length, width)
    send_pair = jnp.concatenate([send_query, send_grad], axis=3)
    send_id = jnp.sum(jnp.where(placed, local_id[None, :], 0), axis=1)
    send_id = send_id.astype(jnp.bfloat16).reshape(owning_devices, capacity)
    own_ids = jnp.arange(texts_here, dtype=jnp.int32) // captions
    own_dq, own_dkv = serve(query, grad_cols[:, 0], own_ids, patch_key_value)
    got_pair, got_id = (
        lax.all_to_all(send_pair, "dp", split_axis=0, concat_axis=0, tiled=True),
        lax.all_to_all(send_id, "dp", split_axis=0, concat_axis=0, tiled=True),
    )
    remote_query_grad, far_dkv = serve(
        got_pair[..., :width].reshape(-1, length, width),
        got_pair[..., width:].reshape(-1, length, width),
        got_id.reshape(-1).astype(jnp.int32),
        patch_key_value,
    )
    returned = lax.all_to_all(
        remote_query_grad.reshape(owning_devices, capacity, length, width),
        "dp",
        split_axis=0,
        concat_axis=0,
        tiled=True,
    )
    returned = returned.reshape(slots_all, length, width)
    per_request = jnp.take(returned, slot, axis=0).reshape(texts_here, NEG, length, width)
    dquery = (own_dq + jnp.sum(per_request, axis=1)).astype(jnp.bfloat16)
    flat_dq = dquery.reshape(texts_here * length, width)
    weight_local = lax.dot_general(
        flat_dq, flat_text, (((0,), (0,)), ((), ())), preferred_element_type=jnp.float32
    )
    weight_grad = lax.psum(weight_local, "dp")
    text_term = jnp.dot(flat_dq, query_weight, preferred_element_type=jnp.float32)
    text_grad = lax.psum_scatter(
        text_term.reshape(texts_here, length, -1), "mp", scatter_dimension=0, tiled=True
    )
    key_value_grad = (own_dkv + far_dkv).astype(jnp.bfloat16)
    return (text_grad.astype(jnp.bfloat16), weight_grad, key_value_grad)


def solution(mesh):
    in_specs = (
        P("dp", None, None),
        P("mp", None),
        P("dp", "mp", None, None),
        P("dp", None, None, None),
        P("dp", None),
    )
    out_specs = (P(("dp", "mp"), None, None), P("mp", None), P("dp", "mp", None, None))
    return jax.shard_map(
        per_device, mesh=mesh, in_specs=in_specs, out_specs=out_specs, check_vma=False
    )
```

profile of v0, /device:TPU:1, one launch (start us, length us, event | category | flops | bytes accessed | tf_op | source)
XLA Modules:
  0.0 1688.8 jit_solution(14444763081385348824)
XLA Ops:
  10.3 13.2 all-to-all-start
  72.5 10.5 all-to-all-start.1
  86.1 75.7 %all-to-all-done.1 = bf16[64,2,35,384]{3,1,2,0:T(2,128)(2,1)} async-done(((bf16[64,2,35,384]{3,1,2,0:T(2,128)(2,1)}), bf16[64,2,35,384]{3,1,2,0:T(2,128)(2,1)}, u32[]{:S(2)}, u32[]{:S(2)}) %all-to-all-start.1) | async-done | bytes 3440672 | tf_op jit(solution)/shard_map/all_to_all | solution.py:94
  193.6 1130.5 %while.2 = (s32[]{:T(128)}, f32[4,3,577,128]{3,2,1,0:T(8,128)}, f32[8,16,35,192]{3,1,0,2:T(8,128)}, s32[8,16]{1,0:T(8,128)S(1)}, bf16[8,16,35,192]{3,1,0,2:T(8,1...) while((s32[]{:T(128)}, f32[4,3,577,128]{3,2,1,0:T(8,128)}, ...), condition=%wide.region_12.14_spmd, body=%wide.region_7.13_spmd.sunk | while | flops 650419136 | bytes 279351616 | solution.py:49
  206.2 10.2 copy.290
  233.4 19.7 %fusion.128 = f32[16,35,3,64]{3,1,2,0:T(8,128)} fusion(f32[16,3,35,577]{3,2,1,0:T(8,128)} %fusion.126, bf16[16,3,577,128]{2,3,1,0:T(8,128)(2,1)} %broadcast_select_fusion.3, f32[16,3,35,577]{3,2,1,0:T(8,128)} %get-tuple-element.209, f32[16,3,35]{2,1,0:T(4,128)S(1)} %get-tuple-element.210), kind=kOutput, calls=%fused_computation.26.clone.1 | convolution fusion | flops 130865856 | bytes 24088576 | tf_op jit(solution)/shard_map/while/body/eval_jaxpr/bhlk,bhkd->blhd/dot_general | solution.py:25
  258.0 20.3 %fusion.127 = f32[16,3,577,64]{2,3,1,0:T(8,128)} fusion(f32[16,3,35,577]{3,2,1,0:T(8,128)} %fusion.126, bf16[16,35,3,64]{3,2,0,1:T(4,128)(2,1)} %reshape.419, f32[16,3,35,577]{3,2,1,0:T(8,128)} %get-tuple-element.209, f32[16,3,35]{2,1,0:T(4,128)S(1)} %get-tuple-element.210), kind=kOutput, calls=%fused_computation.25.clone.1 | convolution fusion | flops 130865856 | bytes 15066816 | tf_op jit(solution)/shard_map/while/body/eval_jaxpr/bhlk,blhd->bhkd/dot_general | solution.py:26
  288.9 15.2 copy.291
  304.1 29.5 %scatter_fusion = f32[4,3,577,128]{3,2,1,0:T(8,128)} fusion(f32[4,3,577,128]{3,2,1,0:T(8,128)} %get-tuple-element.220, s32[16]{0:T(128)S(1)} %fusion.122, f32[16,3,577,128]{3,2,1,0:T(8,128)} %copy.291), kind=kCustom, calls=%fused_computation.3.clone.1 | custom fusion | flops 3545088 | bytes 42541120 | tf_op jit(solution)/shard_map/while/body/eval_jaxpr/scatter-add | solution.py:40
  375.0 19.7 %fusion.128 = f32[16,35,3,64]{3,1,2,0:T(8,128)} fusion(f32[16,3,35,577]{3,2,1,0:T(8,128)} %fusion.126, bf16[16,3,577,128]{2,3,1,0:T(8,128)(2,1)} %broadcast_select_fusion.3, f32[16,3,35,577]{3,2,1,0:T(8,128)} %get-tuple-element.209, f32[16,3,35]{2,1,0:T(4,128)S(1)} %get-tuple-element.210), kind=kOutput, calls=%fused_computation.26.clone.1 | convolution fusion | flops 130865856 | bytes 24088576 | tf_op jit(solution)/shard_map/while/body/eval_jaxpr/bhlk,bhkd->blhd/dot_general | solution.py:25
  399.5 20.3 %fusion.127 = f32[16,3,577,64]{2,3,1,0:T(8,128)} fusion(f32[16,3,35,577]{3,2,1,0:T(8,128)} %fusion.126, bf16[16,35,3,64]{3,2,0,1:T(4,128)(2,1)} %reshape.419, f32[16,3,35,577]{3,2,1,0:T(8,128)} %get-tuple-element.209, f32[16,3,35]{2,1,0:T(4,128)S(1)} %get-tuple-element.210), kind=kOutput, calls=%fused_computation.25.clone.1 | convolution fusion | flops 130865856 | bytes 15066816 | tf_op jit(solution)/shard_map/while/body/eval_jaxpr/bhlk,blhd->bhkd/dot_general | solution.py:26
  430.5 15.2 copy.291
  445.6 28.9 %scatter_fusion = f32[4,3,577,128]{3,2,1,0:T(8,128)} fusion(f32[4,3,577,128]{3,2,1,0:T(8,128)} %get-tuple-element.220, s32[16]{0:T(128)S(1)} %fusion.122, f32[16,3,577,128]{3,2,1,0:T(8,128)} %copy.291), kind=kCustom, calls=%fused_computation.3.clone.1 | custom fusion | flops 3545088 | bytes 42541120 | tf_op jit(solution)/shard_map/while/body/eval_jaxpr/scatter-add | solution.py:40
  488.6 10.2 copy.290
  515.8 19.7 %fusion.128 = f32[16,35,3,64]{3,1,2,0:T(8,128)} fusion(f32[16,3,35,577]{3,2,1,0:T(8,128)} %fusion.126, bf16[16,3,577,128]{2,3,1,0:T(8,128)(2,1)} %broadcast_select_fusion.3, f32[16,3,35,577]{3,2,1,0:T(8,128)} %get-tuple-element.209, f32[16,3,35]{2,1,0:T(4,128)S(1)} %get-tuple-element.210), kind=kOutput, calls=%fused_computation.26.clone.1 | convolution fusion | flops 130865856 | bytes 24088576 | tf_op jit(solution)/shard_map/while/body/eval_jaxpr/bhlk,bhkd->blhd/dot_general | solution.py:25
  540.4 20.3 %fusion.127 = f32[16,3,577,64]{2,3,1,0:T(8,128)} fusion(f32[16,3,35,577]{3,2,1,0:T(8,128)} %fusion.126, bf16[16,35,3,64]{3,2,0,1:T(4,128)(2,1)} %reshape.419, f32[16,3,35,577]{3,2,1,0:T(8,128)} %get-tuple-element.209, f32[16,3,35]{2,1,0:T(4,128)S(1)} %get-tuple-element.210), kind=kOutput, calls=%fused_computation.25.clone.1 | convolution fusion | flops 130865856 | bytes 15066816 | tf_op jit(solution)/shard_map/while/body/eval_jaxpr/bhlk,blhd->bhkd/dot_general | solution.py:26
  571.3 15.2 copy.291
  586.5 29.5 %scatter_fusion = f32[4,3,577,128]{3,2,1,0:T(8,128)} fusion(f32[4,3,577,128]{3,2,1,0:T(8,128)} %get-tuple-element.220, s32[16]{0:T(128)S(1)} %fusion.122, f32[16,3,577,128]{3,2,1,0:T(8,128)} %copy.291), kind=kCustom, calls=%fused_computation.3.clone.1 | custom fusion | flops 3545088 | bytes 42541120 | tf_op jit(solution)/shard_map/while/body/eval_jaxpr/scatter-add | solution.py:40
  657.4 19.7 %fusion.128 = f32[16,35,3,64]{3,1,2,0:T(8,128)} fusion(f32[16,3,35,577]{3,2,1,0:T(8,128)} %fusion.126, bf16[16,3,577,128]{2,3,1,0:T(8,128)(2,1)} %broadcast_select_fusion.3, f32[16,3,35,577]{3,2,1,0:T(8,128)} %get-tuple-element.209, f32[16,3,35]{2,1,0:T(4,128)S(1)} %get-tuple-element.210), kind=kOutput, calls=%fused_computation.26.clone.1 | convolution fusion | flops 130865856 | bytes 24088576 | tf_op jit(solution)/shard_map/while/body/eval_jaxpr/bhlk,bhkd->blhd/dot_general | solution.py:25
  681.9 20.3 %fusion.127 = f32[16,3,577,64]{2,3,1,0:T(8,128)} fusion(f32[16,3,35,577]{3,2,1,0:T(8,128)} %fusion.126, bf16[16,35,3,64]{3,2,0,1:T(4,128)(2,1)} %reshape.419, f32[16,3,35,577]{3,2,1,0:T(8,128)} %get-tuple-element.209, f32[16,3,35]{2,1,0:T(4,128)S(1)} %get-tuple-element.210), kind=kOutput, calls=%fused_computation.25.clone.1 | convolution fusion | flops 130865856 | bytes 15066816 | tf_op jit(solution)/shard_map/while/body/eval_jaxpr/bhlk,blhd->bhkd/dot_general | solution.py:26
  712.9 15.2 copy.291
  728.1 29.2 %scatter_fusion = f32[4,3,577,128]{3,2,1,0:T(8,128)} fusion(f32[4,3,577,128]{3,2,1,0:T(8,128)} %get-tuple-element.220, s32[16]{0:T(128)S(1)} %fusion.122, f32[16,3,577,128]{3,2,1,0:T(8,128)} %copy.291), kind=kCustom, calls=%fused_computation.3.clone.1 | custom fusion | flops 3545088 | bytes 42541120 | tf_op jit(solution)/shard_map/while/body/eval_jaxpr/scatter-add | solution.py:40
  798.7 19.7 %fusion.128 = f32[16,35,3,64]{3,1,2,0:T(8,128)} fusion(f32[16,3,35,577]{3,2,1,0:T(8,128)} %fusion.126, bf16[16,3,577,128]{2,3,1,0:T(8,128)(2,1)} %broadcast_select_fusion.3, f32[16,3,35,577]{3,2,1,0:T(8,128)} %get-tuple-element.209, f32[16,3,35]{2,1,0:T(4,128)S(1)} %get-tuple-element.210), kind=kOutput, calls=%fused_computation.26.clone.1 | convolution fusion | flops 130865856 | bytes 24088576 | tf_op jit(solution)/shard_map/while/body/eval_jaxpr/bhlk,bhkd->blhd/dot_general | solution.py:25
  823.2 20.3 %fusion.127 = f32[16,3,577,64]{2,3,1,0:T(8,128)} fusion(f32[16,3,35,577]{3,2,1,0:T(8,128)} %fusion.126, bf16[16,35,3,64]{3,2,0,1:T(4,128)(2,1)} %reshape.419, f32[16,3,35,577]{3,2,1,0:T(8,128)} %get-tuple-element.209, f32[16,3,35]{2,1,0:T(4,128)S(1)} %get-tuple-element.210), kind=kOutput, calls=%fused_computation.25.clone.1 | convolution fusion | flops 130865856 | bytes 15066816 | tf_op jit(solution)/shard_map/while/body/eval_jaxpr/bhlk,blhd->bhkd/dot_general | solution.py:26
  854.2 15.2 copy.291
  869.3 29.5 %scatter_fusion = f32[4,3,577,128]{3,2,1,0:T(8,128)} fusion(f32[4,3,577,128]{3,2,1,0:T(8,128)} %get-tuple-element.220, s32[16]{0:T(128)S(1)} %fusion.122, f32[16,3,577,128]{3,2,1,0:T(8,128)} %copy.291), kind=kCustom, calls=%fused_computation.3.clone.1 | custom fusion | flops 3545088 | bytes 42541120 | tf_op jit(solution)/shard_map/while/body/eval_jaxpr/scatter-add | solution.py:40
  940.2 19.7 %fusion.128 = f32[16,35,3,64]{3,1,2,0:T(8,128)} fusion(f32[16,3,35,577]{3,2,1,0:T(8,128)} %fusion.126, bf16[16,3,577,128]{2,3,1,0:T(8,128)(2,1)} %broadcast_select_fusion.3, f32[16,3,35,577]{3,2,1,0:T(8,128)} %get-tuple-element.209, f32[16,3,35]{2,1,0:T(4,128)S(1)} %get-tuple-element.210), kind=kOutput, calls=%fused_computation.26.clone.1 | convolution fusion | flops 130865856 | bytes 24088576 | tf_op jit(solution)/shard_map/while/body/eval_jaxpr/bhlk,bhkd->blhd/dot_general | solution.py:25
  964.8 20.3 %fusion.127 = f32[16,3,577,64]{2,3,1,0:T(8,128)} fusion(f32[16,3,35,577]{3,2,1,0:T(8,128)} %fusion.126, bf16[16,35,3,64]{3,2,0,1:T(4,128)(2,1)} %reshape.419, f32[16,3,35,577]{3,2,1,0:T(8,128)} %get-tuple-element.209, f32[16,3,35]{2,1,0:T(4,128)S(1)} %get-tuple-element.210), kind=kOutput, calls=%fused_computation.25.clone.1 | convolution fusion | flops 130865856 | bytes 15066816 | tf_op jit(solution)/shard_map/while/body/eval_jaxpr/bhlk,blhd->bhkd/dot_general | solution.py:26
  995.7 15.2 copy.291
  1010.9 28.9 %scatter_fusion = f32[4,3,577,128]{3,2,1,0:T(8,128)} fusion(f32[4,3,577,128]{3,2,1,0:T(8,128)} %get-tuple-element.220, s32[16]{0:T(128)S(1)} %fusion.122, f32[16,3,577,128]{3,2,1,0:T(8,128)} %copy.291), kind=kCustom, calls=%fused_computation.3.clone.1 | custom fusion | flops 3545088 | bytes 42541120 | tf_op jit(solution)/shard_map/while/body/eval_jaxpr/scatter-add | solution.py:40
  1081.2 19.7 %fusion.128 = f32[16,35,3,64]{3,1,2,0:T(8,128)} fusion(f32[16,3,35,577]{3,2,1,0:T(8,128)} %fusion.126, bf16[16,3,577,128]{2,3,1,0:T(8,128)(2,1)} %broadcast_select_fusion.3, f32[16,3,35,577]{3,2,1,0:T(8,128)} %get-tuple-element.209, f32[16,3,35]{2,1,0:T(4,128)S(1)} %get-tuple-element.210), kind=kOutput, calls=%fused_computation.26.clone.1 | convolution fusion | flops 130865856 | bytes 24088576 | tf_op jit(solution)/shard_map/while/body/eval_jaxpr/bhlk,bhkd->blhd/dot_general | solution.py:25
  1105.7 20.3 %fusion.127 = f32[16,3,577,64]{2,3,1,0:T(8,128)} fusion(f32[16,3,35,577]{3,2,1,0:T(8,128)} %fusion.126, bf16[16,35,3,64]{3,2,0,1:T(4,128)(2,1)} %reshape.419, f32[16,3,35,577]{3,2,1,0:T(8,128)} %get-tuple-element.209, f32[16,3,35]{2,1,0:T(4,128)S(1)} %get-tuple-element.210), kind=kOutput, calls=%fused_computation.25.clone.1 | convolution fusion | flops 130865856 | bytes 15066816 | tf_op jit(solution)/shard_map/while/body/eval_jaxpr/bhlk,blhd->bhkd/dot_general | solution.py:26
  1136.7 15.2 copy.291
  1151.8 29.2 %scatter_fusion = f32[4,3,577,128]{3,2,1,0:T(8,128)} fusion(f32[4,3,577,128]{3,2,1,0:T(8,128)} %get-tuple-element.220, s32[16]{0:T(128)S(1)} %fusion.122, f32[16,3,577,128]{3,2,1,0:T(8,128)} %copy.291), kind=kCustom, calls=%fused_computation.3.clone.1 | custom fusion | flops 3545088 | bytes 42541120 | tf_op jit(solution)/shard_map/while/body/eval_jaxpr/scatter-add | solution.py:40
  1222.4 19.7 %fusion.128 = f32[16,35,3,64]{3,1,2,0:T(8,128)} fusion(f32[16,3,35,577]{3,2,1,0:T(8,128)} %fusion.126, bf16[16,3,577,128]{2,3,1,0:T(8,128)(2,1)} %broadcast_select_fusion.3, f32[16,3,35,577]{3,2,1,0:T(8,128)} %get-tuple-element.209, f32[16,3,35]{2,1,0:T(4,128)S(1)} %get-tuple-element.210), kind=kOutput, calls=%fused_computation.26.clone.1 | convolution fusion | flops 130865856 | bytes 24088576 | tf_op jit(solution)/shard_map/while/body/eval_jaxpr/bhlk,bhkd->blhd/dot_general | solution.py:25
  1247.0 20.3 %fusion.127 = f32[16,3,577,64]{2,3,1,0:T(8,128)} fusion(f32[16,3,35,577]{3,2,1,0:T(8,128)} %fusion.126, bf16[16,35,3,64]{3,2,0,1:T(4,128)(2,1)} %reshape.419, f32[16,3,35,577]{3,2,1,0:T(8,128)} %get-tuple-element.209, f32[16,3,35]{2,1,0:T(4,128)S(1)} %get-tuple-element.210), kind=kOutput, calls=%fused_computation.25.clone.1 | convolution fusion | flops 130865856 | bytes 15066816 | tf_op jit(solution)/shard_map/while/body/eval_jaxpr/bhlk,blhd->bhkd/dot_general | solution.py:26
  1277.9 15.2 copy.291
  1293.1 28.9 %scatter_fusion = f32[4,3,577,128]{3,2,1,0:T(8,128)} fusion(f32[4,3,577,128]{3,2,1,0:T(8,128)} %get-tuple-element.220, s32[16]{0:T(128)S(1)} %fusion.122, f32[16,3,577,128]{3,2,1,0:T(8,128)} %copy.291), kind=kCustom, calls=%fused_computation.3.clone.1 | custom fusion | flops 3545088 | bytes 42541120 | tf_op jit(solution)/shard_map/while/body/eval_jaxpr/scatter-add | solution.py:40
  1336.6 15.8 all-to-all-start.2
  1359.6 20.2 %gather_fusion.2 = bf16[16,3,577,128]{3,0,2,1:T(8,128)(2,1)} fusion(bf16[4,3,577,128]{3,0,2,1:T(4,128)(2,1)} %param.11, s32[1024]{0:T(1024)S(1)} %pad_clamp_fusion.2), kind=kCustom, calls=%fused_computation.1.clone | custom fusion | bytes 14180416 | tf_op jit(solution)/shard_map/while/body/eval_jaxpr/jit(_take)/gather | solution.py:38
  1379.8 11.1 copy.212
  1407.9 20.0 %fusion.59 = f32[16,35,3,64]{3,1,2,0:T(8,128)} fusion(f32[16,3,35,577]{3,2,1,0:T(8,128)} %fusion.41, bf16[16,3,577,128]{2,3,1,0:T(8,128)(2,1)} %broadcast_select_fusion.1, f32[16,3,35,577]{3,2,1,0:T(8,128)} %get-tuple-element.155, f32[16,3,35]{2,1,0:T(4,128)S(1)} %get-tuple-element.154), kind=kOutput, calls=%fused_computation.70 | convolution fusion | flops 130865856 | bytes 24088576 | tf_op jit(solution)/shard_map/while/body/eval_jaxpr/bhlk,bhkd->blhd/dot_general | solution.py:25
  1432.8 21.9 %all-to-all-done.2 = f32[64,2,35,192]{3,1,2,0:T(2,128)} async-done(((f32[64,2,35,192]{3,1,2,0:T(2,128)}), f32[64,2,35,192]{3,1,2,0:T(2,128)}, u32[]{:S(2)}, u32[]{:S(2)}) %all-to-all-start.2) | async-done | bytes 3440672 | tf_op jit(solution)/shard_map/all_to_all | solution.py:103
  1471.2 20.7 %fusion.55 = f32[16,3,577,64]{2,3,1,0:T(8,128)} fusion(f32[16,3,35,577]{3,2,1,0:T(8,128)} %fusion.41, bf16[16,35,3,64]{3,2,1,0:T(4,128)(2,1)} %reshape.340, f32[16,3,35,577]{3,2,1,0:T(8,128)} %get-tuple-element.155, f32[16,3,35]{2,1,0:T(4,128)S(1)} %get-tuple-element.154), kind=kOutput, calls=%fused_computation.68 | convolution fusion | flops 130865856 | bytes 15066816 | tf_op jit(solution)/shard_map/while/body/eval_jaxpr/bhlk,blhd->bhkd/dot_general | solution.py:26
  1500.4 11.1 pad_maximum_fusion.1
  1511.5 15.2 copy.245
  1526.7 28.8 %scatter_fusion.1 = f32[4,3,577,128]{3,2,1,0:T(8,128)} fusion(f32[4,3,577,128]{3,2,1,0:T(8,128)} %get-tuple-element.64, s32[16]{0:T(128)S(1)} %fusion.77, f32[16,3,577,128]{3,2,1,0:T(8,128)} %copy.245), kind=kCustom, calls=%fused_computation.4 | custom fusion | flops 3545088 | bytes 42541120 | tf_op jit(solution)/shard_map/while/body/eval_jaxpr/scatter-add | solution.py:40
  1561.5 117.8 %all-reduce.2.cloned.1.call-done = f32[192,768]{1,0:T(8,128)} async-done(((f32[192,768]{1,0:T(8,128)}), f32[192,768]{1,0:T(8,128)}) %all-reduce.2.cloned.1.call-update) | async-done | bytes 589840 | tf_op jit(solution)/shard_map/psum | solution.py:117
  (298 shorter events, 595.3 us)
Async XLA Ops:
  8.0 27.2 %copy-start = (bf16[16,4,35,768]{3,1,2,0:T(4,128)(2,1)S(1)}, bf16[16,4,35,768]{3,1,2,0:T(4,128)(2,1)}, u32[]{:S(2)}) copy-start(bf16[16,4,35,768]{3,1,2,0:T(4,128)(2,1)} %param.12) | copy-start | bytes 10321924
  8.9 28.6 %copy-start.11 = (s32[16,3]{1,0:T(8,128)}, s32[16,3]{1,0:T(8,128)S(1)}, u32[]{:S(2)}) copy-start(s32[16,3]{1,0:T(8,128)S(1)} %copy.219) | copy-start | bytes 580
  9.4 14.2 copy-start.14
  10.3 62.2 %all-to-all-start = ((bf16[64,1,2]{2,1,0:T(2,128)(2,1)}), bf16[64,1,2]{2,1,0:T(2,128)(2,1)S(1)}, u32[]{:S(2)}, u32[]{:S(2)}) async-start(bf16[64,1,2]{2,1,0:T(2,128)(2,1)} %convert_element_type.81), calls=%async_computation | async-start | bytes 65536 | tf_op jit(solution)/shard_map/all_to_all | solution.py:95
  72.5 89.3 %all-to-all-start.1 = ((bf16[64,2,35,384]{3,1,2,0:T(2,128)(2,1)}), bf16[64,2,35,384]{3,1,2,0:T(2,128)(2,1)}, u32[]{:S(2)}, u32[]{:S(2)}) async-start(bf16[64,2,35,384]{3,1,2,0:T(2,128)(2,1)} %copy.230), calls=%async_computation.1 | async-start | bytes 6881280 | tf_op jit(solution)/shard_map/all_to_all | solution.py:94
  216.4 7.3 copy-start.3
  223.6 5.5 copy-start.1
  223.6 5.5 copy-start.4
  278.3 4.9 copy-start.2
  357.9 7.3 copy-start.3
  365.2 5.5 copy-start.1
  365.2 5.5 copy-start.4
  419.8 4.9 copy-start.2
  498.8 7.3 copy-start.3
  506.0 5.5 copy-start.1
  506.0 5.5 copy-start.4
  560.6 4.9 copy-start.2
  640.3 7.3 copy-start.3
  647.6 5.5 copy-start.1
  647.6 5.5 copy-start.4
  702.2 4.9 copy-start.2
  781.6 7.3 copy-start.3
  788.9 5.5 copy-start.1
  788.9 5.5 copy-start.4
  843.5 4.9 copy-start.2
  923.1 7.3 copy-start.3
  930.4 5.5 copy-start.1
  930.4 5.5 copy-start.4
  985.0 4.9 copy-start.2
  1064.1 7.3 copy-start.3
  1071.4 5.5 copy-start.1
  1071.4 5.5 copy-start.4
  1126.0 4.9 copy-start.2
  1205.3 7.3 copy-start.3
  1212.6 5.5 copy-start.1
  1212.6 5.5 copy-start.4
  1267.2 4.9 copy-start.2
  1336.6 15.9 copy-start.12
  1336.6 118.2 %all-to-all-start.2 = ((f32[64,2,35,192]{3,1,2,0:T(2,128)}), f32[64,2,35,192]{3,1,2,0:T(2,128)}, u32[]{:S(2)}, u32[]{:S(2)}) async-start(f32[64,2,35,192]{3,1,2,0:T(2,128)} %copy.237), calls=%async_computation.2 | async-start | bytes 9175040 | tf_op jit(solution)/shard_map/all_to_all | solution.py:103
  1352.4 207.3 %reduce-scatter.2.cloned.1.call-start = ((), (), s32[]{:S(2)}) async-start(), calls=%async_computation.4 | async-start | bytes 2457600 | tf_op jit(solution)/shard_map/reduce_scatter | solution.py:119
  1391.0 7.3 copy-start.6
  1398.2 5.5 copy-start.5
  1398.2 5.5 copy-start.7
  1407.9 24.9 %copy-start.15 = (s32[48]{0:T(128)S(1)}, s32[48]{0:T(128)}, u32[]{:S(2)}) copy-start(s32[48]{0:T(128)} %copy-done.14) | copy-start | bytes 580
  1432.8 31.7 %copy-start.13 = (pred[16,3]{1,0:T(8,128)(4,1)S(1)}, pred[16,3]{1,0:T(8,128)(4,1)}, u32[]{:S(2)}) copy-start(pred[16,3]{1,0:T(8,128)(4,1)} %get-tuple-element.144) | copy-start | bytes 148
  1471.0 208.3 %all-reduce.2.cloned.1.call-start = ((), (), s32[]{:S(2)}) async-start(), calls=%async_computation.5 | async-start | bytes 1179648 | tf_op jit(solution)/shard_map/psum | solution.py:117
  1491.9 7.1 copy-start.9
  1491.9 7.1 copy-start.10
  (1 other events, 0.7 us)
Sparse Core Ops, SparseCore 0:
  1471.1 29.4 reduce-scatter.1
Sparse Core Ops, SparseCore 1:
  1500.5 178.7 all-reduce.1
where the time goes:
time: 1710 us; the launch traced here: 1690 us
  local copies, waits for them, and re-layouts  521 us (30%)
  matrix products  470 us (27%)
  other arithmetic  426 us (25%)
  waiting for transfers between devices  215 us (13%)
  starting transfers between devices  39.7 us (2%)
    scatter-add x9, other arithmetic, visit(): memory_acc = memory_acc.at[ids].add(pair_dkv)  262 us
    dot_general x9, matrix products, pair_grads(): jnp.einsum('bhlk,blhd->bhkd', dscores, q4, preferred_element_type=jnp.flo...  183 us
    dot_general x9, matrix products, pair_grads(): jnp.einsum('bhlk,bhkd->blhd', dscores, k4, preferred_element_type=jnp.flo...  177 us
    gather x18, local copies, waits for them, and re-layouts, visit(): memory = jnp.take(patch_key_value, ids, axis=0)  160 us
    concatenate x9, local copies, waits for them, and re-layouts, pair_grads(): return (pair_dq, jnp.concatenate([pair_dk, pair_dv], axis=-1))  137 us
    psum x1, waiting for transfers between devices, per_device(): weight_grad = lax.psum(weight_local, 'dp')  118 us
    all_to_all x1, waiting for transfers between devices, per_device(): lax.all_to_all(send_pair, 'dp', split_axis=0, concat_axis=0, tiled=True)  75.7 us
    select_n x10, other arithmetic, visit(): memory = jnp.take(patch_key_value, ids, axis=0)  65.3 us
  transfers between devices with their start and end apart: 5, of which 3 were waited for; matrix products, arithmetic and copies ran while one was open for 13% of the time, Pallas kernels for 0%

commit v1 on v0

v1 whole, which is shorter than its diff:
```python
import functools

import jax
import jax.numpy as jnp
from jax import lax
from jax.experimental import pallas as pl
from jax.experimental.pallas import tpu as pltpu
from jax.sharding import PartitionSpec as P

HEAD_SIZE = 64
NEG = 3
LANES = 128
TILE = 256
VMEM_LIMIT = 48 * 1024 * 1024


def cdiv(a, b):
    return -(-a // b)


def lower_half(shape):
    return lax.broadcasted_iota(jnp.int32, shape, len(shape) - 1) < HEAD_SIZE


def request_slots(neg_ref, rank_ref, owners, images_here, wanted):
    def clear(o, carry):
        rank_ref[wanted + o] = 0
        return carry

    lax.fori_loop(0, owners, clear, 0)

    def count(k, carry):
        o = neg_ref[k] // images_here
        c = rank_ref[wanted + o]
        rank_ref[k] = c
        rank_ref[wanted + o] = c + 1
        return carry

    lax.fori_loop(0, wanted, count, 0)


def pack_kernel(
    heads, length, images_here, mp_ref, neg_ref, text_ref, weight_ref, grad_ref, *rest
):
    wires = rest[:heads]
    own_ref, q_scr, wire_scr, own_scr, rank_ref = rest[heads:]
    texts_here, slots = grad_ref.shape[0], grad_ref.shape[1]
    owners = wires[0].shape[0]
    wire_rows = wires[0].shape[1]
    captions = texts_here // images_here
    wanted = neg_ref.shape[0]
    request_slots(neg_ref, rank_ref, owners, images_here, wanted)
    for h in range(heads):
        w = weight_ref[h * LANES : (h + 1) * LANES, :]
        q = lax.dot_general(
            text_ref[...], w, (((1,), (1,)), ((), ())), preferred_element_type=jnp.float32
        )
        q_scr[h] = q.astype(jnp.bfloat16).astype(jnp.float32)
    low = lower_half((length, LANES))
    first = mp_ref[0] * heads

    def joined(t, s, h, q):
        head = first + h
        col = pl.multiple_of((head // 2) * LANES, LANES)
        g = grad_ref[t, s, :, pl.ds(col, LANES)].astype(jnp.float32)
        g = jnp.where(lax.rem(head, 2) == 1, g, pltpu.roll(g, HEAD_SIZE, 1))
        return jnp.where(low, q, g)

    def one_text(t, carry):
        for h in range(heads):
            q = q_scr[h, pl.ds(t * length, length), :]
            for j in range(slots - 1):
                k = t * (slots - 1) + j
                o = neg_ref[k] // images_here
                row = o * wire_rows + rank_ref[k] * length
                wire_scr[h, pl.ds(row, length), :] = joined(t, j + 1, h, q)
        return carry

    lax.fori_loop(0, texts_here, one_text, 0)
    for h in range(heads):
        wires[h][...] = (
            wire_scr[h].reshape(owners, wire_rows, LANES).astype(jnp.bfloat16)
        )
    for i in range(images_here):
        for h in range(heads):
            own_scr[...] = jnp.zeros(own_scr.shape, jnp.float32)
            for c in range(captions):
                t = i * captions + c
                q = q_scr[h, t * length : (t + 1) * length, :]
                own_scr[c * length : (c + 1) * length, :] = joined(t, 0, h, q)
            own_ref[i, h] = own_scr[...].astype(jnp.bfloat16)


def load_memory(kv, keys, kv_scr, kkt_scr, padded):
    whole = keys // 16 * 16
    low = lower_half((whole, LANES))
    body, tail = kv[:whole], kv[whole:]
    extra = padded - whole
    tail = jnp.concatenate(
        [tail, jnp.zeros((extra - (keys - whole), LANES), jnp.float32)], axis=0
    )
    full = jnp.concatenate([body, tail], axis=0)
    low = lower_half(full.shape)
    k_only = jnp.where(low, full, 0.0)
    kv_scr[:padded, :] = k_only.astype(jnp.bfloat16)
    kv_scr[padded:, :] = jnp.where(low, 0.0, full).astype(jnp.bfloat16)
    twice = k_only + pltpu.roll(k_only, HEAD_SIZE, 1)
    kkt_scr[...] = twice.T.astype(jnp.bfloat16)


def tile_grads(qg, keys, padded, kv_scr, kkt_scr, s_scr, pd_scr):
    tile = qg.shape[0]
    low = lower_half(qg.shape)
    zero = jnp.zeros_like(qg)
    s_scr[...] = lax.dot_general(
        kv_scr[...], qg, (((1,), (1,)), ((), ())), preferred_element_type=jnp.float32
    )
    bounds = list(range(0, padded, 64)) + [padded]
    chunks = list(zip(bounds[:-1], bounds[1:]))
    top = jnp.full((8, tile), -jnp.inf, jnp.float32)
    for a, b in chunks:
        s = s_scr[a:b, :]
        if b > keys:
            row = lax.broadcasted_iota(jnp.int32, s.shape, 0) + a
            s = jnp.where(row < keys, s, -jnp.inf)
            s_scr[a:b, :] = s
        top = jnp.maximum(top, jnp.max(s.reshape((b - a) // 8, 8, tile), axis=0))
    top = jnp.max(top, axis=0, keepdims=True)
    total = jnp.zeros((8, tile), jnp.float32)
    center = jnp.zeros((8, tile), jnp.float32)
    for a, b in chunks:
        e = jnp.exp(s_scr[a:b, :] - top)
        s_scr[a:b, :] = e
        total = total + jnp.sum(e.reshape((b - a) // 8, 8, tile), axis=0)
        d = e * s_scr[padded + a : padded + b, :]
        center = center + jnp.sum(d.reshape((b - a) // 8, 8, tile), axis=0)
    inverse = 1.0 / jnp.sum(total, axis=0, keepdims=True)
    center = jnp.sum(center, axis=0, keepdims=True) * inverse
    for a, b in chunks:
        p = s_scr[a:b, :] * inverse
        pd_scr[a:b, tile:] = p.astype(jnp.bfloat16)
        ds = p * (s_scr[padded + a : padded + b, :] - center)
        pd_scr[a:b, :tile] = ds.astype(jnp.bfloat16)
    both = jnp.concatenate([jnp.where(low, qg, zero), jnp.where(low, zero, qg)], axis=0)
    dkv = jnp.dot(pd_scr[...], both, preferred_element_type=jnp.float32)
    dqt = jnp.dot(kkt_scr[...], pd_scr[:, :tile], preferred_element_type=jnp.float32)
    return dqt.T * (HEAD_SIZE**-0.5), dkv


def own_kernel(keys, padded, qg_ref, kv_ref, acc_ref, dq_ref, kv_scr, kkt_scr, s_scr, pd_scr):
    load_memory(kv_ref[0, 0].astype(jnp.float32), keys, kv_scr, kkt_scr, padded)
    dq, dkv = tile_grads(qg_ref[0, 0], keys, padded, kv_scr, kkt_scr, s_scr, pd_scr)
    acc_ref[0, 0] = dkv
    dq_ref[0, 0] = dq


def far_kernel(
    keys,
    padded,
    length,
    images_here,
    plan_ref,
    wire_ref,
    kv_ref,
    own_ref,
    dkv_in,
    dkv_ref,
    back_ref,
    rows_scr,
    acc_scr,
    kv_scr,
    kkt_scr,
    s_scr,
    pd_scr,
):
    image = pl.program_id(0)
    senders = wire_ref.shape[0]
    slots = 2 * senders

    @pl.when(image == 0)
    def _():
        for i in range(images_here):
            n = plan_ref[slots + images_here + i]

            @pl.when(n > 0)
            def _():
                start = pl.multiple_of(plan_ref[slots + i] + (n - 1) * TILE, TILE)
                rows_scr[pl.ds(start, TILE), :] = jnp.zeros((TILE, LANES), jnp.float32)

        def place(s, carry):
            block = wire_ref[s].astype(jnp.float32)
            for r in range(2):
                pos = plan_ref[2 * s + r]

                @pl.when(pos >= 0)
                def _():
                    rows_scr[pl.ds(pos, length), :] = block[r * length : (r + 1) * length]

            return carry

        lax.fori_loop(0, senders, place, 0)

    load_memory(kv_ref[0, 0].astype(jnp.float32), keys, kv_scr, kkt_scr, padded)
    acc_scr[...] = own_ref[0, 0]
    base = plan_ref[slots + image]

    def step(n, carry):
        start = pl.multiple_of(base + n * TILE, TILE)
        qg = rows_scr[pl.ds(start, TILE), :].astype(jnp.bfloat16)
        dq, dkv = tile_grads(qg, keys, padded, kv_scr, kkt_scr, s_scr, pd_scr)
        acc_scr[...] += dkv
        rows_scr[pl.ds(start, TILE), :] = dq
        return carry

    lax.fori_loop(0, plan_ref[slots + images_here + image], step, 0)
    dkv_ref[0, 0] = acc_scr[:keys, :].astype(jnp.bfloat16)

    @pl.when(image == images_here - 1)
    def _():
        rows = back_ref.shape[1]
        low = lower_half((rows, LANES))

        def give(s, carry):
            p0 = jnp.maximum(plan_ref[2 * s], 0)
            p1 = jnp.maximum(plan_ref[2 * s + 1], 0)
            x0 = rows_scr[pl.ds(p0, rows), :]
            x1 = rows_scr[pl.ds(p1, rows), :]
            back_ref[s] = jnp.where(low, x0, x1).astype(jnp.bfloat16)
            return carry

        lax.fori_loop(0, senders, give, 0)


def gather_kernel(heads, length, images_here, neg_ref, text_ref, own_ref, *rest):
    backs = rest[:heads]
    dq_ref, weight_ref, sum_scr, rank_ref = rest[heads:]
    owners = backs[0].shape[0]
    wanted = neg_ref.shape[0]
    block = own_ref.shape[2]
    count = sum_scr.shape[1]
    per_image = count // images_here
    request_slots(neg_ref, rank_ref, owners, images_here, wanted)
    for h in range(heads):
        for i in range(images_here):
            sum_scr[h, i * per_image : (i + 1) * per_image, :] = own_ref[i, h][:per_image]

    def one(t, carry):
        at = pl.ds(t * length, length)
        for h in range(heads):
            total = sum_scr[h, at, :]
            for j in range(NEG):
                k = t * NEG + j
                o = neg_ref[k] // images_here
                x = backs[h][o].astype(jnp.float32)[:length]
                x = jnp.where(rank_ref[k] == 1, pltpu.roll(x, HEAD_SIZE, 1), x)
                total = total + x
            sum_scr[h, at, :] = total
        return carry

    lax.fori_loop(0, count // length, one, 0)
    text = text_ref[...]
    for h in range(heads):
        dq = sum_scr[h].astype(jnp.bfloat16)
        dq_ref[h] = dq
        full = lax.dot_general(
            dq, text, (((0,), (0,)), ((), ())), preferred_element_type=jnp.float32
        )
        weight_ref[h * HEAD_SIZE : (h + 1) * HEAD_SIZE, :] = full[:HEAD_SIZE].astype(
            jnp.bfloat16
        )


def params():
    return pltpu.CompilerParams(vmem_limit_bytes=VMEM_LIMIT)


SMEM = pl.BlockSpec(memory_space=pltpu.SMEM)
VMEM = pl.BlockSpec(memory_space=pltpu.VMEM)


def per_device(texts, query_weight, patch_key_value, grad_out, negatives):
    owners = lax.axis_size("dp")
    members = lax.axis_size("mp")
    texts_here, length, depth = texts.shape
    images_here, heads, keys, _ = patch_key_value.shape
    width = query_weight.shape[0]
    padded = cdiv(keys, 16) * 16
    count = texts_here * length
    wanted = NEG * texts_here
    slots = 2 * owners
    wire_rows = cdiv(2 * length, 8) * 8
    back_rows = cdiv(length, 8) * 8
    bf16, f32, i32 = jnp.bfloat16, jnp.float32, jnp.int32

    flat_text = texts.reshape(count, depth)
    flat_neg = negatives.reshape(-1)
    scaled = query_weight * jnp.asarray(HEAD_SIZE**-0.5, bf16)
    spread = jnp.pad(
        scaled.reshape(heads, HEAD_SIZE, depth), ((0, 0), (0, LANES - HEAD_SIZE), (0, 0))
    ).reshape(heads * LANES, depth)
    all_weight = lax.all_gather(query_weight, "mp", axis=0, tiled=True)

    packed = pl.pallas_call(
        functools.partial(pack_kernel, heads, length, images_here),
        in_specs=[SMEM, SMEM, VMEM, VMEM, VMEM],
        out_specs=[VMEM] * (heads + 1),
        out_shape=[jax.ShapeDtypeStruct((owners, wire_rows, LANES), bf16)] * heads
        + [jax.ShapeDtypeStruct((images_here, heads, TILE, LANES), bf16)],
        scratch_shapes=[
            pltpu.VMEM((heads, count, LANES), f32),
            pltpu.VMEM((heads, owners * wire_rows, LANES), f32),
            pltpu.VMEM((TILE, LANES), f32),
            pltpu.SMEM((wanted + owners,), i32),
        ],
        compiler_params=params(),
        name="pack",
    )(
        lax.axis_index("mp").reshape(1).astype(i32),
        flat_neg,
        flat_text,
        spread,
        grad_out,
    )
    wires, own_rows = packed[:heads], packed[heads]

    owner = flat_neg // images_here
    order = jnp.arange(wanted, dtype=i32)
    rank = jnp.sum(
        (owner[:, None] == owner[None, :]) & (order[None, :] < order[:, None]), axis=1
    ).astype(i32)
    slot = owner * 2 + rank
    placed = slot[None, :] == jnp.arange(slots, dtype=i32)[:, None]
    send_id = jnp.sum(jnp.where(placed, flat_neg[None, :] % images_here + 1, 0), axis=1) - 1
    got_id = lax.all_to_all(
        send_id.astype(i32).reshape(owners, 2), "dp", split_axis=0, concat_axis=0, tiled=True
    ).reshape(-1)
    got_wires = [lax.all_to_all(w, "dp", split_axis=0, concat_axis=0, tiled=True) for w in wires]

    here = jnp.arange(images_here, dtype=i32)
    all_slots = jnp.arange(slots, dtype=i32)
    ahead = jnp.sum(
        (got_id[:, None] == got_id[None, :]) & (all_slots[None, :] < all_slots[:, None]), axis=1
    ).astype(i32)
    number = jnp.sum(got_id[:, None] == here[None, :], axis=0).astype(i32)
    tiles = (number * length + TILE - 1) // TILE
    base = jnp.sum(jnp.where(here[None, :] < here[:, None], tiles[None, :], 0), axis=1) * TILE
    start = jnp.sum(jnp.where(got_id[:, None] == here[None, :], base[None, :], 0), axis=1)
    pos = jnp.where(got_id >= 0, start + ahead * length, -1)
    plan = jnp.concatenate([pos, base, tiles]).astype(i32)

    math_scratch = [
        pltpu.VMEM((2 * padded, LANES), bf16),
        pltpu.VMEM((LANES, padded), bf16),
        pltpu.VMEM((2 * padded, TILE), f32),
        pltpu.VMEM((padded, 2 * TILE), bf16),
    ]
    own_acc, own_dq = pl.pallas_call(
        functools.partial(own_kernel, keys, padded),
        grid=(images_here, heads),
        in_specs=[
            pl.BlockSpec((1, 1, TILE, LANES), lambda i, h: (i, h, 0, 0)),
            pl.BlockSpec((1, 1, keys, LANES), lambda i, h: (i, h, 0, 0)),
        ],
        out_specs=[
            pl.BlockSpec((1, 1, padded, LANES), lambda i, h: (i, h, 0, 0)),
            pl.BlockSpec((1, 1, TILE, LANES), lambda i, h: (i, h, 0, 0)),
        ],
        out_shape=[
            jax.ShapeDtypeStruct((images_here, heads, padded, LANES), f32),
            jax.ShapeDtypeStruct((images_here, heads, TILE, LANES), f32),
        ],
        scratch_shapes=math_scratch,
        compiler_params=params(),
        name="own",
    )(own_rows, patch_key_value)

    most = (2 * owners * length) // TILE + images_here
    dkv = jnp.zeros(patch_key_value.shape, bf16)
    backs = []
    for h in range(heads):
        dkv, back = pl.pallas_call(
            functools.partial(far_kernel, keys, padded, length, images_here),
            grid=(images_here,),
            in_specs=[
                SMEM,
                pl.BlockSpec((owners, wire_rows, LANES), lambda i: (0, 0, 0)),
                pl.BlockSpec((1, 1, keys, LANES), lambda i, h=h: (i, h, 0, 0)),
                pl.BlockSpec((1, 1, padded, LANES), lambda i, h=h: (i, h, 0, 0)),
                pl.BlockSpec(memory_space=pl.ANY),
            ],
            out_specs=[
                pl.BlockSpec((1, 1, keys, LANES), lambda i, h=h: (i, h, 0, 0)),
                pl.BlockSpec((owners, back_rows, LANES), lambda i: (0, 0, 0)),
            ],
            out_shape=[
                jax.ShapeDtypeStruct(patch_key_value.shape, bf16),
                jax.ShapeDtypeStruct((owners, back_rows, LANES), bf16),
            ],
            scratch_shapes=[
                pltpu.VMEM((most * TILE + 64, LANES), f32),
                pltpu.VMEM((padded, LANES), f32),
            ]
            + math_scratch,
            input_output_aliases={4: 0},
            compiler_params=params(),
            name="far" + str(h),
        )(plan, got_wires[h], patch_key_value, own_acc, dkv)
        backs.append(lax.all_to_all(back, "dp", split_axis=0, concat_axis=0, tiled=True))

    dquery, weight_local = pl.pallas_call(
        functools.partial(gather_kernel, heads, length, images_here),
        in_specs=[SMEM] + [VMEM] * (2 + heads),
        out_specs=[VMEM, VMEM],
        out_shape=[
            jax.ShapeDtypeStruct((heads, count, LANES), bf16),
            jax.ShapeDtypeStruct((width, depth), bf16),
        ],
        scratch_shapes=[
            pltpu.VMEM((heads, count, LANES), f32),
            pltpu.SMEM((wanted + owners,), i32),
        ],
        compiler_params=params(),
        name="gather",
    )(flat_neg, flat_text, own_dq, *backs)

    share = width // owners
    parts = lax.all_to_all(
        weight_local.reshape(owners, share, depth), "dp", split_axis=0, concat_axis=0, tiled=True
    )
    rows = jnp.sum(parts.astype(f32), axis=0).astype(bf16)
    weight_grad = lax.all_to_all(
        jnp.broadcast_to(rows[None], (owners, share, depth)),
        "dp",
        split_axis=0,
        concat_axis=0,
        tiled=True,
    )
    weight_grad = weight_grad.reshape(width, depth).astype(f32)

    mine = count // members
    flat_dq = dquery[:, :, :HEAD_SIZE].transpose(1, 0, 2).reshape(members, mine, width)
    flat_dq = lax.all_to_all(flat_dq, "mp", split_axis=0, concat_axis=0, tiled=True)
    flat_dq = flat_dq.transpose(1, 0, 2).reshape(mine, members * width)
    text_grad = jnp.dot(flat_dq, all_weight, preferred_element_type=f32).astype(bf16)
    text_grad = text_grad.reshape(texts_here // members, length, depth)
    return (text_grad, weight_grad, dkv)


def solution(mesh):
    in_specs = (
        P("dp", None, None),
        P("mp", None),
        P("dp", "mp", None, None),
        P("dp", None, None, None),
        P("dp", None),
    )
    out_specs = (P(("dp", "mp"), None, None), P("mp", None), P("dp", "mp", None, None))
    return jax.shard_map(
        per_device, mesh=mesh, in_specs=in_specs, out_specs=out_specs, check_vma=False
    )
```

time: 1710 us -> 337 us (0.20); the launches traced: 1690 us -> 334 us
  local copies, waits for them, and re-layouts: 521 us -> 33.9 us
  matrix products: 470 us -> 1.62 us
  other arithmetic: 426 us -> 2.81 us
  waiting for transfers between devices: 215 us -> 50.4 us
  Pallas kernels: 0 us -> 79 us
  blocking collectives: 0 us -> 77.9 us
  starting transfers between devices: 39.7 us -> 74.5 us
    dot_general x50 -> x1, matrix products: 470 us -> 1.62 us  [per_device(): jnp.dot(flat_dq, all_weight, preferred_element_type=f32).astype(bf16)]
    scatter-add x9 -> x0, other arithmetic: 262 us -> none  [visit(): memory_acc = memory_acc.at[ids].add(pair_dkv)]
    gather x19 -> x0, local copies, waits for them, and re-layouts: 165 us -> none  [the longest x18 160 us: visit(): memory = jnp.take(patch_key_value, ids, axis=0)]
    concatenate x10 -> x0, local copies, waits for them, and re-layouts: 141 us -> none  [the longest x9 137 us: pair_grads(): return (pair_dq, jnp.concatenate([pair_dk, pair_dv], axis=-1))]
    psum x1 -> x0, waiting for transfers between devices: 118 us -> none  [per_device(): weight_grad = lax.psum(weight_local, 'dp')]
    pallas_call x0 -> x6, Pallas kernels: none -> 79 us  [the longest x3 53.8 us: per_device(): pl.pallas_call(functools.partial(far_kernel, keys, padded, length, images...]
    all_to_all x0 -> x2, blocking collectives: none -> 77.9 us  [per_device(): lax.all_to_all(w, 'dp', split_axis=0, concat_axis=0, tiled=True)]
    select_n x21 -> x3, other arithmetic: 65.4 us -> 0.03 us  [the longest x1 0.01 us: per_device(): tiles = (number * length + TILE - 1) // TILE]
  transfers between devices with their start and end apart: 5 -> 9, of which waited for: 3 -> 4; matrix products, arithmetic and copies ran while one was open for 13% -> 6% of each run, Pallas kernels for 0% -> 24%
where the time goes in v1:
time: 337 us; the launch traced here: 334 us
  Pallas kernels  79 us (23%)
  blocking collectives  77.9 us (23%)
  starting transfers between devices  74.5 us (22%)
  waiting for transfers between devices  50.4 us (15%)
  local copies, waits for them, and re-layouts  33.9 us (10%)
  between operations  14.3 us (4%)
    all_to_all x2, blocking collectives, per_device(): lax.all_to_all(w, 'dp', split_axis=0, concat_axis=0, tiled=True)  77.9 us
    pallas_call x3, Pallas kernels, per_device(): pl.pallas_call(functools.partial(far_kernel, keys, padded, length, images...  53.8 us
    all_to_all x3, starting transfers between devices, per_device(): lax.all_to_all(back, 'dp', split_axis=0, concat_axis=0, tiled=True)  38.1 us
    unnamed x38, local copies, waits for them, and re-layouts  26.3 us
    all_to_all x3, waiting for transfers between devices, per_device(): lax.all_to_all(back, 'dp', split_axis=0, concat_axis=0, tiled=True)  19.6 us
    all_to_all x1, waiting for transfers between devices, per_device(): lax.all_to_all(weight_local.reshape(owners, share, depth), 'dp', split_ax...  13.7 us
    all_to_all x1, starting transfers between devices, per_device(): lax.all_to_all(send_id.astype(i32).reshape(owners, 2), 'dp', split_axis=0...  13.2 us
    pallas_call x1, Pallas kernels, per_device(): pl.pallas_call(functools.partial(own_kernel, keys, padded), grid=(images_...  12.8 us
  transfers between devices with their start and end apart: 9, of which 4 were waited for; matrix products, arithmetic and copies ran while one was open for 6% of the time, Pallas kernels for 24%

profile of v1, /device:TPU:1, one launch (start us, length us, event | category | flops | bytes accessed | tf_op | source)
XLA Modules:
  0.0 334.4 jit_solution(14440648562633887936)
XLA Ops:
  7.2 0.8 copy.57
  8.3 0.8 sub.23
  9.1 13.2 %all-to-all-start = ((s32[64,1,2]{2,1,0:T(1,128)}), s32[64,1,2]{2,1,0:T(1,128)S(1)}, u32[]{:S(2)}, u32[]{:S(2)}) async-start(s32[64,1,2]{2,1,0:T(1,128)} %bitcast.3), calls=%async_computation | async-start | bytes 65536 | tf_op jit(solution)/shard_map/all_to_all | solution.py:334
  22.3 1.0 broadcast_multiply_fusion
  23.2 1.4 copy.58
  25.0 4.5 %copy.59.grad_ref = bf16[16,4,35,768]{3,2,1,0:T(8,128)(2,1)} copy(bf16[16,4,35,768]{3,1,2,0:T(4,128)(2,1)} %param.8) | data formatting | bytes 6881280 | tf_op args[3]
  29.5 7.4 %pack.1 = (bf16[64,72,128]{2,1,0:T(8,128)(2,1)S(1)}, bf16[64,72,128]{2,1,0:T(8,128)(2,1)S(1)}, bf16[64,72,128]{2,1,0:T(8,128)(2,1)}, bf16[4,3,256,128]{3,2,1,0:T(8,128)(2,1)S(1)}) custom-call(s32[1]{0:T(128)} %bitcast.mp_ref, s32[48]{0:T(128)S(1)} %reshape.182.neg_ref, bf16[560,768]{1,0:T(8,128)(2,1)S(1)} %reshape.183.text_ref, ...), custom_call_target="tpu_custom_call" | custom-call | tf_op jit(solution)/shard_map/pack/pallas_call | solution.py:303
  36.9 0.9 copy-done.10
  37.8 40.8 %all_to_all.51.wire_ref = bf16[64,72,128]{2,1,0:T(8,128)(2,1)} all-to-all(bf16[64,72,128]{2,1,0:T(8,128)(2,1)S(1)} %get-tuple-element.19), channel_id=1, replica_groups=mesh['dp'=64,'mp'=4] {'dp'}, dimensions={0} | all-to-all | bytes 2359296 | tf_op jit(solution)/shard_map/all_to_all | solution.py:337
  78.6 37.1 %all_to_all.52.wire_ref = bf16[64,72,128]{2,1,0:T(8,128)(2,1)} all-to-all(bf16[64,72,128]{2,1,0:T(8,128)(2,1)S(1)} %get-tuple-element.22), channel_id=1, replica_groups=mesh['dp'=64,'mp'=4] {'dp'}, dimensions={0} | all-to-all | bytes 2359296 | tf_op jit(solution)/shard_map/all_to_all | solution.py:337
  115.7 6.8 %all-to-all-start.5 = ((bf16[64,72,128]{2,1,0:T(8,128)(2,1)}), bf16[64,72,128]{2,1,0:T(8,128)(2,1)}, u32[]{:S(2)}, u32[]{:S(2)}) async-start(bf16[64,72,128]{2,1,0:T(8,128)(2,1)} %get-tuple-element.25), calls=%async_computation.5 | async-start | bytes 2359296 | tf_op jit(solution)/shard_map/all_to_all | solution.py:337
  122.5 1.8 copy.60.kv_ref
  124.3 12.8 %own.1 = (f32[4,3,592,128]{3,2,1,0:T(8,128)}, f32[4,3,256,128]{3,2,1,0:T(8,128)S(1)}) custom-call(bf16[4,3,256,128]{3,2,1,0:T(8,128)(2,1)S(1)} %copy-done.11, bf16[4,3,577,128]{3,2,1,0:T(8,128)(2,1)S(1)} %copy.60.kv_ref), custom_call_target="tpu_custom_call" | custom-call | tf_op jit(solution)/shard_map/own/pallas_call | solution.py:357
  137.1 1.1 copy-done.8
  138.8 0.7 reduce.4
  140.9 17.8 %far0.1 = (bf16[4,3,577,128]{3,2,1,0:T(8,128)(2,1)S(1)}, bf16[64,40,128]{2,1,0:T(8,128)(2,1)S(1)}) custom-call(s32[136]{0:T(256)S(1)} %pad_add_fusion.plan_ref, bf16[64,72,128]{2,1,0:T(8,128)(2,1)S(1)} %copy-done.7, bf16[4,3,577,128]{3,2,1,0:T(8,128)(2,1)S(1)} %copy.60.kv_ref, ...), custom_call_target="tpu_custom_call", output_to_operand_aliasing={{0}: (4, {})} | custom-call | tf_op jit(solution)/shard_map/far0/pallas_call | solution.py:381
  158.7 1.3 copy-done
  160.0 0.8 copy-done.14
  160.9 12.7 %all-to-all-start.2 = ((bf16[64,40,128]{2,1,0:T(8,128)(2,1)}), bf16[64,40,128]{2,1,0:T(8,128)(2,1)S(1)}, u32[]{:S(2)}, u32[]{:S(2)}) async-start(bf16[64,40,128]{2,1,0:T(8,128)(2,1)} %copy-done.14), calls=%async_computation.2 | async-start | bytes 1310720 | tf_op jit(solution)/shard_map/all_to_all | solution.py:408
  173.6 1.5 copy-done.1
  175.1 1.3 copy-done.6
  176.3 17.8 %far1.1 = (bf16[4,3,577,128]{3,2,1,0:T(8,128)(2,1)S(1)}, bf16[64,40,128]{2,1,0:T(8,128)(2,1)S(1)}) custom-call(s32[136]{0:T(256)S(1)} %pad_add_fusion.plan_ref, bf16[64,72,128]{2,1,0:T(8,128)(2,1)S(1)} %copy-done.6, bf16[4,3,577,128]{3,2,1,0:T(8,128)(2,1)S(1)} %copy.60.kv_ref, ...), custom_call_target="tpu_custom_call", output_to_operand_aliasing={{0}: (4, {})} | custom-call | tf_op jit(solution)/shard_map/far1/pallas_call | solution.py:381
  194.1 1.3 copy-done.2
  195.4 0.9 copy-done.13
  196.3 12.8 %all-to-all-start.4 = ((bf16[64,40,128]{2,1,0:T(8,128)(2,1)}), bf16[64,40,128]{2,1,0:T(8,128)(2,1)}, u32[]{:S(2)}, u32[]{:S(2)}) async-start(bf16[64,40,128]{2,1,0:T(8,128)(2,1)} %copy-done.13), calls=%async_computation.4 | async-start | bytes 1310720 | tf_op jit(solution)/shard_map/all_to_all | solution.py:408
  209.1 1.5 copy-done.3
  210.6 18.2 %far2.1 = (bf16[4,3,577,128]{3,2,1,0:T(8,128)(2,1)S(1)}, bf16[64,40,128]{2,1,0:T(8,128)(2,1)S(1)}) custom-call(s32[136]{0:T(256)S(1)} %pad_add_fusion.plan_ref, bf16[64,72,128]{2,1,0:T(8,128)(2,1)} %all-to-all-done.5.wire_ref, bf16[4,3,577,128]{3,2,1,0:T(8,128)(2,1)S(1)} %copy.60.kv_ref, ...), custom_call_target="tpu_custom_call", output_to_operand_aliasing={{0}: (4, {})} | custom-call | tf_op jit(solution)/shard_map/far2/pallas_call | solution.py:381
  228.8 1.2 copy-done.4
  230.1 0.8 copy-done.12
  230.9 12.7 %all-to-all-start.6 = ((bf16[64,40,128]{2,1,0:T(8,128)(2,1)}), bf16[64,40,128]{2,1,0:T(8,128)(2,1)S(1)}, u32[]{:S(2)}, u32[]{:S(2)}) async-start(bf16[64,40,128]{2,1,0:T(8,128)(2,1)} %copy-done.12), calls=%async_computation.6 | async-start | bytes 1310720 | tf_op jit(solution)/shard_map/all_to_all | solution.py:408
  243.6 0.7 all-gather.2.cloned.1.call-update
  244.3 19.6 %all-to-all-done.6.rest_2_ = bf16[64,40,128]{2,1,0:T(8,128)(2,1)S(1)} async-done(((bf16[64,40,128]{2,1,0:T(8,128)(2,1)}), bf16[64,40,128]{2,1,0:T(8,128)(2,1)S(1)}, u32[]{:S(2)}, u32[]{:S(2)}) %all-to-all-start.6) | async-done | bytes 655392 | tf_op jit(solution)/shard_map/all_to_all | solution.py:408
  263.9 1.4 copy-done.9
  265.4 4.9 %gather.1 = (bf16[3,560,128]{2,1,0:T(8,128)(2,1)S(1)}, bf16[192,768]{1,0:T(8,128)(2,1)S(1)}) custom-call(s32[48]{0:T(128)S(1)} %reshape.182.neg_ref, bf16[560,768]{1,0:T(8,128)(2,1)S(1)} %reshape.183.text_ref, f32[4,3,256,128]{3,2,1,0:T(8,128)S(1)} %copy-done.9, bf16[64,40,128]{2,1,0:T(8,128)(2,1)S(1)} %all-to-all-done.2.rest_0_, ...), custom_call_target="tpu_custom_call" | custom-call | tf_op jit(solution)/shard_map/gather/pallas_call | solution.py:410
  270.3 0.7 copy-done.15
  271.0 1.8 reshape.191
  272.9 5.8 %all-to-all-start.8 = ((bf16[64,3,768]{2,1,0:T(4,128)(2,1)}), bf16[64,3,768]{2,1,0:T(4,128)(2,1)S(1)}, u32[]{:S(2)}, u32[]{:S(2)}) async-start(bf16[64,3,768]{2,1,0:T(4,128)(2,1)} %reshape.191), calls=%async_computation.8 | async-start | bytes 786432 | tf_op jit(solution)/shard_map/all_to_all | solution.py:427
  279.0 1.1 reshape.193
  280.1 13.7 %all-to-all-done.8 = bf16[64,3,768]{2,1,0:T(4,128)(2,1)S(1)} async-done(((bf16[64,3,768]{2,1,0:T(4,128)(2,1)}), bf16[64,3,768]{2,1,0:T(4,128)(2,1)S(1)}, u32[]{:S(2)}, u32[]{:S(2)}) %all-to-all-start.8) | async-done | bytes 294944 | tf_op jit(solution)/shard_map/all_to_all | solution.py:427
  293.8 4.0 %all-to-all-start.7 = ((bf16[4,140,192]{2,1,0:T(8,128)(2,1)}), bf16[4,140,192]{2,1,0:T(8,128)(2,1)S(1)}, u32[]{:S(2)}, u32[]{:S(2)}) async-start(bf16[4,140,192]{2,1,0:T(8,128)(2,1)} %reshape.193), calls=%async_computation.7 | async-start | bytes 589824 | tf_op jit(solution)/shard_map/all_to_all | solution.py:442
  298.0 6.1 %all-to-all-done.7 = bf16[4,140,192]{2,1,0:T(8,128)(2,1)S(1)} async-done(((bf16[4,140,192]{2,1,0:T(8,128)(2,1)}), bf16[4,140,192]{2,1,0:T(8,128)(2,1)S(1)}, u32[]{:S(2)}, u32[]{:S(2)}) %all-to-all-start.7) | async-done | bytes 215072 | tf_op jit(solution)/shard_map/all_to_all | solution.py:442
  304.1 0.8 broadcast_in_dim.68
  304.9 6.6 %all-to-all-start.9 = ((bf16[64,3,768]{2,1,0:T(4,128)(2,1)}), bf16[64,3,768]{2,1,0:T(4,128)(2,1)S(1)}, u32[]{:S(2)}, u32[]{:S(2)}) async-start(bf16[64,3,768]{2,1,0:T(4,128)(2,1)} %broadcast_in_dim.68), calls=%async_computation.9 | async-start | bytes 786432 | tf_op jit(solution)/shard_map/all_to_all | solution.py:431
  311.5 1.9 copy.70
  313.8 1.6 convolution_convert_fusion
  315.5 0.8 copy.69
  316.3 10.2 %all-to-all-done.9 = bf16[64,3,768]{2,1,0:T(4,128)(2,1)S(1)} async-done(((bf16[64,3,768]{2,1,0:T(4,128)(2,1)}), bf16[64,3,768]{2,1,0:T(4,128)(2,1)S(1)}, u32[]{:S(2)}, u32[]{:S(2)}) %all-to-all-start.9) | async-done | bytes 294944 | tf_op jit(solution)/shard_map/all_to_all | solution.py:431
  326.5 1.0 reshape.192
  (50 shorter events, 3.6 us)
Async XLA Ops:
  9.1 28.7 %all-to-all-start = ((s32[64,1,2]{2,1,0:T(1,128)}), s32[64,1,2]{2,1,0:T(1,128)S(1)}, u32[]{:S(2)}, u32[]{:S(2)}) async-start(s32[64,1,2]{2,1,0:T(1,128)} %bitcast.3), calls=%async_computation | async-start | bytes 65536 | tf_op jit(solution)/shard_map/all_to_all | solution.py:334
  36.9 0.9 copy-start.10
  115.7 45.2 %all-to-all-start.5 = ((bf16[64,72,128]{2,1,0:T(8,128)(2,1)}), bf16[64,72,128]{2,1,0:T(8,128)(2,1)}, u32[]{:S(2)}, u32[]{:S(2)}) async-start(bf16[64,72,128]{2,1,0:T(8,128)(2,1)} %get-tuple-element.25), calls=%async_computation.5 | async-start | bytes 2359296 | tf_op jit(solution)/shard_map/all_to_all | solution.py:337
  122.5 1.8 copy-start.11
  137.1 1.1 copy-start.8
  139.7 1.3 copy-start.7
  158.7 1.3 copy-start
  160.0 0.8 copy-start.14
  160.9 35.4 %all-to-all-start.2 = ((bf16[64,40,128]{2,1,0:T(8,128)(2,1)}), bf16[64,40,128]{2,1,0:T(8,128)(2,1)S(1)}, u32[]{:S(2)}, u32[]{:S(2)}) async-start(bf16[64,40,128]{2,1,0:T(8,128)(2,1)} %copy-done.14), calls=%async_computation.2 | async-start | bytes 1310720 | tf_op jit(solution)/shard_map/all_to_all | solution.py:408
  173.6 1.5 copy-start.1
  175.1 1.3 copy-start.6
  194.1 1.3 copy-start.2
  195.4 0.9 copy-start.13
  196.3 34.6 %all-to-all-start.4 = ((bf16[64,40,128]{2,1,0:T(8,128)(2,1)}), bf16[64,40,128]{2,1,0:T(8,128)(2,1)}, u32[]{:S(2)}, u32[]{:S(2)}) async-start(bf16[64,40,128]{2,1,0:T(8,128)(2,1)} %copy-done.13), calls=%async_computation.4 | async-start | bytes 1310720 | tf_op jit(solution)/shard_map/all_to_all | solution.py:408
  209.1 1.5 copy-start.3
  228.8 1.3 copy-start.4
  230.1 0.8 copy-start.12
  230.9 33.0 %all-to-all-start.6 = ((bf16[64,40,128]{2,1,0:T(8,128)(2,1)}), bf16[64,40,128]{2,1,0:T(8,128)(2,1)S(1)}, u32[]{:S(2)}, u32[]{:S(2)}) async-start(bf16[64,40,128]{2,1,0:T(8,128)(2,1)} %copy-done.12), calls=%async_computation.6 | async-start | bytes 1310720 | tf_op jit(solution)/shard_map/all_to_all | solution.py:408
  243.6 70.2 %all-gather.2.cloned.1.call-start = ((), (), s32[]{:S(2)}) async-start(), calls=%async_computation.10 | async-start | bytes 1474560 | tf_op jit(solution)/shard_map/all_gather | solution.py:301
  263.9 1.4 copy-start.9
  270.3 0.7 copy-start.15
  272.9 20.9 %all-to-all-start.8 = ((bf16[64,3,768]{2,1,0:T(4,128)(2,1)}), bf16[64,3,768]{2,1,0:T(4,128)(2,1)S(1)}, u32[]{:S(2)}, u32[]{:S(2)}) async-start(bf16[64,3,768]{2,1,0:T(4,128)(2,1)} %reshape.191), calls=%async_computation.8 | async-start | bytes 786432 | tf_op jit(solution)/shard_map/all_to_all | solution.py:427
  279.0 32.5 %copy-start.5 = (bf16[4,3,577,128]{3,2,1,0:T(8,128)(2,1)S(1)}, bf16[4,3,577,128]{3,2,1,0:T(8,128)(2,1)}, u32[]{:S(2)}) copy-start(bf16[4,3,577,128]{3,2,1,0:T(8,128)(2,1)} %copy-done.4) | copy-start | bytes 5317636
  293.8 10.3 %all-to-all-start.7 = ((bf16[4,140,192]{2,1,0:T(8,128)(2,1)}), bf16[4,140,192]{2,1,0:T(8,128)(2,1)S(1)}, u32[]{:S(2)}, u32[]{:S(2)}) async-start(bf16[4,140,192]{2,1,0:T(8,128)(2,1)} %reshape.193), calls=%async_computation.7 | async-start | bytes 589824 | tf_op jit(solution)/shard_map/all_to_all | solution.py:442
  304.9 21.6 %all-to-all-start.9 = ((bf16[64,3,768]{2,1,0:T(4,128)(2,1)}), bf16[64,3,768]{2,1,0:T(4,128)(2,1)S(1)}, u32[]{:S(2)}, u32[]{:S(2)}) async-start(bf16[64,3,768]{2,1,0:T(4,128)(2,1)} %broadcast_in_dim.68), calls=%async_computation.9 | async-start | bytes 786432 | tf_op jit(solution)/shard_map/all_to_all | solution.py:431
Sparse Core Ops, SparseCore 0:
  246.2 26.8 all-gather.1

commit v2 on v0

v2 whole, which is shorter than its diff:
```python
import functools

import jax
import jax.numpy as jnp
from jax import lax
from jax.experimental import pallas as pl
from jax.experimental.pallas import tpu as pltpu
from jax.sharding import PartitionSpec as P

HEAD_SIZE = 64
NEG = 3
LANES = 128
TILE = 256
WAYS = 4
VMEM_LIMIT = 60 * 1024 * 1024


def cdiv(a, b):
    return -(-a // b)


def lower_half(shape):
    return lax.broadcasted_iota(jnp.int32, shape, len(shape) - 1) < HEAD_SIZE


def request_slots(neg_ref, rank_ref, seen_ref, owners, images_here):
    negatives, texts_here = neg_ref.shape

    def clear(o, carry):
        seen_ref[o] = 0
        return carry

    lax.fori_loop(0, owners, clear, 0)

    def count(t, carry):
        for j in range(negatives):
            o = neg_ref[j, t] // images_here
            c = seen_ref[o]
            rank_ref[j, t] = c
            seen_ref[o] = c + 1
        return carry

    lax.fori_loop(0, texts_here, count, 0)


def joined(g, odd, q):
    g = g.astype(jnp.float32)
    g = jnp.where(odd == 1, g, pltpu.roll(g, HEAD_SIZE, 1))
    return jnp.where(lower_half(g.shape), q, g)


def project(text_ref, weight_ref, query_ref):
    q = lax.dot_general(
        text_ref[...], weight_ref[...], (((1,), (1,)), ((), ())), preferred_element_type=jnp.float32
    )
    q = q.astype(jnp.bfloat16).astype(jnp.float32) * HEAD_SIZE**-0.5
    for h in range(query_ref.shape[0]):
        if h % 2:
            a = (h - 1) * HEAD_SIZE
            query_ref[h] = pltpu.roll(q[:, a : a + LANES], HEAD_SIZE, 1)
        elif (h + 2) * HEAD_SIZE <= q.shape[1]:
            query_ref[h] = q[:, h * HEAD_SIZE : (h + 2) * HEAD_SIZE]
        else:
            query_ref[h, :, :HEAD_SIZE] = q[:, h * HEAD_SIZE :]
            query_ref[h, :, HEAD_SIZE:] = jnp.zeros((q.shape[0], HEAD_SIZE), jnp.float32)


def pack_rows(first, heads, images_here, odd_ref, neg_ref, rank_ref, query_ref, grad_ref, wire_ref, scr):
    texts_here, slots, length, _ = grad_ref.shape
    wire_rows = wire_ref.shape[1]
    tells = wire_rows >= 2 * heads * length + 2
    if tells:
        scr[...] = jnp.full(scr.shape, -1.0, jnp.float32)

    def one_text(t, carry):
        for h in range(heads):
            q = query_ref[first + h, pl.ds(t, length, stride=texts_here), :]
            place = odd_ref[0] + first + h
            col = pl.multiple_of((place // 2) * LANES, LANES)
            for j in range(slots - 1):
                n = neg_ref[j, t]
                r = rank_ref[j, t]
                o = n // images_here
                row = o * wire_rows + (r * heads + h) * length
                g = grad_ref[t, j + 1, :, pl.ds(col, LANES)]
                scr[pl.ds(row, length), :] = joined(g, lax.rem(place, 2), q)
                if h == 0 and tells:
                    tell = o * wire_rows + 2 * heads * length + r
                    image = (n - o * images_here).astype(jnp.float32)
                    scr[pl.ds(tell, 1), :] = jnp.full((1, LANES), image, jnp.float32)
        return carry

    lax.fori_loop(0, texts_here, one_text, 0)
    wire_ref[...] = scr[...].reshape(wire_ref.shape).astype(jnp.bfloat16)


def pack_first_kernel(
    heads, images_here, odd_ref, neg_ref, text_ref, weight_ref, grad_ref, wire_ref, query_ref, rank_ref, scr, seen_ref
):
    request_slots(neg_ref, rank_ref, seen_ref, wire_ref.shape[0], images_here)
    project(text_ref, weight_ref, query_ref)
    pack_rows(0, heads, images_here, odd_ref, neg_ref, rank_ref, query_ref, grad_ref, wire_ref, scr)


def pack_later_kernel(
    first, heads, images_here, odd_ref, neg_ref, rank_ref, query_ref, grad_ref, after_ref, wire_ref, scr
):
    pack_rows(first, heads, images_here, odd_ref, neg_ref, rank_ref, query_ref, grad_ref, wire_ref, scr)


def load_memory(kv, keys, kv_ref, kkt_ref, padded):
    full = jnp.concatenate([kv, jnp.zeros((padded - keys, LANES), jnp.float32)], axis=0)
    low = lower_half(full.shape)
    k_only = jnp.where(low, full, 0.0)
    kv_ref[:padded, :] = k_only.astype(jnp.bfloat16)
    kv_ref[padded:, :] = jnp.where(low, 0.0, full).astype(jnp.bfloat16)
    twice = k_only + pltpu.roll(k_only, HEAD_SIZE, 1)
    kkt_ref[...] = twice.T.astype(jnp.bfloat16)


def tile_scores(qg, kv, s_scr):
    s_scr[...] = lax.dot_general(
        kv, qg, (((1,), (1,)), ((), ())), preferred_element_type=jnp.float32
    )


def tile_softmax(keys, padded, s_scr, pd_scr):
    tile = s_scr.shape[1]
    bounds = list(range(0, padded, 64)) + [padded]
    chunks = list(zip(bounds[:-1], bounds[1:]))
    top = jnp.full((8, tile), -jnp.inf, jnp.float32)
    for a, b in chunks:
        s = s_scr[a:b, :]
        if b > keys:
            row = lax.broadcasted_iota(jnp.int32, s.shape, 0) + a
            s = jnp.where(row < keys, s, -jnp.inf)
            s_scr[a:b, :] = s
        top = jnp.maximum(top, jnp.max(s.reshape((b - a) // 8, 8, tile), axis=0))
    top = jnp.max(top, axis=0, keepdims=True)
    total = jnp.zeros((8, tile), jnp.float32)
    center = jnp.zeros((8, tile), jnp.float32)
    for a, b in chunks:
        e = jnp.exp(s_scr[a:b, :] - top)
        s_scr[a:b, :] = e
        total = total + jnp.sum(e.reshape((b - a) // 8, 8, tile), axis=0)
        d = e * s_scr[padded + a : padded + b, :]
        center = center + jnp.sum(d.reshape((b - a) // 8, 8, tile), axis=0)
    inverse = 1.0 / jnp.sum(total, axis=0, keepdims=True)
    center = jnp.sum(center, axis=0, keepdims=True) * inverse
    for a, b in chunks:
        p = s_scr[a:b, :] * inverse
        pd_scr[a:b, tile:] = p.astype(jnp.bfloat16)
        ds = p * (s_scr[padded + a : padded + b, :] - center)
        pd_scr[a:b, :tile] = ds.astype(jnp.bfloat16)


def tile_outputs(qg, kkt, pd_scr):
    tile = qg.shape[0]
    low = lower_half(qg.shape)
    zero = jnp.zeros_like(qg)
    both = jnp.concatenate([jnp.where(low, qg, zero), jnp.where(low, zero, qg)], axis=0)
    dkv = jnp.dot(pd_scr[...], both, preferred_element_type=jnp.float32)
    dqt = jnp.dot(kkt, pd_scr[:, :tile], preferred_element_type=jnp.float32)
    return dqt.T * (HEAD_SIZE**-0.5), dkv


def own_kernel(
    keys, padded, texts_here, odd_ref, query_ref, grad_ref, kv_ref, acc_ref, dq_ref, both_ref, kkt_ref, own_scr, s_scr, pd_scr
):
    image, h = pl.program_id(0), pl.program_id(1)
    captions, _, length, _ = grad_ref.shape
    load_memory(kv_ref[0, 0].astype(jnp.float32), keys, both_ref.at[0, 0], kkt_ref.at[0, 0], padded)
    place = odd_ref[0] + h
    col = pl.multiple_of((place // 2) * LANES, LANES)
    own_scr[captions * length :, :] = jnp.zeros((TILE - captions * length, LANES), jnp.float32)
    for c in range(captions):
        q = query_ref[0, pl.ds(image * captions + c, length, stride=texts_here), :]
        g = grad_ref[c, 0, :, pl.ds(col, LANES)]
        own_scr[c * length : (c + 1) * length, :] = joined(g, lax.rem(place, 2), q)
    qg = own_scr[...].astype(jnp.bfloat16)
    tile_scores(qg, both_ref[0, 0], s_scr)
    tile_softmax(keys, padded, s_scr, pd_scr)
    dq, dkv = tile_outputs(qg, kkt_ref[0, 0], pd_scr)
    acc_ref[0, 0] = dkv
    dq_ref[0, 0] = dq


def far_kernel(
    keys,
    padded,
    length,
    heads,
    plan_ref,
    wire_ref,
    both_ref,
    kkt_ref,
    own_ref,
    dkv_in,
    dkv_ref,
    back_ref,
    rows_scr,
    acc_scr,
    *pairs,
):
    h = pl.program_id(0)
    images = both_ref.shape[0]
    senders = wire_ref.shape[0]
    slots = 2 * senders
    ways = len(pairs) // 2
    s_scrs, pd_scrs = pairs[:ways], pairs[ways:]

    @pl.when(h == 0)
    def _():
        def clear(start):
            for g in range(heads):
                rows_scr[g, pl.ds(pl.multiple_of(start, TILE), TILE), :] = jnp.zeros(
                    (TILE, LANES), jnp.float32
                )

        for i in range(images):
            n = plan_ref[slots + images + i]

            @pl.when(n > 0)
            def _():
                clear(plan_ref[slots + i] + (n - 1) * TILE)

        end = plan_ref[slots + images - 1] + plan_ref[slots + 2 * images - 1] * TILE
        for w in range(ways - 1):
            clear(end + w * TILE)

        def place(s, carry):
            block = wire_ref[s].astype(jnp.float32)
            for r in range(2):
                pos = plan_ref[2 * s + r]

                @pl.when(pos >= 0)
                def _():
                    for g in range(heads):
                        a = (r * heads + g) * length
                        rows_scr[g, pl.ds(pos, length), :] = block[a : a + length]

            return carry

        lax.fori_loop(0, senders, place, 0)

    for i in range(images):
        acc_scr[i] = own_ref[i, 0]
    edges = [plan_ref[slots + i] // TILE for i in range(1, images)]
    tiles = plan_ref[slots + images - 1] // TILE + plan_ref[slots + 2 * images - 1]

    def step(k, carry):
        starts, images_of, rows = [], [], []
        for w in range(ways):
            n = k * ways + w
            image = jnp.int32(0)
            for e in edges:
                image = image + (n >= e).astype(jnp.int32)
            start = pl.multiple_of(n * TILE, TILE)
            qg = rows_scr[h, pl.ds(start, TILE), :].astype(jnp.bfloat16)
            starts.append(start)
            images_of.append(image)
            rows.append(qg)
            tile_scores(qg, both_ref[image, 0], s_scrs[w])
        for w in range(ways):
            tile_softmax(keys, padded, s_scrs[w], pd_scrs[w])
            dq, dkv = tile_outputs(rows[w], kkt_ref[images_of[w], 0], pd_scrs[w])
            acc_scr[images_of[w]] += dkv
            rows_scr[h, pl.ds(starts[w], TILE), :] = dq
        return carry

    lax.fori_loop(0, (tiles + ways - 1) // ways, step, 0)
    for i in range(images):
        dkv_ref[i, 0] = acc_scr[i, :keys, :].astype(jnp.bfloat16)

    @pl.when(h == heads - 1)
    def _():
        rows = back_ref.shape[1]
        low = lower_half((length, LANES))
        spare = rows - heads * length

        def give(s, carry):
            p0 = jnp.maximum(plan_ref[2 * s], 0)
            p1 = jnp.maximum(plan_ref[2 * s + 1], 0)
            parts = []
            for g in range(heads):
                x0 = rows_scr[g, pl.ds(p0, length), :]
                x1 = rows_scr[g, pl.ds(p1, length), :]
                parts.append(jnp.where(low, x0, x1))
            if spare:
                parts.append(jnp.zeros((spare, LANES), jnp.float32))
            back_ref[s] = jnp.concatenate(parts, axis=0).astype(jnp.bfloat16)
            return carry

        lax.fori_loop(0, senders, give, 0)


def sum_requests(heads, length, images_here, neg_ref, rank_ref, own_ref, back_ref, sum_scr):
    texts_here = sum_scr.shape[1] // length
    captions = texts_here // images_here

    def one(t, carry):
        image = t // captions
        totals = [
            own_ref[image, h, pl.ds((t - image * captions) * length, length), :]
            for h in range(heads)
        ]
        for j in range(NEG):
            block = back_ref[neg_ref[j, t] // images_here].astype(jnp.float32)
            block = jnp.where(rank_ref[j, t] == 1, pltpu.roll(block, HEAD_SIZE, 1), block)
            for h in range(heads):
                totals[h] = totals[h] + block[h * length : (h + 1) * length]
        for h in range(heads):
            sum_scr[h, pl.ds(t, length, stride=texts_here), :] = totals[h]
        return carry

    lax.fori_loop(0, texts_here, one, 0)


def gather_two_kernel(
    length, images_here, neg_ref, rank_ref, text_ref, own_ref, back_ref, dq_ref, weight_ref, sum_scr
):
    sum_requests(2, length, images_here, neg_ref, rank_ref, own_ref, back_ref, sum_scr)
    pair = jnp.where(
        lower_half(sum_scr.shape[1:]), sum_scr[0], pltpu.roll(sum_scr[1], HEAD_SIZE, 1)
    )
    dq = pair.astype(jnp.bfloat16)
    dq_ref[...] = dq
    weight_ref[...] = lax.dot_general(
        dq, text_ref[...], (((0,), (0,)), ((), ())), preferred_element_type=jnp.float32
    )


def gather_last_kernel(
    length, images_here, neg_ref, rank_ref, text_ref, own_ref, back_ref, head_ref, dq_ref, weight_ref, sum_scr
):
    sum_requests(1, length, images_here, neg_ref, rank_ref, own_ref, back_ref, sum_scr)
    dq = sum_scr[0].astype(jnp.bfloat16)
    dq_ref[...] = dq
    last = lax.dot_general(
        dq, text_ref[...], (((0,), (0,)), ((), ())), preferred_element_type=jnp.float32
    )
    half = weight_ref.shape[2]
    before = head_ref.shape[0] // 8
    for b in range(before + HEAD_SIZE // 8):
        rows = head_ref[b * 8 : b * 8 + 8, :] if b < before else last[(b - before) * 8 : (b - before) * 8 + 8]
        for side in range(2):
            weight_ref[2 * b + side] = rows[:, side * half : (side + 1) * half].astype(jnp.bfloat16)


def total_kernel(parts_ref, out_ref):
    total = parts_ref[0].astype(jnp.float32)
    for d in range(1, parts_ref.shape[0]):
        total = total + parts_ref[d].astype(jnp.float32)
    total = total.astype(jnp.bfloat16)
    for d in range(out_ref.shape[0]):
        out_ref[d] = total


def unfold_kernel(pieces_ref, out_ref):
    half = pieces_ref.shape[2]
    for b in range(out_ref.shape[0] // 8):
        for side in range(2):
            out_ref[b * 8 : b * 8 + 8, side * half : (side + 1) * half] = pieces_ref[
                2 * b + side
            ].astype(jnp.float32)


def params():
    return pltpu.CompilerParams(vmem_limit_bytes=VMEM_LIMIT)


def cost(us):
    return pl.CostEstimate(
        flops=int(us * 1e6 * 1150 / 2), bytes_accessed=int(us * 1e-6 * 3.6e12), transcendentals=0
    )


SMEM = pl.BlockSpec(memory_space=pltpu.SMEM)
VMEM = pl.BlockSpec(memory_space=pltpu.VMEM)
ANY = pl.BlockSpec(memory_space=pl.ANY)


def math_scratch(padded, ways):
    return [pltpu.VMEM((2 * padded, TILE), jnp.float32)] * ways + [
        pltpu.VMEM((padded, 2 * TILE), jnp.bfloat16)
    ] * ways


def far_call(plan, wire, first, many, both, kkt, own_acc, dkv, us, length):
    owners, rows, _ = wire.shape
    images, _, keys, _ = dkv.shape
    padded = own_acc.shape[2]
    back_rows = cdiv(many * length, 8) * 8
    most = (2 * owners * length) // TILE + images + WAYS - 1
    return pl.pallas_call(
        functools.partial(far_kernel, keys, padded, length, many),
        grid=(many,),
        in_specs=[
            SMEM,
            pl.BlockSpec((owners, rows, LANES), lambda h: (0, 0, 0)),
            pl.BlockSpec((images, 1, 2 * padded, LANES), lambda h: (0, first + h, 0, 0)),
            pl.BlockSpec((images, 1, LANES, padded), lambda h: (0, first + h, 0, 0)),
            pl.BlockSpec((images, 1, padded, LANES), lambda h: (0, first + h, 0, 0)),
            ANY,
        ],
        out_specs=[
            pl.BlockSpec((images, 1, keys, LANES), lambda h: (0, first + h, 0, 0)),
            pl.BlockSpec((owners, back_rows, LANES), lambda h: (0, 0, 0)),
        ],
        out_shape=[
            jax.ShapeDtypeStruct(dkv.shape, jnp.bfloat16),
            jax.ShapeDtypeStruct((owners, back_rows, LANES), jnp.bfloat16),
        ],
        scratch_shapes=[
            pltpu.VMEM((many, most * TILE + 64, LANES), jnp.float32),
            pltpu.VMEM((images, padded, LANES), jnp.float32),
        ]
        + math_scratch(padded, WAYS),
        input_output_aliases={5: 0},
        compiler_params=params(),
        cost_estimate=cost(us),
        name="far" + str(first),
    )(plan, wire, both, kkt, own_acc, dkv)


def exchange(x):
    return lax.all_to_all(x, "dp", split_axis=0, concat_axis=0, tiled=True)


def per_device(texts, query_weight, patch_key_value, grad_out, negatives):
    owners = lax.axis_size("dp")
    members = lax.axis_size("mp")
    member = lax.axis_index("mp")
    texts_here, length, depth = texts.shape
    images_here, heads, keys, _ = patch_key_value.shape
    width = query_weight.shape[0]
    captions = texts_here // images_here
    padded = cdiv(keys, 16) * 16
    count = texts_here * length
    slots = 2 * owners
    bf16, f32, i32 = jnp.bfloat16, jnp.float32, jnp.int32
    early = heads - 1
    first_rows = cdiv(2 * early * length + 2, 8) * 8
    later_rows = cdiv(2 * length, 8) * 8

    flat_text = texts.transpose(1, 0, 2).reshape(count, depth)
    neg = negatives.T
    all_weight = lax.all_gather(query_weight, "mp", axis=0, tiled=True)
    start_col = member * width // LANES * LANES
    odd = ((member * width - start_col) // HEAD_SIZE).reshape(1).astype(i32)
    window = lax.dynamic_slice_in_dim(grad_out, start_col, 2 * LANES, 3)

    wire_first, query, rank = pl.pallas_call(
        functools.partial(pack_first_kernel, early, images_here),
        in_specs=[SMEM, SMEM, VMEM, VMEM, VMEM],
        out_specs=[VMEM, VMEM, SMEM],
        out_shape=[
            jax.ShapeDtypeStruct((owners, first_rows, LANES), bf16),
            jax.ShapeDtypeStruct((heads, count, LANES), f32),
            jax.ShapeDtypeStruct(neg.shape, i32),
        ],
        scratch_shapes=[
            pltpu.VMEM((owners * first_rows, LANES), f32),
            pltpu.SMEM((owners,), i32),
        ],
        compiler_params=params(),
        cost_estimate=cost(5),
        name="pack_first",
    )(odd, neg, flat_text, query_weight, window)
    got_first = exchange(wire_first)

    own_acc, own_dq, both, kkt = pl.pallas_call(
        functools.partial(own_kernel, keys, padded, texts_here),
        grid=(images_here, heads),
        in_specs=[
            SMEM,
            pl.BlockSpec((1, count, LANES), lambda i, h: (h, 0, 0)),
            pl.BlockSpec((captions, 1, length, 2 * LANES), lambda i, h: (i, 0, 0, 0)),
            pl.BlockSpec((1, 1, keys, LANES), lambda i, h: (i, h, 0, 0)),
        ],
        out_specs=[
            pl.BlockSpec((1, 1, padded, LANES), lambda i, h: (i, h, 0, 0)),
            pl.BlockSpec((1, 1, TILE, LANES), lambda i, h: (i, h, 0, 0)),
            pl.BlockSpec((1, 1, 2 * padded, LANES), lambda i, h: (i, h, 0, 0)),
            pl.BlockSpec((1, 1, LANES, padded), lambda i, h: (i, h, 0, 0)),
        ],
        out_shape=[
            jax.ShapeDtypeStruct((images_here, heads, padded, LANES), f32),
            jax.ShapeDtypeStruct((images_here, heads, TILE, LANES), f32),
            jax.ShapeDtypeStruct((images_here, heads, 2 * padded, LANES), bf16),
            jax.ShapeDtypeStruct((images_here, heads, LANES, padded), bf16),
        ],
        scratch_shapes=[pltpu.VMEM((TILE, LANES), f32)] + math_scratch(padded, 1),
        compiler_params=params(),
        cost_estimate=cost(13),
        name="own",
    )(odd, query, window, patch_key_value)

    wire_later = pl.pallas_call(
        functools.partial(pack_later_kernel, early, heads - early, images_here),
        in_specs=[SMEM, SMEM, SMEM, VMEM, VMEM, ANY],
        out_specs=VMEM,
        out_shape=jax.ShapeDtypeStruct((owners, later_rows, LANES), bf16),
        scratch_shapes=[pltpu.VMEM((owners * later_rows, LANES), f32)],
        compiler_params=params(),
        cost_estimate=cost(4),
        name="pack_later",
    )(odd, neg, rank, query, window, own_acc)
    got_later = exchange(wire_later)

    tell = 2 * early * length
    got_id = got_first[:, tell : tell + 2, 0].astype(i32).reshape(-1)
    here = jnp.arange(images_here, dtype=i32)
    all_slots = jnp.arange(slots, dtype=i32)
    ahead = jnp.sum(
        (got_id[:, None] == got_id[None, :]) & (all_slots[None, :] < all_slots[:, None]), axis=1
    ).astype(i32)
    number = jnp.sum(got_id[:, None] == here[None, :], axis=0).astype(i32)
    tiles = (number * length + TILE - 1) // TILE
    base = jnp.sum(jnp.where(here[None, :] < here[:, None], tiles[None, :], 0), axis=1) * TILE
    start = jnp.sum(jnp.where(got_id[:, None] == here[None, :], base[None, :], 0), axis=1)
    pos = jnp.where(got_id >= 0, start + ahead * length, -1)
    plan = jnp.concatenate([pos, base, tiles]).astype(i32)

    dkv = jnp.zeros(patch_key_value.shape, bf16)
    dkv, back_first = far_call(
        plan, got_first, 0, early, both, kkt, own_acc, dkv, 22, length
    )
    home_first = exchange(back_first)
    dkv, back_later = far_call(
        plan, got_later, early, heads - early, both, kkt, own_acc, dkv, 12, length
    )
    home_later = exchange(back_later)

    half = depth // 2
    dq_first, weight_first = pl.pallas_call(
        functools.partial(gather_two_kernel, length, images_here),
        grid=(1,),
        in_specs=[
            SMEM,
            SMEM,
            VMEM,
            pl.BlockSpec((images_here, early, TILE, LANES), lambda n: (0, 0, 0, 0)),
            VMEM,
        ],
        out_specs=[VMEM, VMEM],
        out_shape=[
            jax.ShapeDtypeStruct((count, LANES), bf16),
            jax.ShapeDtypeStruct((early * HEAD_SIZE, depth), f32),
        ],
        scratch_shapes=[pltpu.VMEM((early, count, LANES), f32)],
        compiler_params=params(),
        cost_estimate=cost(4),
        name="gather_two",
    )(neg, rank, flat_text, own_dq, home_first)
    dq_later, weight_local = pl.pallas_call(
        functools.partial(gather_last_kernel, length, images_here),
        grid=(1,),
        in_specs=[
            SMEM,
            SMEM,
            VMEM,
            pl.BlockSpec((images_here, 1, TILE, LANES), lambda n: (0, early, 0, 0)),
            VMEM,
            VMEM,
        ],
        out_specs=[VMEM, VMEM],
        out_shape=[
            jax.ShapeDtypeStruct((count, LANES), bf16),
            jax.ShapeDtypeStruct((owners, 8, half), bf16),
        ],
        scratch_shapes=[pltpu.VMEM((1, count, LANES), f32)],
        compiler_params=params(),
        cost_estimate=cost(3),
        name="gather_last",
    )(neg, rank, flat_text, own_dq, home_later, weight_first)

    parts = exchange(weight_local)
    piece = pl.pallas_call(
        total_kernel,
        in_specs=[VMEM],
        out_specs=VMEM,
        out_shape=jax.ShapeDtypeStruct(parts.shape, bf16),
        compiler_params=params(),
        name="total",
    )(parts)
    weight_grad = pl.pallas_call(
        unfold_kernel,
        in_specs=[VMEM],
        out_specs=VMEM,
        out_shape=jax.ShapeDtypeStruct((width, depth), f32),
        compiler_params=params(),
        name="unfold",
    )(exchange(piece))

    mine = texts_here // members
    dq = jnp.concatenate([dq_first, dq_later[:, :HEAD_SIZE]], axis=1)
    dq = dq.reshape(length, texts_here, width)
    text_grad = jnp.zeros((length * mine, depth), f32)
    for r in range(members):
        to = lax.rem(member + r, members)
        block = lax.dynamic_slice_in_dim(dq, to * mine, mine, 1)
        if r:
            block = lax.ppermute(block, "mp", [(i, (i + r) % members) for i in range(members)])
        source = lax.rem(member + members - r, members)
        weight = lax.dynamic_slice_in_dim(all_weight, source * width, width, 0)
        text_grad = text_grad + jnp.dot(
            block.reshape(length * mine, width), weight, preferred_element_type=f32
        )
    text_grad = text_grad.astype(bf16).reshape(length, mine, depth).transpose(1, 0, 2)
    return (text_grad, weight_grad, dkv)


def solution(mesh):
    in_specs = (
        P("dp", None, None),
        P("mp", None),
        P("dp", "mp", None, None),
        P("dp", None, None, None),
        P("dp", None),
    )
    out_specs = (P(("dp", "mp"), None, None), P("mp", None), P("dp", "mp", None, None))
    return jax.shard_map(
        per_device, mesh=mesh, in_specs=in_specs, out_specs=out_specs, check_vma=False
    )
```

time: 1710 us -> 251 us (0.15); the launches traced: 1690 us -> 250 us
  local copies, waits for them, and re-layouts: 521 us -> 19.1 us
  matrix products: 470 us -> 6.38 us
  other arithmetic: 426 us -> 3.28 us
  waiting for transfers between devices: 215 us -> 79 us
  Pallas kernels: 0 us -> 72.2 us
    dot_general x50 -> x4, matrix products: 470 us -> 6.38 us  [per_device(): jnp.dot(block.reshape(length * mine, width), weight, preferred_element_ty...]
    scatter-add x9 -> x0, other arithmetic: 262 us -> none  [visit(): memory_acc = memory_acc.at[ids].add(pair_dkv)]
    gather x19 -> x0, local copies, waits for them, and re-layouts: 165 us -> none  [the longest x18 160 us: visit(): memory = jnp.take(patch_key_value, ids, axis=0)]
    concatenate x10 -> x0, local copies, waits for them, and re-layouts: 141 us -> none  [the longest x9 137 us: pair_grads(): return (pair_dq, jnp.concatenate([pair_dk, pair_dv], axis=-1))]
    psum x1 -> x0, waiting for transfers between devices: 118 us -> none  [per_device(): weight_grad = lax.psum(weight_local, 'dp')]
    pallas_call x0 -> x9, Pallas kernels: none -> 72.2 us  [the longest x2 33 us: far_call(): pl.pallas_call(functools.partial(far_kernel, keys, padded, length, many),...]
    select_n x21 -> x2, other arithmetic: 65.4 us -> 0.02 us  [the longest x1 0.01 us: per_device(): tiles = (number * length + TILE - 1) // TILE]
    concatenate x10 -> x2, other arithmetic: 61.4 us -> 0.7 us  [the longest x1 0.64 us: per_device(): plan = jnp.concatenate([pos, base, tiles]).astype(i32)]
  transfers between devices with their start and end apart: 5 -> 10, of which waited for: 3 -> 6; matrix products, arithmetic and copies ran while one was open for 13% -> 10% of each run, Pallas kernels for 0% -> 26%
where the time goes in v2:
time: 251 us; the launch traced here: 250 us
  waiting for transfers between devices  79 us (31%)
  Pallas kernels  72.2 us (29%)
  starting transfers between devices  55.3 us (22%)
  local copies, waits for them, and re-layouts  19.1 us (8%)
  between operations  14.3 us (6%)
  matrix products  6.38 us (3%)
  other arithmetic  3.28 us (1%)
    all_to_all x6, waiting for transfers between devices, exchange(): return lax.all_to_all(x, 'dp', split_axis=0, concat_axis=0, tiled=True)  78.3 us
    all_to_all x6, starting transfers between devices, exchange(): return lax.all_to_all(x, 'dp', split_axis=0, concat_axis=0, tiled=True)  50.9 us
    pallas_call x2, Pallas kernels, far_call(): pl.pallas_call(functools.partial(far_kernel, keys, padded, length, many),...  33 us
    pallas_call x1, Pallas kernels, per_device(): pl.pallas_call(functools.partial(own_kernel, keys, padded, texts_here), g...  15.8 us
    unnamed x11, local copies, waits for them, and re-layouts  9.64 us
    pallas_call x1, Pallas kernels, per_device(): pl.pallas_call(functools.partial(pack_first_kernel, early, images_here),...  6.43 us
    dot_general x4, matrix products, per_device(): jnp.dot(block.reshape(length * mine, width), weight, preferred_element_ty...  6.38 us
  transfers between devices with their start and end apart: 10, of which 6 were waited for; matrix products, arithmetic and copies ran while one was open for 10% of the time, Pallas kernels for 26%

profile of v2, /device:TPU:1, one launch (start us, length us, event | category | flops | bytes accessed | tf_op | source)
XLA Modules:
  0.0 249.6 jit_solution(6520378872112567081)
XLA Ops:
  7.2 1.9 copy-done
  9.1 0.4 constant_dynamic-slice_fusion.4
  9.5 1.3 copy.23.grad_ref
  10.9 6.4 %pack_first.1 = (bf16[64,144,128]{2,1,0:T(8,128)(2,1)}, f32[3,560,128]{2,1,0:T(8,128)}, s32[3,16]{1,0:T(4,128)}) custom-call(s32[1]{0:T(128)} %bitcast.1.odd_ref, s32[3,16]{1,0:T(4,128)} %bitcast.18, bf16[560,768]{1,0:T(8,128)(2,1)} %bitcast.15, bf16[192,768]{1,0:T(8,128)(2,1)} %weight_ref.1, bf16[16,4,35,256]{3,2,1,0:T(8,128)(2,1)} %copy.23.grad_ref), custom_call_target="tpu_custom_call" | custom-call | flops 2875000064 | bytes 18000000 | tf_op jit(solution)/shard_map/pack_first/pallas_call | solution.py:453
  17.3 13.3 %all-to-all-start = ((bf16[64,144,128]{2,1,0:T(8,128)(2,1)}), bf16[64,144,128]{2,1,0:T(8,128)(2,1)}, u32[]{:S(2)}, u32[]{:S(2)}) async-start(bf16[64,144,128]{2,1,0:T(8,128)(2,1)} %get-tuple-element.21), calls=%async_computation | async-start | bytes 4718592 | tf_op jit(solution)/shard_map/all_to_all | solution.py:427
  30.6 3.0 %copy.20.kv_ref = bf16[4,3,577,128]{3,2,1,0:T(8,128)(2,1)} copy(bf16[4,3,577,128]{3,0,2,1:T(4,128)(2,1)} %param.7) | data formatting | bytes 3545088 | tf_op args[2]
  33.6 15.8 %own.1 = (f32[4,3,592,128]{3,2,1,0:T(8,128)}, f32[4,3,256,128]{3,2,1,0:T(8,128)}, bf16[4,3,1184,128]{3,2,1,0:T(8,128)(2,1)}, bf16[4,3,128,592]{3,2,1,0:T(8,128)(2,1)}) custom-call(s32[1]{0:T(128)} %bitcast.1.odd_ref, f32[3,560,128]{2,1,0:T(8,128)} %get-tuple-element.19.query_ref, bf16[16,4,35,256]{3,2,1,0:T(8,128)(2,1)} %copy.23.grad_ref, ...), custom_call_target="tpu_custom_call" | custom-call | flops 7474999808 | bytes 46800000 | tf_op jit(solution)/shard_map/own/pallas_call | solution.py:472
  49.4 4.3 %pack_later.1 = bf16[64,72,128]{2,1,0:T(8,128)(2,1)} custom-call(s32[1]{0:T(128)} %bitcast.1.odd_ref, s32[3,16]{1,0:T(4,128)} %bitcast.19, s32[3,16]{1,0:T(4,128)} %get-tuple-element.18.rank_ref, f32[3,560,128]{2,1,0:T(8,128)} %get-tuple-element.19.query_ref, bf16[16,4,35,256]{3,2,1,0:T(8,128)(2,1)} %copy.23.grad_ref, ...), custom_call_target="tpu_custom_call" | custom-call | flops 2300000000 | bytes 14400000 | tf_op jit(solution)/shard_map/pack_later/pallas_call | solution.py:499
  53.7 32.0 %all-to-all-done.wire_ref = bf16[64,144,128]{2,1,0:T(8,128)(2,1)} async-done(((bf16[64,144,128]{2,1,0:T(8,128)(2,1)}), bf16[64,144,128]{2,1,0:T(8,128)(2,1)}, u32[]{:S(2)}, u32[]{:S(2)}) %all-to-all-start) | async-done | bytes 2359328 | tf_op jit(solution)/shard_map/all_to_all | solution.py:427
  85.7 7.3 %all-to-all-start.2 = ((bf16[64,72,128]{2,1,0:T(8,128)(2,1)}), bf16[64,72,128]{2,1,0:T(8,128)(2,1)}, u32[]{:S(2)}, u32[]{:S(2)}) async-start(bf16[64,72,128]{2,1,0:T(8,128)(2,1)} %pack_later.1), calls=%async_computation.2 | async-start | bytes 2359296 | tf_op jit(solution)/shard_map/all_to_all | solution.py:427
  93.1 2.1 convert_reduce_fusion
  95.1 0.1 reshape.74
  95.3 0.1 convert_reduce_fusion.2
  95.4 0.1 select_reduce_fusion.1
  95.5 0.1 select_reduce_fusion
  95.6 0.2 convert_reduce_fusion.1
  95.8 0.6 pad_add_fusion.plan_ref
  96.5 1.4 broadcast_in_dim.44.clone.dkv_in
  97.9 20.4 %far0.1 = (bf16[4,3,577,128]{3,2,1,0:T(8,128)(2,1)}, bf16[64,72,128]{2,1,0:T(8,128)(2,1)}) custom-call(s32[136]{0:T(256)} %pad_add_fusion.plan_ref, bf16[64,144,128]{2,1,0:T(8,128)(2,1)} %all-to-all-done.wire_ref, bf16[4,3,1184,128]{3,2,1,0:T(8,128)(2,1)} %get-tuple-element.22.both_ref, ...), custom_call_target="tpu_custom_call", output_to_operand_aliasing={{0}: (5, {})} | custom-call | flops 12650000384 | bytes 79200000 | tf_op jit(solution)/shard_map/far0/pallas_call | solution.py:395
  118.3 5.3 %all-to-all-done.2.wire_ref = bf16[64,72,128]{2,1,0:T(8,128)(2,1)} async-done(((bf16[64,72,128]{2,1,0:T(8,128)(2,1)}), bf16[64,72,128]{2,1,0:T(8,128)(2,1)}, u32[]{:S(2)}, u32[]{:S(2)}) %all-to-all-start.2) | async-done | bytes 1179680 | tf_op jit(solution)/shard_map/all_to_all | solution.py:427
  123.6 11.5 %all-to-all-start.1 = ((bf16[64,72,128]{2,1,0:T(8,128)(2,1)}), bf16[64,72,128]{2,1,0:T(8,128)(2,1)}, u32[]{:S(2)}, u32[]{:S(2)}) async-start(bf16[64,72,128]{2,1,0:T(8,128)(2,1)} %get-tuple-element.25), calls=%async_computation.1 | async-start | bytes 2359296 | tf_op jit(solution)/shard_map/all_to_all | solution.py:427
  135.1 12.6 %far2.1 = (bf16[4,3,577,128]{3,2,1,0:T(8,128)(2,1)}, bf16[64,40,128]{2,1,0:T(8,128)(2,1)}) custom-call(s32[136]{0:T(256)} %pad_add_fusion.plan_ref, bf16[64,72,128]{2,1,0:T(8,128)(2,1)} %all-to-all-done.2.wire_ref, bf16[4,3,1184,128]{3,2,1,0:T(8,128)(2,1)} %get-tuple-element.22.both_ref, ...), custom_call_target="tpu_custom_call", output_to_operand_aliasing={{0}: (5, {})} | custom-call | flops 6899999744 | bytes 43200000 | tf_op jit(solution)/shard_map/far2/pallas_call | solution.py:395
  147.7 17.9 %all-to-all-done.1.back_ref = bf16[64,72,128]{2,1,0:T(8,128)(2,1)} async-done(((bf16[64,72,128]{2,1,0:T(8,128)(2,1)}), bf16[64,72,128]{2,1,0:T(8,128)(2,1)}, u32[]{:S(2)}, u32[]{:S(2)}) %all-to-all-start.1) | async-done | bytes 1179680 | tf_op jit(solution)/shard_map/all_to_all | solution.py:427
  165.7 6.8 %all-to-all-start.3 = ((bf16[64,40,128]{2,1,0:T(8,128)(2,1)}), bf16[64,40,128]{2,1,0:T(8,128)(2,1)}, u32[]{:S(2)}, u32[]{:S(2)}) async-start(bf16[64,40,128]{2,1,0:T(8,128)(2,1)} %get-tuple-element.28), calls=%async_computation.3 | async-start | bytes 1310720 | tf_op jit(solution)/shard_map/all_to_all | solution.py:427
  172.5 0.7 all-gather.2.cloned.1.call-update
  173.2 4.7 %gather_two.1 = (bf16[560,128]{1,0:T(8,128)(2,1)}, f32[128,768]{1,0:T(8,128)}) custom-call(s32[3,16]{1,0:T(4,128)} %bitcast.20, s32[3,16]{1,0:T(4,128)} %get-tuple-element.18.rank_ref, bf16[560,768]{1,0:T(8,128)(2,1)} %bitcast.16, f32[4,3,256,128]{3,2,1,0:T(8,128)} %get-tuple-element.20.own_ref, bf16[64,72,128]{2,1,0:T(8,128)(2,1)} %all-to-all-done.1.back_ref), custom_call_target="tpu_custom_call" | custom-call | flops 2300000000 | bytes 14400000 | tf_op jit(solution)/shard_map/gather_two/pallas_call | solution.py:536
  177.9 14.9 %all-to-all-done.3.back_ref = bf16[64,40,128]{2,1,0:T(8,128)(2,1)} async-done(((bf16[64,40,128]{2,1,0:T(8,128)(2,1)}), bf16[64,40,128]{2,1,0:T(8,128)(2,1)}, u32[]{:S(2)}, u32[]{:S(2)}) %all-to-all-start.3) | async-done | bytes 655392 | tf_op jit(solution)/shard_map/all_to_all | solution.py:427
  192.8 4.3 %gather_last.1 = (bf16[560,128]{1,0:T(8,128)(2,1)}, bf16[64,8,384]{2,1,0:T(8,128)(2,1)}) custom-call(s32[3,16]{1,0:T(4,128)} %bitcast.21, s32[3,16]{1,0:T(4,128)} %get-tuple-element.18.rank_ref, bf16[560,768]{1,0:T(8,128)(2,1)} %bitcast.17, f32[4,3,256,128]{3,2,1,0:T(8,128)} %get-tuple-element.20.own_ref, bf16[64,40,128]{2,1,0:T(8,128)(2,1)} %all-to-all-done.3.back_ref, ...), custom_call_target="tpu_custom_call" | custom-call | flops 1724999936 | bytes 10800000 | tf_op jit(solution)/shard_map/gather_last/pallas_call | solution.py:556
  197.1 6.0 %all-to-all-start.4 = ((bf16[64,8,384]{2,1,0:T(8,128)(2,1)}), bf16[64,8,384]{2,1,0:T(8,128)(2,1)}, u32[]{:S(2)}, u32[]{:S(2)}) async-start(bf16[64,8,384]{2,1,0:T(8,128)(2,1)} %get-tuple-element.31), calls=%async_computation.4 | async-start | bytes 786432 | tf_op jit(solution)/shard_map/all_to_all | solution.py:427
  203.1 3.4 %copy.22 = bf16[4,3,577,128]{3,0,2,1:T(4,128)(2,1)} copy(bf16[4,3,577,128]{3,2,1,0:T(8,128)(2,1)} %get-tuple-element.44) | data formatting | bytes 3545088
  206.6 0.8 constant_dynamic-slice_fusion.1
  207.5 2.5 %collective-permute-start.2 = (bf16[35,4,192]{2,1,0:T(4,128)(2,1)}, bf16[35,4,192]{2,1,0:T(4,128)(2,1)}, u32[]{:S(2)}, u32[]{:S(2)}) collective-permute-start(bf16[35,4,192]{2,1,0:T(4,128)(2,1)} %get-tuple-element.46), channel_id=1, source_target_pairs={{0,3},{1,0},{2,1},{3,2},{4,7},{5,4},{6,5},{7,6},{8,11},{9,8},{10,9... | collective-permute-start | bytes 161288 | tf_op jit(solution)/shard_map/ppermute | solution.py:604
  210.0 0.9 reshape.69
  210.9 0.1 collective-permute-start
  211.0 1.7 collective-permute-start.1
  212.7 5.4 %all-to-all-done.4.parts_ref = bf16[64,8,384]{2,1,0:T(8,128)(2,1)} async-done(((bf16[64,8,384]{2,1,0:T(8,128)(2,1)}), bf16[64,8,384]{2,1,0:T(8,128)(2,1)}, u32[]{:S(2)}, u32[]{:S(2)}) %all-to-all-start.4) | async-done | bytes 393248 | tf_op jit(solution)/shard_map/all_to_all | solution.py:427
  218.1 1.9 total.1
  219.9 5.9 %all-to-all-start.5 = ((bf16[64,8,384]{2,1,0:T(8,128)(2,1)}), bf16[64,8,384]{2,1,0:T(8,128)(2,1)}, u32[]{:S(2)}, u32[]{:S(2)}) async-start(bf16[64,8,384]{2,1,0:T(8,128)(2,1)} %total.1), calls=%async_computation.5 | async-start | bytes 786432 | tf_op jit(solution)/shard_map/all_to_all | solution.py:427
  225.9 1.9 fusion.6
  227.9 1.6 reshape.72
  229.4 0.9 reshape.70
  230.4 1.5 reshape.71
  231.9 1.2 fusion.2
  233.2 1.3 convolution_add_fusion.1
  234.5 1.9 fusion.1
  236.4 1.7 reshape.73
  238.1 2.8 %all-to-all-done.5.pieces_ref = bf16[64,8,384]{2,1,0:T(8,128)(2,1)} async-done(((bf16[64,8,384]{2,1,0:T(8,128)(2,1)}), bf16[64,8,384]{2,1,0:T(8,128)(2,1)}, u32[]{:S(2)}, u32[]{:S(2)}) %all-to-all-start.5) | async-done | bytes 393248 | tf_op jit(solution)/shard_map/all_to_all | solution.py:427
  240.9 1.8 unfold.1
  (16 shorter events, 0.2 us)
Async XLA Ops:
  7.2 2.0 copy-start
  17.3 68.4 %all-to-all-start = ((bf16[64,144,128]{2,1,0:T(8,128)(2,1)}), bf16[64,144,128]{2,1,0:T(8,128)(2,1)}, u32[]{:S(2)}, u32[]{:S(2)}) async-start(bf16[64,144,128]{2,1,0:T(8,128)(2,1)} %get-tuple-element.21), calls=%async_computation | async-start | bytes 4718592 | tf_op jit(solution)/shard_map/all_to_all | solution.py:427
  85.7 37.9 %all-to-all-start.2 = ((bf16[64,72,128]{2,1,0:T(8,128)(2,1)}), bf16[64,72,128]{2,1,0:T(8,128)(2,1)}, u32[]{:S(2)}, u32[]{:S(2)}) async-start(bf16[64,72,128]{2,1,0:T(8,128)(2,1)} %pack_later.1), calls=%async_computation.2 | async-start | bytes 2359296 | tf_op jit(solution)/shard_map/all_to_all | solution.py:427
  123.6 42.1 %all-to-all-start.1 = ((bf16[64,72,128]{2,1,0:T(8,128)(2,1)}), bf16[64,72,128]{2,1,0:T(8,128)(2,1)}, u32[]{:S(2)}, u32[]{:S(2)}) async-start(bf16[64,72,128]{2,1,0:T(8,128)(2,1)} %get-tuple-element.25), calls=%async_computation.1 | async-start | bytes 2359296 | tf_op jit(solution)/shard_map/all_to_all | solution.py:427
  165.7 27.1 %all-to-all-start.3 = ((bf16[64,40,128]{2,1,0:T(8,128)(2,1)}), bf16[64,40,128]{2,1,0:T(8,128)(2,1)}, u32[]{:S(2)}, u32[]{:S(2)}) async-start(bf16[64,40,128]{2,1,0:T(8,128)(2,1)} %get-tuple-element.28), calls=%async_computation.3 | async-start | bytes 1310720 | tf_op jit(solution)/shard_map/all_to_all | solution.py:427
  172.5 53.4 %all-gather.2.cloned.1.call-start = ((), (), s32[]{:S(2)}) async-start(), calls=%async_computation.6 | async-start | bytes 1474560 | tf_op jit(solution)/shard_map/all_gather | solution.py:448
  197.1 21.0 %all-to-all-start.4 = ((bf16[64,8,384]{2,1,0:T(8,128)(2,1)}), bf16[64,8,384]{2,1,0:T(8,128)(2,1)}, u32[]{:S(2)}, u32[]{:S(2)}) async-start(bf16[64,8,384]{2,1,0:T(8,128)(2,1)} %get-tuple-element.31), calls=%async_computation.4 | async-start | bytes 786432 | tf_op jit(solution)/shard_map/all_to_all | solution.py:427
  203.1 3.4 %copy-start.2 = (bf16[560,128]{1,0:T(8,128)(2,1)S(1)}, bf16[560,128]{1,0:T(8,128)(2,1)}, u32[]{:S(2)}) copy-start(bf16[560,128]{1,0:T(8,128)(2,1)} %get-tuple-element.26) | copy-start | bytes 430084
  203.1 3.4 %copy-start.3 = (bf16[560,128]{1,0:T(8,128)(2,1)S(1)}, bf16[560,128]{1,0:T(8,128)(2,1)}, u32[]{:S(2)}) copy-start(bf16[560,128]{1,0:T(8,128)(2,1)} %get-tuple-element.30) | copy-start | bytes 430084
  207.5 20.4 %collective-permute-start.2 = (bf16[35,4,192]{2,1,0:T(4,128)(2,1)}, bf16[35,4,192]{2,1,0:T(4,128)(2,1)}, u32[]{:S(2)}, u32[]{:S(2)}) collective-permute-start(bf16[35,4,192]{2,1,0:T(4,128)(2,1)} %get-tuple-element.46), channel_id=1, source_target_pairs={{0,3},{1,0},{2,1},{3,2},{4,7},{5,4},{6,5},{7,6},{8,11},{9,8},{10,9... | collective-permute-start | bytes 161288 | tf_op jit(solution)/shard_map/ppermute | solution.py:604
  210.9 18.5 %collective-permute-start = (bf16[35,4,192]{2,1,0:T(4,128)(2,1)}, bf16[35,4,192]{2,1,0:T(4,128)(2,1)}, u32[]{:S(2)}, u32[]{:S(2)}) collective-permute-start(bf16[35,4,192]{2,1,0:T(4,128)(2,1)} %get-tuple-element.47), channel_id=1, source_target_pairs={{0,1},{1,2},{2,3},{3,0},{4,5},{5,6},{6,7},{7,4},{8,9},{9,10},{10,1... | collective-permute-start | bytes 161288 | tf_op jit(solution)/shard_map/ppermute | solution.py:604
  211.0 19.4 %collective-permute-start.1 = (bf16[35,4,192]{2,1,0:T(4,128)(2,1)}, bf16[35,4,192]{2,1,0:T(4,128)(2,1)}, u32[]{:S(2)}, u32[]{:S(2)}) collective-permute-start(bf16[35,4,192]{2,1,0:T(4,128)(2,1)} %get-tuple-element.45), channel_id=1, source_target_pairs={{0,2},{1,3},{2,0},{3,1},{4,6},{5,7},{6,4},{7,5},{8,10},{9,11},{10,... | collective-permute-start | bytes 161288 | tf_op jit(solution)/shard_map/ppermute | solution.py:604
  219.9 20.9 %all-to-all-start.5 = ((bf16[64,8,384]{2,1,0:T(8,128)(2,1)}), bf16[64,8,384]{2,1,0:T(8,128)(2,1)}, u32[]{:S(2)}, u32[]{:S(2)}) async-start(bf16[64,8,384]{2,1,0:T(8,128)(2,1)} %total.1), calls=%async_computation.5 | async-start | bytes 786432 | tf_op jit(solution)/shard_map/all_to_all | solution.py:427
  231.9 2.6 %copy-start.1 = (bf16[140,192]{1,0:T(8,128)(2,1)S(1)}, bf16[140,192]{1,0:T(8,128)(2,1)}, u32[]{:S(2)}) copy-start(bf16[140,192]{1,0:T(8,128)(2,1)} %reshape.71) | copy-start | bytes 161284
Sparse Core Ops, SparseCore 0:
  175.1 26.9 all-gather.1

commit v3 on v2

--- a/solution.py
+++ b/solution.py
@@ -12,6 +12,7 @@
 LANES = 128
 TILE = 256
 WAYS = 4
+PARTS = 4
 VMEM_LIMIT = 60 * 1024 * 1024
 
 
@@ -65,9 +66,10 @@
             query_ref[h, :, HEAD_SIZE:] = jnp.zeros((q.shape[0], HEAD_SIZE), jnp.float32)
 
 
-def pack_rows(first, heads, images_here, odd_ref, neg_ref, rank_ref, query_ref, grad_ref, wire_ref, scr):
+def place_rows(
+    first, heads, images_here, odd_ref, neg_ref, rank_ref, query_ref, grad_ref, wire_rows, scr
+):
     texts_here, slots, length, _ = grad_ref.shape
-    wire_rows = wire_ref.shape[1]
     tells = wire_rows >= 2 * heads * length + 2
     if tells:
         scr[...] = jnp.full(scr.shape, -1.0, jnp.float32)
@@ -91,21 +93,59 @@
         return carry
 
     lax.fori_loop(0, texts_here, one_text, 0)
-    wire_ref[...] = scr[...].reshape(wire_ref.shape).astype(jnp.bfloat16)
 
 
 def pack_first_kernel(
-    heads, images_here, odd_ref, neg_ref, text_ref, weight_ref, grad_ref, wire_ref, query_ref, rank_ref, scr, seen_ref
+    heads,
+    images_here,
+    odd_ref,
+    neg_ref,
+    text_ref,
+    weight_ref,
+    grad_hbm,
+    wire_hbm,
+    query_hbm,
+    rank_ref,
+    scr,
+    grad_scr,
+    query_scr,
+    wire_scr,
+    seen_ref,
+    sems,
 ):
-    request_slots(neg_ref, rank_ref, seen_ref, wire_ref.shape[0], images_here)
-    project(text_ref, weight_ref, query_ref)
-    pack_rows(0, heads, images_here, odd_ref, neg_ref, rank_ref, query_ref, grad_ref, wire_ref, scr)
+    load = pltpu.make_async_copy(grad_hbm, grad_scr, sems.at[0])
+    load.start()
+    request_slots(neg_ref, rank_ref, seen_ref, wire_scr.shape[0], images_here)
+    project(text_ref, weight_ref, query_scr)
+    keep = pltpu.make_async_copy(query_scr, query_hbm, sems.at[1])
+    keep.start()
+    load.wait()
+    place_rows(
+        0, heads, images_here, odd_ref, neg_ref, rank_ref, query_scr, grad_scr, wire_scr.shape[1], scr
+    )
+    owners, rows, _ = wire_scr.shape
+    part = owners // PARTS
+    sends = []
+    for p in range(PARTS):
+        block = scr[p * part * rows : (p + 1) * part * rows, :]
+        wire_scr[p * part : (p + 1) * part] = block.reshape(part, rows, LANES).astype(jnp.bfloat16)
+        send = pltpu.make_async_copy(
+            wire_scr.at[pl.ds(p * part, part)], wire_hbm.at[pl.ds(p * part, part)], sems.at[2 + p]
+        )
+        send.start()
+        sends.append(send)
+    keep.wait()
+    for send in sends:
+        send.wait()
 
 
 def pack_later_kernel(
     first, heads, images_here, odd_ref, neg_ref, rank_ref, query_ref, grad_ref, after_ref, wire_ref, scr
 ):
-    pack_rows(first, heads, images_here, odd_ref, neg_ref, rank_ref, query_ref, grad_ref, wire_ref, scr)
+    place_rows(
+        first, heads, images_here, odd_ref, neg_ref, rank_ref, query_ref, grad_ref, wire_ref.shape[1], scr
+    )
+    wire_ref[...] = scr[...].reshape(wire_ref.shape).astype(jnp.bfloat16)
 
 
 def load_memory(kv, keys, kv_ref, kkt_ref, padded):
@@ -185,6 +225,42 @@
     dq_ref[0, 0] = dq
 
 
+def plan_kernel(length, images, tell, wire_hbm, plan_ref, tail_scr, sem):
+    senders, rows, _ = tail_scr.shape
+    first = tell // 16 * 16
+    copy = pltpu.make_async_copy(wire_hbm.at[:, pl.ds(first, rows), :], tail_scr, sem)
+    copy.start()
+    copy.wait()
+    tail = tail_scr[...].astype(jnp.float32)
+    id0, id1 = tail[:, tell - first, :], tail[:, tell - first + 1, :]
+    lane = lax.broadcasted_iota(jnp.int32, (senders, LANES), 1)
+    image = lane.astype(jnp.float32)
+    hot0 = jnp.where(id0 == image, 1.0, 0.0)
+    hot1 = jnp.where(id1 == image, 1.0, 0.0)
+    both = hot0 + hot1
+    row = lax.broadcasted_iota(jnp.int32, (senders, senders), 0)
+    col = lax.broadcasted_iota(jnp.int32, (senders, senders), 1)
+    before = jnp.where(col < row, 1.0, 0.0).astype(jnp.bfloat16)
+    ahead = jnp.dot(before, both.astype(jnp.bfloat16), preferred_element_type=jnp.float32)
+    number = jnp.sum(both, axis=0, keepdims=True).astype(jnp.int32)
+    tiles = (number * length + (TILE - 1)) // TILE
+    tiles = jnp.broadcast_to(tiles, (8, LANES))
+    row = lax.broadcasted_iota(jnp.int32, (LANES, LANES), 0)
+    col = lax.broadcasted_iota(jnp.int32, (LANES, LANES), 1)
+    before = jnp.where(row < col, 1.0, 0.0).astype(jnp.bfloat16)
+    first_tile = jnp.dot(
+        tiles.astype(jnp.float32).astype(jnp.bfloat16), before, preferred_element_type=jnp.float32
+    )
+    at = first_tile[0:1] * TILE + ahead * length
+    pos0 = jnp.sum(hot0 * at, axis=1, keepdims=True)
+    pos1 = jnp.sum(hot1 * (at + hot0 * length), axis=1, keepdims=True)
+    pos0 = jnp.where(id0 >= 0, pos0, -1.0)
+    pos1 = jnp.where(id1 >= 0, pos1, -1.0)
+    plan_ref[:senders, :] = jnp.where(lane == 0, pos0, pos1).astype(jnp.int32)
+    low = lax.broadcasted_iota(jnp.int32, (8, LANES), 0)
+    plan_ref[senders:, :] = jnp.where(low == 0, first_tile.astype(jnp.int32), tiles)
+
+
 def far_kernel(
     keys,
     padded,
@@ -195,18 +271,14 @@
     both_ref,
     kkt_ref,
     own_ref,
-    dkv_in,
-    dkv_ref,
-    back_ref,
-    rows_scr,
-    acc_scr,
-    *pairs,
+    *rest,
 ):
     h = pl.program_id(0)
     images = both_ref.shape[0]
     senders = wire_ref.shape[0]
-    slots = 2 * senders
-    ways = len(pairs) // 2
+    dkv_ref, back_ref, rows_scr, acc_scr = rest[-4 - 2 * WAYS : -2 * WAYS]
+    pairs = rest[-2 * WAYS :]
+    ways = WAYS
     s_scrs, pd_scrs = pairs[:ways], pairs[ways:]
 
     @pl.when(h == 0)
@@ -218,20 +290,20 @@
                 )
 
         for i in range(images):
-            n = plan_ref[slots + images + i]
+            n = plan_ref[senders + 1, i]
 
             @pl.when(n > 0)
             def _():
-                clear(plan_ref[slots + i] + (n - 1) * TILE)
-
-        end = plan_ref[slots + images - 1] + plan_ref[slots + 2 * images - 1] * TILE
+                clear((plan_ref[senders, i] + n - 1) * TILE)
+
+        end = plan_ref[senders, images - 1] + plan_ref[senders + 1, images - 1]
         for w in range(ways - 1):
-            clear(end + w * TILE)
+            clear((end + w) * TILE)
 
         def place(s, carry):
             block = wire_ref[s].astype(jnp.float32)
             for r in range(2):
-                pos = plan_ref[2 * s + r]
+                pos = plan_ref[s, r]
 
                 @pl.when(pos >= 0)
                 def _():
@@ -245,8 +317,8 @@
 
     for i in range(images):
         acc_scr[i] = own_ref[i, 0]
-    edges = [plan_ref[slots + i] // TILE for i in range(1, images)]
-    tiles = plan_ref[slots + images - 1] // TILE + plan_ref[slots + 2 * images - 1]
+    edges = [plan_ref[senders, i] for i in range(1, images)]
+    tiles = plan_ref[senders, images - 1] + plan_ref[senders + 1, images - 1]
 
     def step(k, carry):
         starts, images_of, rows = [], [], []
@@ -279,8 +351,8 @@
         spare = rows - heads * length
 
         def give(s, carry):
-            p0 = jnp.maximum(plan_ref[2 * s], 0)
-            p1 = jnp.maximum(plan_ref[2 * s + 1], 0)
+            p0 = jnp.maximum(plan_ref[s, 0], 0)
+            p1 = jnp.maximum(plan_ref[s, 1], 0)
             parts = []
             for g in range(heads):
                 x0 = rows_scr[g, pl.ds(p0, length), :]
@@ -294,7 +366,7 @@
         lax.fori_loop(0, senders, give, 0)
 
 
-def sum_requests(heads, length, images_here, neg_ref, rank_ref, own_ref, back_ref, sum_scr):
+def sum_requests(heads, length, images_here, neg_ref, rank_ref, own_ref, back_ref, sum_scr, text_scr):
     texts_here = sum_scr.shape[1] // length
     captions = texts_here // images_here
 
@@ -311,31 +383,39 @@
                 totals[h] = totals[h] + block[h * length : (h + 1) * length]
         for h in range(heads):
             sum_scr[h, pl.ds(t, length, stride=texts_here), :] = totals[h]
+            text_scr[h, pl.ds(t * length, length), :] = totals[h]
         return carry
 
     lax.fori_loop(0, texts_here, one, 0)
 
 
 def gather_two_kernel(
-    length, images_here, neg_ref, rank_ref, text_ref, own_ref, back_ref, dq_ref, weight_ref, sum_scr
+    length, images_here, neg_ref, rank_ref, text_ref, own_ref, back_ref, dq_ref, weight_ref, sum_scr, text_scr
 ):
-    sum_requests(2, length, images_here, neg_ref, rank_ref, own_ref, back_ref, sum_scr)
-    pair = jnp.where(
-        lower_half(sum_scr.shape[1:]), sum_scr[0], pltpu.roll(sum_scr[1], HEAD_SIZE, 1)
-    )
-    dq = pair.astype(jnp.bfloat16)
-    dq_ref[...] = dq
+    sum_requests(2, length, images_here, neg_ref, rank_ref, own_ref, back_ref, sum_scr, text_scr)
+    members, mine, _ = dq_ref.shape
+
+    def paired(x0, x1):
+        x = jnp.where(lower_half(x0.shape), x0, pltpu.roll(x1, HEAD_SIZE, 1))
+        return x.astype(jnp.bfloat16)
+
+    for m in range(members):
+        at = slice(m * mine, (m + 1) * mine)
+        dq_ref[m] = paired(text_scr[0, at, :], text_scr[1, at, :])
+    dq = paired(sum_scr[0], sum_scr[1])
     weight_ref[...] = lax.dot_general(
         dq, text_ref[...], (((0,), (0,)), ((), ())), preferred_element_type=jnp.float32
     )
 
 
 def gather_last_kernel(
-    length, images_here, neg_ref, rank_ref, text_ref, own_ref, back_ref, head_ref, dq_ref, weight_ref, sum_scr
+    length, images_here, neg_ref, rank_ref, text_ref, own_ref, back_ref, head_ref, after_ref, dq_ref, weight_ref, sum_scr, text_scr
 ):
-    sum_requests(1, length, images_here, neg_ref, rank_ref, own_ref, back_ref, sum_scr)
+    sum_requests(1, length, images_here, neg_ref, rank_ref, own_ref, back_ref, sum_scr, text_scr)
+    members, mine, _ = dq_ref.shape
+    for m in range(members):
+        dq_ref[m] = text_scr[0, m * mine : (m + 1) * mine, :].astype(jnp.bfloat16)
     dq = sum_scr[0].astype(jnp.bfloat16)
-    dq_ref[...] = dq
     last = lax.dot_general(
         dq, text_ref[...], (((0,), (0,)), ((), ())), preferred_element_type=jnp.float32
     )
@@ -386,10 +466,10 @@
     ] * ways
 
 
-def far_call(plan, wire, first, many, both, kkt, own_acc, dkv, us, length):
+def far_call(plan, wire, first, many, both, kkt, own_acc, dkv, keys, us, length):
     owners, rows, _ = wire.shape
-    images, _, keys, _ = dkv.shape
-    padded = own_acc.shape[2]
+    images, all_heads, padded, _ = own_acc.shape
+    more = () if dkv is None else (dkv,)
     back_rows = cdiv(many * length, 8) * 8
     most = (2 * owners * length) // TILE + images + WAYS - 1
     return pl.pallas_call(
@@ -401,14 +481,14 @@
             pl.BlockSpec((images, 1, 2 * padded, LANES), lambda h: (0, first + h, 0, 0)),
             pl.BlockSpec((images, 1, LANES, padded), lambda h: (0, first + h, 0, 0)),
             pl.BlockSpec((images, 1, padded, LANES), lambda h: (0, first + h, 0, 0)),
-            ANY,
-        ],
+        ]
+        + [ANY] * len(more),
         out_specs=[
             pl.BlockSpec((images, 1, keys, LANES), lambda h: (0, first + h, 0, 0)),
             pl.BlockSpec((owners, back_rows, LANES), lambda h: (0, 0, 0)),
         ],
         out_shape=[
-            jax.ShapeDtypeStruct(dkv.shape, jnp.bfloat16),
+            jax.ShapeDtypeStruct((images, all_heads, keys, LANES), jnp.bfloat16),
             jax.ShapeDtypeStruct((owners, back_rows, LANES), jnp.bfloat16),
         ],
         scratch_shapes=[
@@ -416,11 +496,11 @@
             pltpu.VMEM((images, padded, LANES), jnp.float32),
         ]
         + math_scratch(padded, WAYS),
-        input_output_aliases={5: 0},
+        input_output_aliases={5: 0} if more else {},
         compiler_params=params(),
         cost_estimate=cost(us),
         name="far" + str(first),
-    )(plan, wire, both, kkt, own_acc, dkv)
+    )(plan, wire, both, kkt, own_acc, *more)
 
 
 def exchange(x):
@@ -437,7 +517,6 @@
     captions = texts_here // images_here
     padded = cdiv(keys, 16) * 16
     count = texts_here * length
-    slots = 2 * owners
     bf16, f32, i32 = jnp.bfloat16, jnp.float32, jnp.int32
     early = heads - 1
     first_rows = cdiv(2 * early * length + 2, 8) * 8
@@ -452,8 +531,8 @@
 
     wire_first, query, rank = pl.pallas_call(
         functools.partial(pack_first_kernel, early, images_here),
-        in_specs=[SMEM, SMEM, VMEM, VMEM, VMEM],
-        out_specs=[VMEM, VMEM, SMEM],
+        in_specs=[SMEM, SMEM, VMEM, VMEM, ANY],
+        out_specs=[ANY, ANY, SMEM],
         out_shape=[
             jax.ShapeDtypeStruct((owners, first_rows, LANES), bf16),
             jax.ShapeDtypeStruct((heads, count, LANES), f32),
@@ -461,7 +540,11 @@
         ],
         scratch_shapes=[
             pltpu.VMEM((owners * first_rows, LANES), f32),
+            pltpu.VMEM(window.shape, bf16),
+            pltpu.VMEM((heads, count, LANES), f32),
+            pltpu.VMEM((owners, first_rows, LANES), bf16),
             pltpu.SMEM((owners,), i32),
+            pltpu.SemaphoreType.DMA((2 + PARTS,)),
         ],
         compiler_params=params(),
         cost_estimate=cost(5),
@@ -509,26 +592,26 @@
     got_later = exchange(wire_later)
 
     tell = 2 * early * length
-    got_id = got_first[:, tell : tell + 2, 0].astype(i32).reshape(-1)
-    here = jnp.arange(images_here, dtype=i32)
-    all_slots = jnp.arange(slots, dtype=i32)
-    ahead = jnp.sum(
-        (got_id[:, None] == got_id[None, :]) & (all_slots[None, :] < all_slots[:, None]), axis=1
-    ).astype(i32)
-    number = jnp.sum(got_id[:, None] == here[None, :], axis=0).astype(i32)
-    tiles = (number * length + TILE - 1) // TILE
-    base = jnp.sum(jnp.where(here[None, :] < here[:, None], tiles[None, :], 0), axis=1) * TILE
-    start = jnp.sum(jnp.where(got_id[:, None] == here[None, :], base[None, :], 0), axis=1)
-    pos = jnp.where(got_id >= 0, start + ahead * length, -1)
-    plan = jnp.concatenate([pos, base, tiles]).astype(i32)
-
-    dkv = jnp.zeros(patch_key_value.shape, bf16)
+    plan = pl.pallas_call(
+        functools.partial(plan_kernel, length, images_here, tell),
+        in_specs=[ANY],
+        out_specs=VMEM,
+        out_shape=jax.ShapeDtypeStruct((owners + 8, LANES), i32),
+        scratch_shapes=[
+            pltpu.VMEM((owners, first_rows - tell // 16 * 16, LANES), bf16),
+            pltpu.SemaphoreType.DMA,
+        ],
+        compiler_params=params(),
+        cost_estimate=cost(2),
+        name="plan",
+    )(got_first)
+
     dkv, back_first = far_call(
-        plan, got_first, 0, early, both, kkt, own_acc, dkv, 22, length
+        plan, got_first, 0, early, both, kkt, own_acc, None, keys, 22, length
     )
     home_first = exchange(back_first)
     dkv, back_later = far_call(
-        plan, got_later, early, heads - early, both, kkt, own_acc, dkv, 12, length
+        plan, got_later, early, heads - early, both, kkt, own_acc, dkv, keys, 12, length
     )
     home_later = exchange(back_later)
 
@@ -545,14 +628,33 @@
         ],
         out_specs=[VMEM, VMEM],
         out_shape=[
-            jax.ShapeDtypeStruct((count, LANES), bf16),
+            jax.ShapeDtypeStruct((members, count // members, LANES), bf16),
             jax.ShapeDtypeStruct((early * HEAD_SIZE, depth), f32),
         ],
-        scratch_shapes=[pltpu.VMEM((early, count, LANES), f32)],
+        scratch_shapes=[pltpu.VMEM((early, count, LANES), f32)] * 2,
         compiler_params=params(),
         cost_estimate=cost(4),
         name="gather_two",
     )(neg, rank, flat_text, own_dq, home_first)
+    def swap(dq):
+        rows = []
+        for r in range(members):
+            block = lax.dynamic_index_in_dim(dq, lax.rem(member + r, members), 0, False)
+            if r:
+                block = lax.ppermute(block, "mp", [(i, (i + r) % members) for i in range(members)])
+            rows.append(block)
+        return rows
+
+    def text_part(rows, skip, wide):
+        total = None
+        for r in range(members):
+            source = lax.rem(member + members - r, members)
+            weight = lax.dynamic_slice_in_dim(all_weight, source * width + skip, wide, 0)
+            part = jnp.dot(rows[r][:, :wide], weight, preferred_element_type=f32)
+            total = part if total is None else total + part
+        return total
+
+    rows_first = swap(dq_first)
     dq_later, weight_local = pl.pallas_call(
         functools.partial(gather_last_kernel, length, images_here),
         grid=(1,),
@@ -563,17 +665,18 @@
             pl.BlockSpec((images_here, 1, TILE, LANES), lambda n: (0, early, 0, 0)),
             VMEM,
             VMEM,
+            ANY,
         ],
         out_specs=[VMEM, VMEM],
         out_shape=[
-            jax.ShapeDtypeStruct((count, LANES), bf16),
+            jax.ShapeDtypeStruct((members, count // members, LANES), bf16),
             jax.ShapeDtypeStruct((owners, 8, half), bf16),
         ],
-        scratch_shapes=[pltpu.VMEM((1, count, LANES), f32)],
+        scratch_shapes=[pltpu.VMEM((1, count, LANES), f32)] * 2,
         compiler_params=params(),
         cost_estimate=cost(3),
         name="gather_last",
-    )(neg, rank, flat_text, own_dq, home_later, weight_first)
+    )(neg, rank, flat_text, own_dq, home_later, weight_first, rows_first[-1])
 
     parts = exchange(weight_local)
     piece = pl.pallas_call(
@@ -593,21 +696,10 @@
         name="unfold",
     )(exchange(piece))
 
-    mine = texts_here // members
-    dq = jnp.concatenate([dq_first, dq_later[:, :HEAD_SIZE]], axis=1)
-    dq = dq.reshape(length, texts_here, width)
-    text_grad = jnp.zeros((length * mine, depth), f32)
-    for r in range(members):
-        to = lax.rem(member + r, members)
-        block = lax.dynamic_slice_in_dim(dq, to * mine, mine, 1)
-        if r:
-            block = lax.ppermute(block, "mp", [(i, (i + r) % members) for i in range(members)])
-        source = lax.rem(member + members - r, members)
-        weight = lax.dynamic_slice_in_dim(all_weight, source * width, width, 0)
-        text_grad = text_grad + jnp.dot(
-            block.reshape(length * mine, width), weight, preferred_element_type=f32
-        )
-    text_grad = text_grad.astype(bf16).reshape(length, mine, depth).transpose(1, 0, 2)
+    rows_later = swap(dq_later)
+    text_grad = text_part(rows_first, 0, early * HEAD_SIZE)
+    text_grad = text_grad + text_part(rows_later, early * HEAD_SIZE, (heads - early) * HEAD_SIZE)
+    text_grad = text_grad.astype(bf16).reshape(texts_here // members, length, depth)
     return (text_grad, weight_grad, dkv)
 
 

time: 251 us -> 250 us (level)
  Pallas kernels: 72.2 us -> 60.5 us
  waiting for transfers between devices: 79 us -> 86.8 us
  matrix products: 6.38 us -> 13 us
  other arithmetic: 3.28 us -> 0 us
    pallas_call x2, Pallas kernels: 33 us -> 19.3 us  [far_call(): pl.pallas_call(functools.partial(far_kernel, keys, padded, length, many),...]
    all_to_all x6, waiting for transfers between devices: 78.3 us -> 86.1 us  [exchange(): return lax.all_to_all(x, 'dp', split_axis=0, concat_axis=0, tiled=True)]
    dot_general x4 -> x8, matrix products: 6.38 us -> 13 us  [text_part(): part = jnp.dot(rows[r][:, :wide], weight, preferred_element_type=f32)]
    reshape x5 -> x1, local copies, waits for them, and re-layouts: 6.65 us -> 1.69 us  [per_device(): text_grad.astype(bf16).reshape(texts_here // members, length, depth)]
    ppermute x3 -> x6, starting transfers between devices: 4.3 us -> 7.68 us  [swap(): lax.ppermute(block, 'mp', [(i, (i + r) % members) for i in range(members)])]
    squeeze x0 -> x2, local copies, waits for them, and re-layouts: none -> 2.93 us  [swap(): block = lax.dynamic_index_in_dim(dq, lax.rem(member + r, members), 0, False)]
    unnamed x11 -> x14, local copies, waits for them, and re-layouts: 9.64 us -> 11.9 us
  transfers between devices with their start and end apart: 10 -> 13, of which waited for: 6 -> 6; matrix products, arithmetic and copies ran while one was open for 10% -> 10% of each run, Pallas kernels for 26% -> 21%
where the time goes in v3:
time: 250 us; the launch traced here: 248 us
  waiting for transfers between devices  86.8 us (35%)
  Pallas kernels  60.5 us (24%)
  starting transfers between devices  56.9 us (23%)
  local copies, waits for them, and re-layouts  16.9 us (7%)
  between operations  14.3 us (6%)
  matrix products  13 us (5%)
    all_to_all x6, waiting for transfers between devices, exchange(): return lax.all_to_all(x, 'dp', split_axis=0, concat_axis=0, tiled=True)  86.1 us
    all_to_all x6, starting transfers between devices, exchange(): return lax.all_to_all(x, 'dp', split_axis=0, concat_axis=0, tiled=True)  49.2 us
    pallas_call x2, Pallas kernels, far_call(): pl.pallas_call(functools.partial(far_kernel, keys, padded, length, many),...  19.3 us
    pallas_call x1, Pallas kernels, per_device(): pl.pallas_call(functools.partial(own_kernel, keys, padded, texts_here), g...  15.9 us
    dot_general x8, matrix products, text_part(): part = jnp.dot(rows[r][:, :wide], weight, preferred_element_type=f32)  13 us
    unnamed x14, local copies, waits for them, and re-layouts  11.9 us
    ppermute x6, starting transfers between devices, swap(): lax.ppermute(block, 'mp', [(i, (i + r) % members) for i in range(members)])  7.68 us
    pallas_call x1, Pallas kernels, per_device(): pl.pallas_call(functools.partial(pack_first_kernel, early, images_here),...  6.45 us
  transfers between devices with their start and end apart: 13, of which 6 were waited for; matrix products, arithmetic and copies ran while one was open for 10% of the time, Pallas kernels for 21%

profile of v3, /device:TPU:1, one launch (start us, length us, event | category | flops | bytes accessed | tf_op | source)
XLA Modules:
  0.0 248.5 jit_solution(15481061925507132825)
XLA Ops:
  7.2 1.9 copy-done
  9.1 0.4 constant_dynamic-slice_fusion
  9.5 1.3 copy.17.grad_hbm.grad_ref
  10.8 6.5 %pack_first.1 = (bf16[64,144,128]{2,1,0:T(8,128)(2,1)}, f32[3,560,128]{2,1,0:T(8,128)}, s32[3,16]{1,0:T(4,128)}) custom-call(s32[1]{0:T(128)} %bitcast.1.odd_ref, s32[3,16]{1,0:T(4,128)} %bitcast.28, bf16[560,768]{1,0:T(8,128)(2,1)} %bitcast.25, bf16[192,768]{1,0:T(8,128)(2,1)} %weight_ref.1, bf16[16,4,35,256]{3,2,1,0:T(8,128)(2,1)} %copy.17.grad_hbm.grad_ref), custom_call_target="tpu_custom_call" | custom-call | flops 2875000064 | bytes 18000000 | tf_op jit(solution)/shard_map/pack_first/pallas_call | solution.py:532
  17.3 13.3 %all-to-all-start = ((bf16[64,144,128]{2,1,0:T(8,128)(2,1)}), bf16[64,144,128]{2,1,0:T(8,128)(2,1)}, u32[]{:S(2)}, u32[]{:S(2)}) async-start(bf16[64,144,128]{2,1,0:T(8,128)(2,1)} %get-tuple-element.21), calls=%async_computation | async-start | bytes 4718592 | tf_op jit(solution)/shard_map/all_to_all | solution.py:507
  30.6 2.9 %copy.14.kv_ref = bf16[4,3,577,128]{3,2,1,0:T(8,128)(2,1)} copy(bf16[4,3,577,128]{3,0,2,1:T(4,128)(2,1)} %param.7) | data formatting | bytes 3545088 | tf_op args[2]
  33.6 15.9 %own.1 = (f32[4,3,592,128]{3,2,1,0:T(8,128)}, f32[4,3,256,128]{3,2,1,0:T(8,128)}, bf16[4,3,1184,128]{3,2,1,0:T(8,128)(2,1)}, bf16[4,3,128,592]{3,2,1,0:T(8,128)(2,1)}) custom-call(s32[1]{0:T(128)} %bitcast.1.odd_ref, f32[3,560,128]{2,1,0:T(8,128)} %get-tuple-element.19.query_ref, bf16[16,4,35,256]{3,2,1,0:T(8,128)(2,1)} %copy.17.grad_hbm.grad_ref, ...), custom_call_target="tpu_custom_call" | custom-call | flops 7474999808 | bytes 46800000 | tf_op jit(solution)/shard_map/own/pallas_call | solution.py:555
  49.4 4.3 %pack_later.1 = bf16[64,72,128]{2,1,0:T(8,128)(2,1)} custom-call(s32[1]{0:T(128)} %bitcast.1.odd_ref, s32[3,16]{1,0:T(4,128)} %bitcast.29, s32[3,16]{1,0:T(4,128)} %get-tuple-element.18.rank_ref, f32[3,560,128]{2,1,0:T(8,128)} %get-tuple-element.19.query_ref, bf16[16,4,35,256]{3,2,1,0:T(8,128)(2,1)} %copy.17.grad_hbm.grad_ref, ...), custom_call_target="tpu_custom_call" | custom-call | flops 2300000000 | bytes 14400000 | tf_op jit(solution)/shard_map/pack_later/pallas_call | solution.py:582
  53.7 32.0 %all-to-all-done.wire_hbm.wire_ref = bf16[64,144,128]{2,1,0:T(8,128)(2,1)} async-done(((bf16[64,144,128]{2,1,0:T(8,128)(2,1)}), bf16[64,144,128]{2,1,0:T(8,128)(2,1)}, u32[]{:S(2)}, u32[]{:S(2)}) %all-to-all-start) | async-done | bytes 2359328 | tf_op jit(solution)/shard_map/all_to_all | solution.py:507
  85.7 7.3 %all-to-all-start.2 = ((bf16[64,72,128]{2,1,0:T(8,128)(2,1)}), bf16[64,72,128]{2,1,0:T(8,128)(2,1)}, u32[]{:S(2)}, u32[]{:S(2)}) async-start(bf16[64,72,128]{2,1,0:T(8,128)(2,1)} %pack_later.1), calls=%async_computation.2 | async-start | bytes 2359296 | tf_op jit(solution)/shard_map/all_to_all | solution.py:507
  93.0 1.9 plan.1.plan_ref
  94.9 11.3 %far0.1 = (bf16[4,3,577,128]{3,2,1,0:T(8,128)(2,1)}, bf16[64,72,128]{2,1,0:T(8,128)(2,1)}) custom-call(s32[72,128]{1,0:T(8,128)} %plan.1.plan_ref, bf16[64,144,128]{2,1,0:T(8,128)(2,1)} %all-to-all-done.wire_hbm.wire_ref, bf16[4,3,1184,128]{3,2,1,0:T(8,128)(2,1)} %get-tuple-element.22.both_ref, bf16[4,3,128,592]{3,2,1,0:T(8,128)(2,1)} %get-tuple-element.23.kkt_ref, ...), custom_call_target="tpu_custom_call" | custom-call | flops 12650000384 | bytes 79200000 | tf_op jit(solution)/shard_map/far0/pallas_call | solution.py:475
  106.2 17.4 %all-to-all-done.2.wire_ref = bf16[64,72,128]{2,1,0:T(8,128)(2,1)} async-done(((bf16[64,72,128]{2,1,0:T(8,128)(2,1)}), bf16[64,72,128]{2,1,0:T(8,128)(2,1)}, u32[]{:S(2)}, u32[]{:S(2)}) %all-to-all-start.2) | async-done | bytes 1179680 | tf_op jit(solution)/shard_map/all_to_all | solution.py:507
  123.6 7.9 %all-to-all-start.1 = ((bf16[64,72,128]{2,1,0:T(8,128)(2,1)}), bf16[64,72,128]{2,1,0:T(8,128)(2,1)}, u32[]{:S(2)}, u32[]{:S(2)}) async-start(bf16[64,72,128]{2,1,0:T(8,128)(2,1)} %get-tuple-element.25), calls=%async_computation.1 | async-start | bytes 2359296 | tf_op jit(solution)/shard_map/all_to_all | solution.py:507
  131.5 0.0 all-gather.2.cloned.1.call-start
  131.5 0.7 all-gather.2.cloned.1.call-update
  132.2 8.0 %far2.1 = (bf16[4,3,577,128]{3,2,1,0:T(8,128)(2,1)}, bf16[64,40,128]{2,1,0:T(8,128)(2,1)}) custom-call(s32[72,128]{1,0:T(8,128)} %plan.1.plan_ref, bf16[64,72,128]{2,1,0:T(8,128)(2,1)} %all-to-all-done.2.wire_ref, bf16[4,3,1184,128]{3,2,1,0:T(8,128)(2,1)} %get-tuple-element.22.both_ref, ...), custom_call_target="tpu_custom_call", output_to_operand_aliasing={{0}: (5, {})} | custom-call | flops 6899999744 | bytes 43200000 | tf_op jit(solution)/shard_map/far2/pallas_call | solution.py:475
  140.2 21.8 %all-to-all-done.1.back_ref = bf16[64,72,128]{2,1,0:T(8,128)(2,1)} async-done(((bf16[64,72,128]{2,1,0:T(8,128)(2,1)}), bf16[64,72,128]{2,1,0:T(8,128)(2,1)}, u32[]{:S(2)}, u32[]{:S(2)}) %all-to-all-start.1) | async-done | bytes 1179680 | tf_op jit(solution)/shard_map/all_to_all | solution.py:507
  162.0 7.0 %all-to-all-start.3 = ((bf16[64,40,128]{2,1,0:T(8,128)(2,1)}), bf16[64,40,128]{2,1,0:T(8,128)(2,1)}, u32[]{:S(2)}, u32[]{:S(2)}) async-start(bf16[64,40,128]{2,1,0:T(8,128)(2,1)} %get-tuple-element.28), calls=%async_computation.3 | async-start | bytes 1310720 | tf_op jit(solution)/shard_map/all_to_all | solution.py:507
  169.1 3.4 %copy.16 = bf16[4,3,577,128]{3,0,2,1:T(4,128)(2,1)} copy(bf16[4,3,577,128]{3,2,1,0:T(8,128)(2,1)} %get-tuple-element.38) | data formatting | bytes 3545088
  172.4 4.8 %gather_two.1 = (bf16[4,140,128]{2,1,0:T(8,128)(2,1)}, f32[128,768]{1,0:T(8,128)}) custom-call(s32[3,16]{1,0:T(4,128)} %bitcast.30, s32[3,16]{1,0:T(4,128)} %get-tuple-element.18.rank_ref, bf16[560,768]{1,0:T(8,128)(2,1)} %bitcast.26, f32[4,3,256,128]{3,2,1,0:T(8,128)} %get-tuple-element.20.own_ref, bf16[64,72,128]{2,1,0:T(8,128)(2,1)} %all-to-all-done.1.back_ref), custom_call_target="tpu_custom_call" | custom-call | flops 2300000000 | bytes 14400000 | tf_op jit(solution)/shard_map/gather_two/pallas_call | solution.py:619
  177.2 1.4 dynamic-slice_bitcast_fusion.5
  178.6 1.2 collective-permute-start
  179.8 1.5 collective-permute-start.2
  181.3 1.5 collective-permute-start.1
  182.8 1.9 fusion.8
  184.8 4.5 %all-to-all-done.3.back_ref = bf16[64,40,128]{2,1,0:T(8,128)(2,1)} async-done(((bf16[64,40,128]{2,1,0:T(8,128)(2,1)}), bf16[64,40,128]{2,1,0:T(8,128)(2,1)}, u32[]{:S(2)}, u32[]{:S(2)}) %all-to-all-start.3) | async-done | bytes 655392 | tf_op jit(solution)/shard_map/all_to_all | solution.py:507
  189.3 0.6 copy-done.4
  189.9 4.3 %gather_last.1 = (bf16[4,140,128]{2,1,0:T(8,128)(2,1)}, bf16[64,8,384]{2,1,0:T(8,128)(2,1)}) custom-call(s32[3,16]{1,0:T(4,128)} %bitcast.31, s32[3,16]{1,0:T(4,128)} %get-tuple-element.18.rank_ref, bf16[560,768]{1,0:T(8,128)(2,1)} %bitcast.27, f32[4,3,256,128]{3,2,1,0:T(8,128)} %get-tuple-element.20.own_ref, bf16[64,40,128]{2,1,0:T(8,128)(2,1)} %all-to-all-done.3.back_ref, ...), custom_call_target="tpu_custom_call" | custom-call | flops 1724999936 | bytes 10800000 | tf_op jit(solution)/shard_map/gather_last/pallas_call | solution.py:658
  194.2 6.8 %all-to-all-start.4 = ((bf16[64,8,384]{2,1,0:T(8,128)(2,1)}), bf16[64,8,384]{2,1,0:T(8,128)(2,1)}, u32[]{:S(2)}, u32[]{:S(2)}) async-start(bf16[64,8,384]{2,1,0:T(8,128)(2,1)} %get-tuple-element.31), calls=%async_computation.4 | async-start | bytes 786432 | tf_op jit(solution)/shard_map/all_to_all | solution.py:507
  201.0 1.5 dynamic-slice_bitcast_fusion.1
  202.5 0.5 collective-permute-start.3
  202.9 2.2 collective-permute-start.5
  205.1 0.8 collective-permute-start.4
  205.9 1.9 fusion.4
  207.8 1.9 convolution_add_fusion.3
  209.7 1.9 fusion.14
  211.6 4.4 %all-to-all-done.4.parts_ref = bf16[64,8,384]{2,1,0:T(8,128)(2,1)} async-done(((bf16[64,8,384]{2,1,0:T(8,128)(2,1)}), bf16[64,8,384]{2,1,0:T(8,128)(2,1)}, u32[]{:S(2)}, u32[]{:S(2)}) %all-to-all-start.4) | async-done | bytes 393248 | tf_op jit(solution)/shard_map/all_to_all | solution.py:507
  215.9 1.9 total.1
  217.8 6.9 %all-to-all-start.5 = ((bf16[64,8,384]{2,1,0:T(8,128)(2,1)}), bf16[64,8,384]{2,1,0:T(8,128)(2,1)}, u32[]{:S(2)}, u32[]{:S(2)}) async-start(bf16[64,8,384]{2,1,0:T(8,128)(2,1)} %total.1), calls=%async_computation.5 | async-start | bytes 786432 | tf_op jit(solution)/shard_map/all_to_all | solution.py:507
  224.8 1.3 convolution_add_fusion.1
  226.1 1.2 fusion.10
  227.3 1.1 fusion.2
  228.4 1.8 fusion.3
  230.3 1.7 reshape.17
  232.0 1.7 copy.15
  233.7 6.1 %all-to-all-done.5.pieces_ref = bf16[64,8,384]{2,1,0:T(8,128)(2,1)} async-done(((bf16[64,8,384]{2,1,0:T(8,128)(2,1)}), bf16[64,8,384]{2,1,0:T(8,128)(2,1)}, u32[]{:S(2)}, u32[]{:S(2)}) %all-to-all-start.5) | async-done | bytes 393248 | tf_op jit(solution)/shard_map/all_to_all | solution.py:507
  239.8 1.8 unfold.1
  (15 shorter events, 0.0 us)
Async XLA Ops:
  7.2 2.0 copy-start
  17.3 68.4 %all-to-all-start = ((bf16[64,144,128]{2,1,0:T(8,128)(2,1)}), bf16[64,144,128]{2,1,0:T(8,128)(2,1)}, u32[]{:S(2)}, u32[]{:S(2)}) async-start(bf16[64,144,128]{2,1,0:T(8,128)(2,1)} %get-tuple-element.21), calls=%async_computation | async-start | bytes 4718592 | tf_op jit(solution)/shard_map/all_to_all | solution.py:507
  85.7 37.9 %all-to-all-start.2 = ((bf16[64,72,128]{2,1,0:T(8,128)(2,1)}), bf16[64,72,128]{2,1,0:T(8,128)(2,1)}, u32[]{:S(2)}, u32[]{:S(2)}) async-start(bf16[64,72,128]{2,1,0:T(8,128)(2,1)} %pack_later.1), calls=%async_computation.2 | async-start | bytes 2359296 | tf_op jit(solution)/shard_map/all_to_all | solution.py:507
  123.6 38.4 %all-to-all-start.1 = ((bf16[64,72,128]{2,1,0:T(8,128)(2,1)}), bf16[64,72,128]{2,1,0:T(8,128)(2,1)}, u32[]{:S(2)}, u32[]{:S(2)}) async-start(bf16[64,72,128]{2,1,0:T(8,128)(2,1)} %get-tuple-element.25), calls=%async_computation.1 | async-start | bytes 2359296 | tf_op jit(solution)/shard_map/all_to_all | solution.py:507
  131.5 51.4 %all-gather.2.cloned.1.call-start = ((), (), s32[]{:S(2)}) async-start(), calls=%async_computation.6 | async-start | bytes 1474560 | tf_op jit(solution)/shard_map/all_gather | solution.py:527
  162.0 27.3 %all-to-all-start.3 = ((bf16[64,40,128]{2,1,0:T(8,128)(2,1)}), bf16[64,40,128]{2,1,0:T(8,128)(2,1)}, u32[]{:S(2)}, u32[]{:S(2)}) async-start(bf16[64,40,128]{2,1,0:T(8,128)(2,1)} %get-tuple-element.28), calls=%async_computation.3 | async-start | bytes 1310720 | tf_op jit(solution)/shard_map/all_to_all | solution.py:507
  178.6 29.2 %collective-permute-start = (bf16[140,128]{1,0:T(8,128)(2,1)}, bf16[140,128]{1,0:T(8,128)(2,1)S(1)}, u32[]{:S(2)}, u32[]{:S(2)}) collective-permute-start(bf16[140,128]{1,0:T(8,128)(2,1)} %get-tuple-element.41), channel_id=1, source_target_pairs={{0,1},{1,2},{2,3},{3,0},{4,5},{5,6},{6,7},{7,4},{8,9},{9,10},{10,1... | collective-permute-start | bytes 107528 | tf_op jit(solution)/shard_map/ppermute | solution.py:644
  179.8 9.4 %collective-permute-start.2 = (bf16[140,128]{1,0:T(8,128)(2,1)S(1)}, bf16[140,128]{1,0:T(8,128)(2,1)S(1)}, u32[]{:S(2)}, u32[]{:S(2)}) collective-permute-start(bf16[140,128]{1,0:T(8,128)(2,1)S(1)} %get-tuple-element.40), channel_id=1, source_target_pairs={{0,3},{1,0},{2,1},{3,2},{4,7},{5,4},{6,5},{7,6},{8,11},{9,8},{10,9... | collective-permute-start | bytes 107528 | tf_op jit(solution)/shard_map/ppermute | solution.py:644
  181.3 47.1 %collective-permute-start.1 = (bf16[140,128]{1,0:T(8,128)(2,1)}, bf16[140,128]{1,0:T(8,128)(2,1)}, u32[]{:S(2)}, u32[]{:S(2)}) collective-permute-start(bf16[140,128]{1,0:T(8,128)(2,1)} %get-tuple-element.39), channel_id=1, source_target_pairs={{0,2},{1,3},{2,0},{3,1},{4,6},{5,7},{6,4},{7,5},{8,10},{9,11},{10,... | collective-permute-start | bytes 107528 | tf_op jit(solution)/shard_map/ppermute | solution.py:644
  189.3 0.6 copy-start.4
  194.2 21.8 %all-to-all-start.4 = ((bf16[64,8,384]{2,1,0:T(8,128)(2,1)}), bf16[64,8,384]{2,1,0:T(8,128)(2,1)}, u32[]{:S(2)}, u32[]{:S(2)}) async-start(bf16[64,8,384]{2,1,0:T(8,128)(2,1)} %get-tuple-element.31), calls=%async_computation.4 | async-start | bytes 786432 | tf_op jit(solution)/shard_map/all_to_all | solution.py:507
  200.9 6.9 %copy-start.2 = (f32[140,768]{1,0:T(8,128)S(1)}, f32[140,768]{1,0:T(8,128)}, u32[]{:S(2)}) copy-start(f32[140,768]{1,0:T(8,128)} %fusion.8) | copy-start | bytes 1290244
  202.5 22.3 %collective-permute-start.3 = (bf16[140,128]{1,0:T(8,128)(2,1)}, bf16[140,128]{1,0:T(8,128)(2,1)}, u32[]{:S(2)}, u32[]{:S(2)}) collective-permute-start(bf16[140,128]{1,0:T(8,128)(2,1)} %get-tuple-element.44), channel_id=1, source_target_pairs={{0,1},{1,2},{2,3},{3,0},{4,5},{5,6},{6,7},{7,4},{8,9},{9,10},{10,1... | collective-permute-start | bytes 107528 | tf_op jit(solution)/shard_map/ppermute | solution.py:644
  202.9 23.2 %collective-permute-start.5 = (bf16[140,128]{1,0:T(8,128)(2,1)S(1)}, bf16[140,128]{1,0:T(8,128)(2,1)}, u32[]{:S(2)}, u32[]{:S(2)}) collective-permute-start(bf16[140,128]{1,0:T(8,128)(2,1)S(1)} %get-tuple-element.43), channel_id=1, source_target_pairs={{0,3},{1,0},{2,1},{3,2},{4,7},{5,4},{6,5},{7,6},{8,11},{9,8},{10,9... | collective-permute-start | bytes 107528 | tf_op jit(solution)/shard_map/ppermute | solution.py:644
  205.1 22.2 %collective-permute-start.4 = (bf16[140,128]{1,0:T(8,128)(2,1)S(1)}, bf16[140,128]{1,0:T(8,128)(2,1)}, u32[]{:S(2)}, u32[]{:S(2)}) collective-permute-start(bf16[140,128]{1,0:T(8,128)(2,1)S(1)} %get-tuple-element.42), channel_id=1, source_target_pairs={{0,2},{1,3},{2,0},{3,1},{4,6},{5,7},{6,4},{7,5},{8,10},{9,11},{10,... | collective-permute-start | bytes 107528 | tf_op jit(solution)/shard_map/ppermute | solution.py:644
  217.8 21.9 %all-to-all-start.5 = ((bf16[64,8,384]{2,1,0:T(8,128)(2,1)}), bf16[64,8,384]{2,1,0:T(8,128)(2,1)}, u32[]{:S(2)}, u32[]{:S(2)}) async-start(bf16[64,8,384]{2,1,0:T(8,128)(2,1)} %total.1), calls=%async_computation.5 | async-start | bytes 786432 | tf_op jit(solution)/shard_map/all_to_all | solution.py:507
  226.1 2.4 copy-start.1
  226.1 2.4 copy-start.3
Sparse Core Ops, SparseCore 0:
  134.1 26.8 all-gather.1

commit v4 on v3

--- a/solution.py
+++ b/solution.py
@@ -92,7 +92,7 @@
                     scr[pl.ds(tell, 1), :] = jnp.full((1, LANES), image, jnp.float32)
         return carry
 
-    lax.fori_loop(0, texts_here, one_text, 0)
+    lax.fori_loop(0, texts_here, one_text, 0, unroll=2)
 
 
 def pack_first_kernel(
@@ -313,7 +313,7 @@
 
             return carry
 
-        lax.fori_loop(0, senders, place, 0)
+        lax.fori_loop(0, senders, place, 0, unroll=4)
 
     for i in range(images):
         acc_scr[i] = own_ref[i, 0]
@@ -363,7 +363,7 @@
             back_ref[s] = jnp.concatenate(parts, axis=0).astype(jnp.bfloat16)
             return carry
 
-        lax.fori_loop(0, senders, give, 0)
+        lax.fori_loop(0, senders, give, 0, unroll=4)
 
 
 def sum_requests(heads, length, images_here, neg_ref, rank_ref, own_ref, back_ref, sum_scr, text_scr):
@@ -386,7 +386,7 @@
             text_scr[h, pl.ds(t * length, length), :] = totals[h]
         return carry
 
-    lax.fori_loop(0, texts_here, one, 0)
+    lax.fori_loop(0, texts_here, one, 0, unroll=2)
 
 
 def gather_two_kernel(
@@ -409,7 +409,22 @@
 
 
 def gather_last_kernel(
-    length, images_here, neg_ref, rank_ref, text_ref, own_ref, back_ref, head_ref, after_ref, dq_ref, weight_ref, sum_scr, text_scr
+    length,
+    images_here,
+    core_ref,
+    neg_ref,
+    rank_ref,
+    text_ref,
+    own_ref,
+    back_ref,
+    head_ref,
+    after_ref,
+    dq_ref,
+    keep_ref,
+    give_ref,
+    sum_scr,
+    text_scr,
+    cut_scr,
 ):
     sum_requests(1, length, images_here, neg_ref, rank_ref, own_ref, back_ref, sum_scr, text_scr)
     members, mine, _ = dq_ref.shape
@@ -419,12 +434,21 @@
     last = lax.dot_general(
         dq, text_ref[...], (((0,), (0,)), ((), ())), preferred_element_type=jnp.float32
     )
-    half = weight_ref.shape[2]
+    half = cut_scr.shape[3]
     before = head_ref.shape[0] // 8
-    for b in range(before + HEAD_SIZE // 8):
+    blocks = before + HEAD_SIZE // 8
+    for b in range(blocks):
         rows = head_ref[b * 8 : b * 8 + 8, :] if b < before else last[(b - before) * 8 : (b - before) * 8 + 8]
         for side in range(2):
-            weight_ref[2 * b + side] = rows[:, side * half : (side + 1) * half].astype(jnp.bfloat16)
+            cut_scr[2 * b // blocks, 2 * b % blocks + side] = rows[:, side * half : (side + 1) * half]
+    core = core_ref[0]
+    keep_ref[...] = cut_scr[core]
+    give_ref[...] = cut_scr[1 - core].astype(jnp.bfloat16)
+
+
+def pair_kernel(keep_ref, got_ref, dq_ref, out_ref, same_ref):
+    pieces = keep_ref.shape[0]
+    out_ref[:pieces] = (keep_ref[...] + got_ref[...].astype(jnp.float32)).astype(jnp.bfloat16)
 
 
 def total_kernel(parts_ref, out_ref):
@@ -436,13 +460,14 @@
         out_ref[d] = total
 
 
-def unfold_kernel(pieces_ref, out_ref):
-    half = pieces_ref.shape[2]
-    for b in range(out_ref.shape[0] // 8):
-        for side in range(2):
-            out_ref[b * 8 : b * 8 + 8, side * half : (side + 1) * half] = pieces_ref[
-                2 * b + side
-            ].astype(jnp.float32)
+def unfold_kernel(core_ref, mine_ref, other_ref, out_ref):
+    half = mine_ref.shape[2]
+    rows = out_ref.shape[0] // 2
+    for which, ref in ((core_ref[0], mine_ref), (1 - core_ref[0], other_ref)):
+        for b in range(rows // 8):
+            at = pl.ds(pl.multiple_of(which * rows + b * 8, 8), 8)
+            for side in range(2):
+                out_ref[at, side * half : (side + 1) * half] = ref[2 * b + side].astype(jnp.float32)
 
 
 def params():
@@ -503,8 +528,10 @@
     )(plan, wire, both, kkt, own_acc, *more)
 
 
-def exchange(x):
-    return lax.all_to_all(x, "dp", split_axis=0, concat_axis=0, tiled=True)
+def exchange(x, groups=None):
+    return lax.all_to_all(
+        x, "dp", split_axis=0, concat_axis=0, axis_index_groups=groups, tiled=True
+    )
 
 
 def per_device(texts, query_weight, patch_key_value, grad_out, negatives):
@@ -616,6 +643,10 @@
     home_later = exchange(back_later)
 
     half = depth // 2
+    cut = width // 8
+    core = lax.rem(lax.axis_index("dp"), 2).reshape(1).astype(i32)
+    chips = [list(range(c, owners, 2)) for c in range(2)]
+    partner = [(d, d ^ 1) for d in range(owners)]
     dq_first, weight_first = pl.pallas_call(
         functools.partial(gather_two_kernel, length, images_here),
         grid=(1,),
@@ -655,10 +686,11 @@
         return total
 
     rows_first = swap(dq_first)
-    dq_later, weight_local = pl.pallas_call(
+    dq_later, keep, give = pl.pallas_call(
         functools.partial(gather_last_kernel, length, images_here),
         grid=(1,),
         in_specs=[
+            SMEM,
             SMEM,
             SMEM,
             VMEM,
@@ -667,34 +699,53 @@
             VMEM,
             ANY,
         ],
-        out_specs=[VMEM, VMEM],
+        out_specs=[VMEM, VMEM, VMEM],
         out_shape=[
             jax.ShapeDtypeStruct((members, count // members, LANES), bf16),
-            jax.ShapeDtypeStruct((owners, 8, half), bf16),
-        ],
-        scratch_shapes=[pltpu.VMEM((1, count, LANES), f32)] * 2,
+            jax.ShapeDtypeStruct((cut, 8, half), f32),
+            jax.ShapeDtypeStruct((cut, 8, half), bf16),
+        ],
+        scratch_shapes=[pltpu.VMEM((1, count, LANES), f32)] * 2
+        + [pltpu.VMEM((2, cut, 8, half), f32)],
         compiler_params=params(),
         cost_estimate=cost(3),
         name="gather_last",
-    )(neg, rank, flat_text, own_dq, home_later, weight_first, rows_first[-1])
-
-    parts = exchange(weight_local)
+    )(core, neg, rank, flat_text, own_dq, home_later, weight_first, rows_first[-1])
+
+    got = lax.ppermute(give, "dp", partner)
+    summed, dq_later = pl.pallas_call(
+        pair_kernel,
+        in_specs=[VMEM, VMEM, ANY],
+        out_specs=[VMEM, ANY],
+        out_shape=[
+            jax.ShapeDtypeStruct((owners // 2, 8, half), bf16),
+            jax.ShapeDtypeStruct(dq_later.shape, bf16),
+        ],
+        input_output_aliases={2: 1},
+        compiler_params=params(),
+        cost_estimate=cost(2),
+        name="pair",
+    )(keep, got, dq_later)
+    parts = exchange(summed, chips)
     piece = pl.pallas_call(
         total_kernel,
         in_specs=[VMEM],
         out_specs=VMEM,
         out_shape=jax.ShapeDtypeStruct(parts.shape, bf16),
         compiler_params=params(),
+        cost_estimate=cost(2),
         name="total",
     )(parts)
+    pieces = exchange(piece, chips)[:cut]
     weight_grad = pl.pallas_call(
         unfold_kernel,
-        in_specs=[VMEM],
+        in_specs=[SMEM, VMEM, VMEM],
         out_specs=VMEM,
         out_shape=jax.ShapeDtypeStruct((width, depth), f32),
         compiler_params=params(),
+        cost_estimate=cost(2),
         name="unfold",
-    )(exchange(piece))
+    )(core, pieces, lax.ppermute(pieces, "dp", partner))
 
     rows_later = swap(dq_later)
     text_grad = text_part(rows_first, 0, early * HEAD_SIZE)

time: 250 us -> 257 us (1.028)
  waiting for transfers between devices: 86.8 us -> 75.1 us
  Pallas kernels: 60.5 us -> 72 us
  starting transfers between devices: 56.9 us -> 60.1 us
    pallas_call x2, Pallas kernels: 19.3 us -> 31.4 us  [far_call(): pl.pallas_call(functools.partial(far_kernel, keys, padded, length, many),...]
    all_to_all x6, waiting for transfers between devices: 86.1 us -> 74.4 us  [exchange(): lax.all_to_all(x, 'dp', split_axis=0, concat_axis=0, axis_index_groups=gr...]
    ppermute x0 -> x2, starting transfers between devices: none -> 3.63 us  [the longest x1 3.08 us: per_device(): lax.ppermute(pieces, 'dp', partner)]
    unnamed x14 -> x12, local copies, waits for them, and re-layouts: 11.9 us -> 12.5 us
  transfers between devices with their start and end apart: 13 -> 15, of which waited for: 6 -> 6; matrix products, arithmetic and copies ran while one was open for 10% -> 11% of each run, Pallas kernels for 21% -> 25%
where the time goes in v4:
time: 257 us; the launch traced here: 254 us
  waiting for transfers between devices  75.1 us (29%)
  Pallas kernels  72 us (28%)
  starting transfers between devices  60.1 us (23%)
  local copies, waits for them, and re-layouts  18.5 us (7%)
  between operations  14.3 us (6%)
  matrix products  14.1 us (5%)
    all_to_all x6, waiting for transfers between devices, exchange(): lax.all_to_all(x, 'dp', split_axis=0, concat_axis=0, axis_index_groups=gr...  74.4 us
    all_to_all x6, starting transfers between devices, exchange(): lax.all_to_all(x, 'dp', split_axis=0, concat_axis=0, axis_index_groups=gr...  48.1 us
    pallas_call x2, Pallas kernels, far_call(): pl.pallas_call(functools.partial(far_kernel, keys, padded, length, many),...  31.4 us
    pallas_call x1, Pallas kernels, per_device(): pl.pallas_call(functools.partial(own_kernel, keys, padded, texts_here), g...  15.8 us
    dot_general x8, matrix products, text_part(): part = jnp.dot(rows[r][:, :wide], weight, preferred_element_type=f32)  14.1 us
    unnamed x12, local copies, waits for them, and re-layouts  12.5 us
    ppermute x6, starting transfers between devices, swap(): lax.ppermute(block, 'mp', [(i, (i + r) % members) for i in range(members)])  8.36 us
    pallas_call x1, Pallas kernels, per_device(): pl.pallas_call(functools.partial(pack_first_kernel, early, images_here),...  6.2 us
  transfers between devices with their start and end apart: 15, of which 6 were waited for; matrix products, arithmetic and copies ran while one was open for 11% of the time, Pallas kernels for 25%

profile of v4, /device:TPU:1, one launch (start us, length us, event | category | flops | bytes accessed | tf_op | source)
XLA Modules:
  0.0 254.1 jit_solution(17915814687179248345)
XLA Ops:
  7.2 1.9 copy-done
  9.5 1.3 copy.18.grad_hbm.grad_ref
  10.8 6.2 %pack_first.1 = (bf16[64,144,128]{2,1,0:T(8,128)(2,1)}, f32[3,560,128]{2,1,0:T(8,128)}, s32[3,16]{1,0:T(4,128)}) custom-call(s32[1]{0:T(128)} %bitcast.1.odd_ref, s32[3,16]{1,0:T(4,128)} %bitcast.29, bf16[560,768]{1,0:T(8,128)(2,1)} %bitcast.26, bf16[192,768]{1,0:T(8,128)(2,1)} %weight_ref.1, bf16[16,4,35,256]{3,2,1,0:T(8,128)(2,1)} %copy.18.grad_hbm.grad_ref), custom_call_target="tpu_custom_call" | custom-call | flops 2875000064 | bytes 18000000 | tf_op jit(solution)/shard_map/pack_first/pallas_call | solution.py:559
  17.0 13.3 %all-to-all-start = ((bf16[64,144,128]{2,1,0:T(8,128)(2,1)}), bf16[64,144,128]{2,1,0:T(8,128)(2,1)}, u32[]{:S(2)}, u32[]{:S(2)}) async-start(bf16[64,144,128]{2,1,0:T(8,128)(2,1)} %get-tuple-element.24), calls=%async_computation | async-start | bytes 4718592 | tf_op jit(solution)/shard_map/all_to_all | solution.py:532
  30.4 3.0 %copy.15.kv_ref = bf16[4,3,577,128]{3,2,1,0:T(8,128)(2,1)} copy(bf16[4,3,577,128]{3,0,2,1:T(4,128)(2,1)} %param.7) | data formatting | bytes 3545088 | tf_op args[2]
  33.3 15.8 %own.1 = (f32[4,3,592,128]{3,2,1,0:T(8,128)}, f32[4,3,256,128]{3,2,1,0:T(8,128)}, bf16[4,3,1184,128]{3,2,1,0:T(8,128)(2,1)}, bf16[4,3,128,592]{3,2,1,0:T(8,128)(2,1)}) custom-call(s32[1]{0:T(128)} %bitcast.1.odd_ref, f32[3,560,128]{2,1,0:T(8,128)} %get-tuple-element.22.query_ref, bf16[16,4,35,256]{3,2,1,0:T(8,128)(2,1)} %copy.18.grad_hbm.grad_ref, ...), custom_call_target="tpu_custom_call" | custom-call | flops 7474999808 | bytes 46800000 | tf_op jit(solution)/shard_map/own/pallas_call | solution.py:582
  49.2 3.7 %pack_later.1 = bf16[64,72,128]{2,1,0:T(8,128)(2,1)} custom-call(s32[1]{0:T(128)} %bitcast.1.odd_ref, s32[3,16]{1,0:T(4,128)} %bitcast.30, s32[3,16]{1,0:T(4,128)} %get-tuple-element.21.rank_ref, f32[3,560,128]{2,1,0:T(8,128)} %get-tuple-element.22.query_ref, bf16[16,4,35,256]{3,2,1,0:T(8,128)(2,1)} %copy.18.grad_hbm.grad_ref, ...), custom_call_target="tpu_custom_call" | custom-call | flops 2300000000 | bytes 14400000 | tf_op jit(solution)/shard_map/pack_later/pallas_call | solution.py:609
  52.8 32.6 %all-to-all-done.wire_hbm.wire_ref = bf16[64,144,128]{2,1,0:T(8,128)(2,1)} async-done(((bf16[64,144,128]{2,1,0:T(8,128)(2,1)}), bf16[64,144,128]{2,1,0:T(8,128)(2,1)}, u32[]{:S(2)}, u32[]{:S(2)}) %all-to-all-start) | async-done | bytes 2359328 | tf_op jit(solution)/shard_map/all_to_all | solution.py:532
  85.5 7.3 %all-to-all-start.2 = ((bf16[64,72,128]{2,1,0:T(8,128)(2,1)}), bf16[64,72,128]{2,1,0:T(8,128)(2,1)}, u32[]{:S(2)}, u32[]{:S(2)}) async-start(bf16[64,72,128]{2,1,0:T(8,128)(2,1)} %pack_later.1), calls=%async_computation.2 | async-start | bytes 2359296 | tf_op jit(solution)/shard_map/all_to_all | solution.py:532
  92.8 1.9 plan.1.plan_ref
  94.7 19.7 %far0.1 = (bf16[4,3,577,128]{3,2,1,0:T(8,128)(2,1)}, bf16[64,72,128]{2,1,0:T(8,128)(2,1)}) custom-call(s32[72,128]{1,0:T(8,128)} %plan.1.plan_ref, bf16[64,144,128]{2,1,0:T(8,128)(2,1)} %all-to-all-done.wire_hbm.wire_ref, bf16[4,3,1184,128]{3,2,1,0:T(8,128)(2,1)} %get-tuple-element.25.both_ref, bf16[4,3,128,592]{3,2,1,0:T(8,128)(2,1)} %get-tuple-element.26.kkt_ref, ...), custom_call_target="tpu_custom_call" | custom-call | flops 12650000384 | bytes 79200000 | tf_op jit(solution)/shard_map/far0/pallas_call | solution.py:500
  114.3 9.0 %all-to-all-done.2.wire_ref = bf16[64,72,128]{2,1,0:T(8,128)(2,1)} async-done(((bf16[64,72,128]{2,1,0:T(8,128)(2,1)}), bf16[64,72,128]{2,1,0:T(8,128)(2,1)}, u32[]{:S(2)}, u32[]{:S(2)}) %all-to-all-start.2) | async-done | bytes 1179680 | tf_op jit(solution)/shard_map/all_to_all | solution.py:532
  123.3 8.9 %all-to-all-start.1 = ((bf16[64,72,128]{2,1,0:T(8,128)(2,1)}), bf16[64,72,128]{2,1,0:T(8,128)(2,1)}, u32[]{:S(2)}, u32[]{:S(2)}) async-start(bf16[64,72,128]{2,1,0:T(8,128)(2,1)} %get-tuple-element.28), calls=%async_computation.1 | async-start | bytes 2359296 | tf_op jit(solution)/shard_map/all_to_all | solution.py:532
  132.2 0.7 all-gather.2.cloned.1.call-update
  132.9 11.7 %far2.1 = (bf16[4,3,577,128]{3,2,1,0:T(8,128)(2,1)}, bf16[64,40,128]{2,1,0:T(8,128)(2,1)}) custom-call(s32[72,128]{1,0:T(8,128)} %plan.1.plan_ref, bf16[64,72,128]{2,1,0:T(8,128)(2,1)} %all-to-all-done.2.wire_ref, bf16[4,3,1184,128]{3,2,1,0:T(8,128)(2,1)} %get-tuple-element.25.both_ref, ...), custom_call_target="tpu_custom_call", output_to_operand_aliasing={{0}: (5, {})} | custom-call | flops 6899999744 | bytes 43200000 | tf_op jit(solution)/shard_map/far2/pallas_call | solution.py:500
  144.7 18.1 %all-to-all-done.1.back_ref = bf16[64,72,128]{2,1,0:T(8,128)(2,1)} async-done(((bf16[64,72,128]{2,1,0:T(8,128)(2,1)}), bf16[64,72,128]{2,1,0:T(8,128)(2,1)}, u32[]{:S(2)}, u32[]{:S(2)}) %all-to-all-start.1) | async-done | bytes 1179680 | tf_op jit(solution)/shard_map/all_to_all | solution.py:532
  162.7 7.0 %all-to-all-start.3 = ((bf16[64,40,128]{2,1,0:T(8,128)(2,1)}), bf16[64,40,128]{2,1,0:T(8,128)(2,1)}, u32[]{:S(2)}, u32[]{:S(2)}) async-start(bf16[64,40,128]{2,1,0:T(8,128)(2,1)} %get-tuple-element.31), calls=%async_computation.3 | async-start | bytes 1310720 | tf_op jit(solution)/shard_map/all_to_all | solution.py:532
  169.8 3.4 %copy.17 = bf16[4,3,577,128]{3,0,2,1:T(4,128)(2,1)} copy(bf16[4,3,577,128]{3,2,1,0:T(8,128)(2,1)} %get-tuple-element.44) | data formatting | bytes 3545088
  173.2 4.1 %gather_two.1 = (bf16[4,140,128]{2,1,0:T(8,128)(2,1)}, f32[128,768]{1,0:T(8,128)}) custom-call(s32[3,16]{1,0:T(4,128)} %bitcast.31, s32[3,16]{1,0:T(4,128)} %get-tuple-element.21.rank_ref, bf16[560,768]{1,0:T(8,128)(2,1)} %bitcast.27, f32[4,3,256,128]{3,2,1,0:T(8,128)} %get-tuple-element.23.own_ref, bf16[64,72,128]{2,1,0:T(8,128)(2,1)} %all-to-all-done.1.back_ref), custom_call_target="tpu_custom_call" | custom-call | flops 2300000000 | bytes 14400000 | tf_op jit(solution)/shard_map/gather_two/pallas_call | solution.py:650
  177.3 1.4 dynamic-slice_bitcast_fusion.5
  178.7 2.5 collective-permute-start.2
  181.2 1.7 collective-permute-start.1
  182.9 1.9 fusion.8
  184.9 5.2 %all-to-all-done.3.back_ref = bf16[64,40,128]{2,1,0:T(8,128)(2,1)} async-done(((bf16[64,40,128]{2,1,0:T(8,128)(2,1)}), bf16[64,40,128]{2,1,0:T(8,128)(2,1)}, u32[]{:S(2)}, u32[]{:S(2)}) %all-to-all-start.3) | async-done | bytes 655392 | tf_op jit(solution)/shard_map/all_to_all | solution.py:532
  190.6 3.8 %gather_last.1 = (bf16[4,140,128]{2,1,0:T(8,128)(2,1)}, f32[24,8,384]{2,1,0:T(8,128)}, bf16[24,8,384]{2,1,0:T(8,128)(2,1)}) custom-call(s32[1]{0:T(128)} %bitcast.8.core_ref, s32[3,16]{1,0:T(4,128)} %bitcast.32, s32[3,16]{1,0:T(4,128)} %get-tuple-element.21.rank_ref, bf16[560,768]{1,0:T(8,128)(2,1)} %bitcast.28, ...), custom_call_target="tpu_custom_call" | custom-call | flops 1724999936 | bytes 10800000 | tf_op jit(solution)/shard_map/gather_last/pallas_call | solution.py:689
  194.9 1.9 convolution_add_fusion.3
  196.8 1.9 fusion.4
  198.8 0.7 copy-done.3
  199.4 1.7 pair.1
  201.1 5.1 %all-to-all-start.4 = ((bf16[32,8,384]{2,1,0:T(8,128)(2,1)}), bf16[32,8,384]{2,1,0:T(8,128)(2,1)}, u32[]{:S(2)}, u32[]{:S(2)}) async-start(bf16[32,8,384]{2,1,0:T(8,128)(2,1)} %get-tuple-element.37), calls=%async_computation.4 | async-start | bytes 393216 | tf_op jit(solution)/shard_map/all_to_all | solution.py:532
  206.2 0.8 dynamic-slice_bitcast_fusion.1
  207.1 1.6 collective-permute-start.4
  208.7 1.1 collective-permute-start.6
  209.8 1.4 collective-permute-start.5
  211.3 1.1 fusion.14
  212.3 1.9 convolution_add_fusion.1
  214.2 2.8 %all-to-all-done.4.parts_ref = bf16[32,8,384]{2,1,0:T(8,128)(2,1)} async-done(((bf16[32,8,384]{2,1,0:T(8,128)(2,1)}), bf16[32,8,384]{2,1,0:T(8,128)(2,1)}, u32[]{:S(2)}, u32[]{:S(2)}) %all-to-all-start.4) | async-done | bytes 196640 | tf_op jit(solution)/shard_map/all_to_all | solution.py:532
  217.0 1.7 total.1
  218.7 6.5 %all-to-all-start.5 = ((bf16[32,8,384]{2,1,0:T(8,128)(2,1)}), bf16[32,8,384]{2,1,0:T(8,128)(2,1)}, u32[]{:S(2)}, u32[]{:S(2)}) async-start(bf16[32,8,384]{2,1,0:T(8,128)(2,1)} %total.1), calls=%async_computation.5 | async-start | bytes 393216 | tf_op jit(solution)/shard_map/all_to_all | solution.py:532
  225.1 1.1 fusion.10
  226.3 2.0 fusion.2
  228.3 6.7 %all-to-all-done.5 = bf16[32,8,384]{2,1,0:T(8,128)(2,1)} async-done(((bf16[32,8,384]{2,1,0:T(8,128)(2,1)}), bf16[32,8,384]{2,1,0:T(8,128)(2,1)}, u32[]{:S(2)}, u32[]{:S(2)}) %all-to-all-start.5) | async-done | bytes 196640 | tf_op jit(solution)/shard_map/all_to_all | solution.py:532
  235.0 1.6 slice.24.mine_ref
  236.6 3.1 %collective-permute-start.7 = (bf16[24,8,384]{2,1,0:T(8,128)(2,1)}, bf16[24,8,384]{2,1,0:T(8,128)(2,1)}, u32[]{:S(2)}, u32[]{:S(2)}) collective-permute-start(bf16[24,8,384]{2,1,0:T(8,128)(2,1)} %slice.24.mine_ref), channel_id=1, source_target_pairs={{0,4},{4,0},{8,12},{12,8},{16,20},{20,16},{24,28},{28,24},{32,36},... | collective-permute-start | bytes 442376 | tf_op jit(solution)/shard_map/ppermute | solution.py:748
  239.7 2.3 fusion.3
  242.0 1.7 reshape.21
  243.7 1.7 copy.16
  245.4 1.8 unfold.1
  (19 shorter events, 1.6 us)
Async XLA Ops:
  7.2 2.0 copy-start
  17.0 68.4 %all-to-all-start = ((bf16[64,144,128]{2,1,0:T(8,128)(2,1)}), bf16[64,144,128]{2,1,0:T(8,128)(2,1)}, u32[]{:S(2)}, u32[]{:S(2)}) async-start(bf16[64,144,128]{2,1,0:T(8,128)(2,1)} %get-tuple-element.24), calls=%async_computation | async-start | bytes 4718592 | tf_op jit(solution)/shard_map/all_to_all | solution.py:532
  85.5 37.9 %all-to-all-start.2 = ((bf16[64,72,128]{2,1,0:T(8,128)(2,1)}), bf16[64,72,128]{2,1,0:T(8,128)(2,1)}, u32[]{:S(2)}, u32[]{:S(2)}) async-start(bf16[64,72,128]{2,1,0:T(8,128)(2,1)} %pack_later.1), calls=%async_computation.2 | async-start | bytes 2359296 | tf_op jit(solution)/shard_map/all_to_all | solution.py:532
  123.3 39.4 %all-to-all-start.1 = ((bf16[64,72,128]{2,1,0:T(8,128)(2,1)}), bf16[64,72,128]{2,1,0:T(8,128)(2,1)}, u32[]{:S(2)}, u32[]{:S(2)}) async-start(bf16[64,72,128]{2,1,0:T(8,128)(2,1)} %get-tuple-element.28), calls=%async_computation.1 | async-start | bytes 2359296 | tf_op jit(solution)/shard_map/all_to_all | solution.py:532
  132.2 50.8 %all-gather.2.cloned.1.call-start = ((), (), s32[]{:S(2)}) async-start(), calls=%async_computation.6 | async-start | bytes 1474560 | tf_op jit(solution)/shard_map/all_gather | solution.py:554
  162.7 27.3 %all-to-all-start.3 = ((bf16[64,40,128]{2,1,0:T(8,128)(2,1)}), bf16[64,40,128]{2,1,0:T(8,128)(2,1)}, u32[]{:S(2)}, u32[]{:S(2)}) async-start(bf16[64,40,128]{2,1,0:T(8,128)(2,1)} %get-tuple-element.31), calls=%async_computation.3 | async-start | bytes 1310720 | tf_op jit(solution)/shard_map/all_to_all | solution.py:532
  178.7 11.3 %collective-permute-start.2 = (bf16[140,128]{1,0:T(8,128)(2,1)}, bf16[140,128]{1,0:T(8,128)(2,1)S(1)}, u32[]{:S(2)}, u32[]{:S(2)}) collective-permute-start(bf16[140,128]{1,0:T(8,128)(2,1)} %get-tuple-element.46), channel_id=1, source_target_pairs={{0,3},{1,0},{2,1},{3,2},{4,7},{5,4},{6,5},{7,6},{8,11},{9,8},{10,9... | collective-permute-start | bytes 107528 | tf_op jit(solution)/shard_map/ppermute | solution.py:675
  181.2 13.7 %collective-permute-start = (bf16[140,128]{1,0:T(8,128)(2,1)S(1)}, bf16[140,128]{1,0:T(8,128)(2,1)S(1)}, u32[]{:S(2)}, u32[]{:S(2)}) collective-permute-start(bf16[140,128]{1,0:T(8,128)(2,1)S(1)} %get-tuple-element.47), channel_id=1, source_target_pairs={{0,1},{1,2},{2,3},{3,0},{4,5},{5,6},{6,7},{7,4},{8,9},{9,10},{10,1... | collective-permute-start | bytes 107528 | tf_op jit(solution)/shard_map/ppermute | solution.py:675
  181.2 58.5 %collective-permute-start.1 = (bf16[140,128]{1,0:T(8,128)(2,1)}, bf16[140,128]{1,0:T(8,128)(2,1)}, u32[]{:S(2)}, u32[]{:S(2)}) collective-permute-start(bf16[140,128]{1,0:T(8,128)(2,1)} %get-tuple-element.45), channel_id=1, source_target_pairs={{0,2},{1,3},{2,0},{3,1},{4,6},{5,7},{6,4},{7,5},{8,10},{9,11},{10,... | collective-permute-start | bytes 107528 | tf_op jit(solution)/shard_map/ppermute | solution.py:675
  190.0 0.6 copy-start.2
  190.6 4.3 %copy-start.1 = (f32[140,768]{1,0:T(8,128)S(1)}, f32[140,768]{1,0:T(8,128)}, u32[]{:S(2)}) copy-start(f32[140,768]{1,0:T(8,128)} %fusion.8) | copy-start | bytes 1290244
  194.4 4.4 %collective-permute-start.3 = (bf16[24,8,384]{2,1,0:T(8,128)(2,1)}, bf16[24,8,384]{2,1,0:T(8,128)(2,1)S(1)}, u32[]{:S(2)}, u32[]{:S(2)}) collective-permute-start(bf16[24,8,384]{2,1,0:T(8,128)(2,1)} %get-tuple-element.34), channel_id=1, source_target_pairs={{0,4},{4,0},{8,12},{12,8},{16,20},{20,16},{24,28},{28,24},{32,36},... | collective-permute-start | bytes 442376 | tf_op jit(solution)/shard_map/ppermute | solution.py:715
  198.8 0.7 copy-start.3
  201.1 15.9 %all-to-all-start.4 = ((bf16[32,8,384]{2,1,0:T(8,128)(2,1)}), bf16[32,8,384]{2,1,0:T(8,128)(2,1)}, u32[]{:S(2)}, u32[]{:S(2)}) async-start(bf16[32,8,384]{2,1,0:T(8,128)(2,1)} %get-tuple-element.37), calls=%async_computation.4 | async-start | bytes 393216 | tf_op jit(solution)/shard_map/all_to_all | solution.py:532
  207.1 5.2 %collective-permute-start.4 = (bf16[140,128]{1,0:T(8,128)(2,1)S(1)}, bf16[140,128]{1,0:T(8,128)(2,1)S(1)}, u32[]{:S(2)}, u32[]{:S(2)}) collective-permute-start(bf16[140,128]{1,0:T(8,128)(2,1)S(1)} %get-tuple-element.50), channel_id=1, source_target_pairs={{0,1},{1,2},{2,3},{3,0},{4,5},{5,6},{6,7},{7,4},{8,9},{9,10},{10,1... | collective-permute-start | bytes 107528 | tf_op jit(solution)/shard_map/ppermute | solution.py:675
  208.7 16.4 %collective-permute-start.6 = (bf16[140,128]{1,0:T(8,128)(2,1)S(1)}, bf16[140,128]{1,0:T(8,128)(2,1)}, u32[]{:S(2)}, u32[]{:S(2)}) collective-permute-start(bf16[140,128]{1,0:T(8,128)(2,1)S(1)} %get-tuple-element.49), channel_id=1, source_target_pairs={{0,3},{1,0},{2,1},{3,2},{4,7},{5,4},{6,5},{7,6},{8,11},{9,8},{10,9... | collective-permute-start | bytes 107528 | tf_op jit(solution)/shard_map/ppermute | solution.py:675
  209.8 16.4 %collective-permute-start.5 = (bf16[140,128]{1,0:T(8,128)(2,1)S(1)}, bf16[140,128]{1,0:T(8,128)(2,1)S(1)}, u32[]{:S(2)}, u32[]{:S(2)}) collective-permute-start(bf16[140,128]{1,0:T(8,128)(2,1)S(1)} %get-tuple-element.48), channel_id=1, source_target_pairs={{0,2},{1,3},{2,0},{3,1},{4,6},{5,7},{6,4},{7,5},{8,10},{9,11},{10,... | collective-permute-start | bytes 107528 | tf_op jit(solution)/shard_map/ppermute | solution.py:675
  218.7 16.4 %all-to-all-start.5 = ((bf16[32,8,384]{2,1,0:T(8,128)(2,1)}), bf16[32,8,384]{2,1,0:T(8,128)(2,1)}, u32[]{:S(2)}, u32[]{:S(2)}) async-start(bf16[32,8,384]{2,1,0:T(8,128)(2,1)} %total.1), calls=%async_computation.5 | async-start | bytes 393216 | tf_op jit(solution)/shard_map/all_to_all | solution.py:532
  236.6 8.8 %collective-permute-start.7 = (bf16[24,8,384]{2,1,0:T(8,128)(2,1)}, bf16[24,8,384]{2,1,0:T(8,128)(2,1)}, u32[]{:S(2)}, u32[]{:S(2)}) collective-permute-start(bf16[24,8,384]{2,1,0:T(8,128)(2,1)} %slice.24.mine_ref), channel_id=1, source_target_pairs={{0,4},{4,0},{8,12},{12,8},{16,20},{20,16},{24,28},{28,24},{32,36},... | collective-permute-start | bytes 442376 | tf_op jit(solution)/shard_map/ppermute | solution.py:748
Sparse Core Ops, SparseCore 0:
  134.8 26.8 all-gather.1

commit v5 on v4

--- a/solution.py
+++ b/solution.py
@@ -13,6 +13,7 @@
 TILE = 256
 WAYS = 4
 PARTS = 4
+
 VMEM_LIMIT = 60 * 1024 * 1024
 
 
@@ -72,7 +73,10 @@
     texts_here, slots, length, _ = grad_ref.shape
     tells = wire_rows >= 2 * heads * length + 2
     if tells:
-        scr[...] = jnp.full(scr.shape, -1.0, jnp.float32)
+        for o in range(scr.shape[0] // wire_rows):
+            scr[(o + 1) * wire_rows - 8 : (o + 1) * wire_rows, :] = jnp.full(
+                (8, LANES), -1.0, jnp.float32
+            )
 
     def one_text(t, carry):
         for h in range(heads):
@@ -366,7 +370,7 @@
         lax.fori_loop(0, senders, give, 0, unroll=4)
 
 
-def sum_requests(heads, length, images_here, neg_ref, rank_ref, own_ref, back_ref, sum_scr, text_scr):
+def sum_requests(heads, length, images_here, neg_ref, rank_ref, own_ref, back_ref, sum_scr, text_scr, per):
     texts_here = sum_scr.shape[1] // length
     captions = texts_here // images_here
 
@@ -383,7 +387,8 @@
                 totals[h] = totals[h] + block[h * length : (h + 1) * length]
         for h in range(heads):
             sum_scr[h, pl.ds(t, length, stride=texts_here), :] = totals[h]
-            text_scr[h, pl.ds(t * length, length), :] = totals[h]
+            at = t // per * (per * length) + lax.rem(t, per)
+            text_scr[h, pl.ds(at, length, stride=per), :] = totals[h]
         return carry
 
     lax.fori_loop(0, texts_here, one, 0, unroll=2)
@@ -392,7 +397,10 @@
 def gather_two_kernel(
     length, images_here, neg_ref, rank_ref, text_ref, own_ref, back_ref, dq_ref, weight_ref, sum_scr, text_scr
 ):
-    sum_requests(2, length, images_here, neg_ref, rank_ref, own_ref, back_ref, sum_scr, text_scr)
+    per = dq_ref.shape[1] // length
+    sum_requests(
+        2, length, images_here, neg_ref, rank_ref, own_ref, back_ref, sum_scr, text_scr, per
+    )
     members, mine, _ = dq_ref.shape
 
     def paired(x0, x1):
@@ -426,7 +434,10 @@
     text_scr,
     cut_scr,
 ):
-    sum_requests(1, length, images_here, neg_ref, rank_ref, own_ref, back_ref, sum_scr, text_scr)
+    per = dq_ref.shape[1] // length
+    sum_requests(
+        1, length, images_here, neg_ref, rank_ref, own_ref, back_ref, sum_scr, text_scr, per
+    )
     members, mine, _ = dq_ref.shape
     for m in range(members):
         dq_ref[m] = text_scr[0, m * mine : (m + 1) * mine, :].astype(jnp.bfloat16)
@@ -446,7 +457,8 @@
     give_ref[...] = cut_scr[1 - core].astype(jnp.bfloat16)
 
 
-def pair_kernel(keep_ref, got_ref, dq_ref, out_ref, same_ref):
+def pair_kernel(keep_ref, got_ref, *rest):
+    out_ref = rest[len(rest) // 2]
     pieces = keep_ref.shape[0]
     out_ref[:pieces] = (keep_ref[...] + got_ref[...].astype(jnp.float32)).astype(jnp.bfloat16)
 
@@ -468,6 +480,24 @@
             at = pl.ds(pl.multiple_of(which * rows + b * 8, 8), 8)
             for side in range(2):
                 out_ref[at, side * half : (side + 1) * half] = ref[2 * b + side].astype(jnp.float32)
+
+
+def text_kernel(width, wides, member_ref, weight_ref, *refs):
+    rows, out_ref = refs[:-1], refs[-1]
+    members = len(rows) // len(wides)
+    total = jnp.zeros(out_ref.shape, jnp.float32)
+    for r in range(members):
+        source = lax.rem(member_ref[0] + members - r, members)
+        skip = 0
+        for group, wide in enumerate(wides):
+            at = pl.ds(pl.multiple_of(source * width + skip, HEAD_SIZE), wide)
+            total = total + jnp.dot(
+                rows[group * members + r][:, :wide],
+                weight_ref[at, :],
+                preferred_element_type=jnp.float32,
+            )
+            skip += wide
+    out_ref[...] = total.astype(jnp.bfloat16)
 
 
 def params():
@@ -676,15 +706,6 @@
             rows.append(block)
         return rows
 
-    def text_part(rows, skip, wide):
-        total = None
-        for r in range(members):
-            source = lax.rem(member + members - r, members)
-            weight = lax.dynamic_slice_in_dim(all_weight, source * width + skip, wide, 0)
-            part = jnp.dot(rows[r][:, :wide], weight, preferred_element_type=f32)
-            total = part if total is None else total + part
-        return total
-
     rows_first = swap(dq_first)
     dq_later, keep, give = pl.pallas_call(
         functools.partial(gather_last_kernel, length, images_here),
@@ -713,19 +734,18 @@
     )(core, neg, rank, flat_text, own_dq, home_later, weight_first, rows_first[-1])
 
     got = lax.ppermute(give, "dp", partner)
+    later = [dq_later]
     summed, dq_later = pl.pallas_call(
         pair_kernel,
-        in_specs=[VMEM, VMEM, ANY],
-        out_specs=[VMEM, ANY],
-        out_shape=[
-            jax.ShapeDtypeStruct((owners // 2, 8, half), bf16),
-            jax.ShapeDtypeStruct(dq_later.shape, bf16),
-        ],
-        input_output_aliases={2: 1},
+        in_specs=[VMEM, VMEM] + [ANY] * len(later),
+        out_specs=[VMEM] + [ANY] * len(later),
+        out_shape=[jax.ShapeDtypeStruct((owners // 2, 8, half), bf16)]
+        + [jax.ShapeDtypeStruct(x.shape, x.dtype) for x in later],
+        input_output_aliases={2 + n: 1 + n for n in range(len(later))},
         compiler_params=params(),
         cost_estimate=cost(2),
         name="pair",
-    )(keep, got, dq_later)
+    )(keep, got, *later)
     parts = exchange(summed, chips)
     piece = pl.pallas_call(
         total_kernel,
@@ -736,7 +756,30 @@
         cost_estimate=cost(2),
         name="total",
     )(parts)
-    pieces = exchange(piece, chips)[:cut]
+    rows_later = swap(dq_later)
+    mine = texts_here // members
+    text_grad = pl.pallas_call(
+        functools.partial(text_kernel, width, (early * HEAD_SIZE, (heads - early) * HEAD_SIZE)),
+        in_specs=[SMEM] + [VMEM] * (1 + 2 * members),
+        out_specs=VMEM,
+        out_shape=jax.ShapeDtypeStruct((length * mine, depth), bf16),
+        compiler_params=params(),
+        cost_estimate=cost(3),
+        name="text",
+    )(member.reshape(1).astype(i32), all_weight, *rows_first, *rows_later)
+    pieces, text_grad = pl.pallas_call(
+        lambda *refs: None,
+        in_specs=[ANY, ANY],
+        out_specs=[ANY, ANY],
+        out_shape=[
+            jax.ShapeDtypeStruct(piece.shape, bf16),
+            jax.ShapeDtypeStruct(text_grad.shape, bf16),
+        ],
+        input_output_aliases={0: 0, 1: 1},
+        cost_estimate=cost(1),
+        name="order",
+    )(exchange(piece, chips), text_grad)
+    text_grad = text_grad.reshape(length, mine, depth).transpose(1, 0, 2)
     weight_grad = pl.pallas_call(
         unfold_kernel,
         in_specs=[SMEM, VMEM, VMEM],
@@ -747,10 +790,6 @@
         name="unfold",
     )(core, pieces, lax.ppermute(pieces, "dp", partner))
 
-    rows_later = swap(dq_later)
-    text_grad = text_part(rows_first, 0, early * HEAD_SIZE)
-    text_grad = text_grad + text_part(rows_later, early * HEAD_SIZE, (heads - early) * HEAD_SIZE)
-    text_grad = text_grad.astype(bf16).reshape(texts_here // members, length, depth)
     return (text_grad, weight_grad, dkv)
 
 

time: 257 us -> 252 us (0.981)
  blocking collectives: 0 us -> 15.5 us
  matrix products: 14.1 us -> 0 us
  waiting for transfers between devices: 75.1 us -> 83.4 us
  starting transfers between devices: 60.1 us -> 54 us
  Pallas kernels: 72 us -> 67.8 us
  local copies, waits for them, and re-layouts: 18.5 us -> 15.2 us
    all_to_all x0 -> x1, blocking collectives: none -> 15.5 us  [exchange(): lax.all_to_all(x, 'dp', split_axis=0, concat_axis=0, axis_index_groups=gr...]
    dot_general x8 -> x0, matrix products: 14.1 us -> none  [text_part(): part = jnp.dot(rows[r][:, :wide], weight, preferred_element_type=f32)]
    all_to_all x6 -> x5, starting transfers between devices: 48.1 us -> 40.7 us  [exchange(): lax.all_to_all(x, 'dp', split_axis=0, concat_axis=0, axis_index_groups=gr...]
    pallas_call x2, Pallas kernels: 31.4 us -> 24.8 us  [far_call(): pl.pallas_call(functools.partial(far_kernel, keys, padded, length, many),...]
    all_to_all x6 -> x5, waiting for transfers between devices: 74.4 us -> 78.6 us  [exchange(): lax.all_to_all(x, 'dp', split_axis=0, concat_axis=0, axis_index_groups=gr...]
    ppermute x6, waiting for transfers between devices: 0.02 us -> 2.92 us  [swap(): lax.ppermute(block, 'mp', [(i, (i + r) % members) for i in range(members)])]
    pallas_call x1 -> x3, Pallas kernels: 1.7 us -> 4.36 us  [the longest x1 2.65 us: per_device(): pl.pallas_call(functools.partial(text_kernel, width, (early * HEAD_SIZE,...]
    unnamed x12 -> x7, local copies, waits for them, and re-layouts: 12.5 us -> 10.2 us
  transfers between devices with their start and end apart: 15 -> 14, of which waited for: 6 -> 8; matrix products, arithmetic and copies ran while one was open for 11% -> 4% of each run, Pallas kernels for 25% -> 24%
where the time goes in v5:
time: 252 us; the launch traced here: 250 us
  waiting for transfers between devices  83.4 us (33%)
  Pallas kernels  67.8 us (27%)
  starting transfers between devices  54 us (21%)
  blocking collectives  15.5 us (6%)
  local copies, waits for them, and re-layouts  15.2 us (6%)
  between operations  14.2 us (6%)
    all_to_all x5, waiting for transfers between devices, exchange(): lax.all_to_all(x, 'dp', split_axis=0, concat_axis=0, axis_index_groups=gr...  78.6 us
    all_to_all x5, starting transfers between devices, exchange(): lax.all_to_all(x, 'dp', split_axis=0, concat_axis=0, axis_index_groups=gr...  40.7 us
    pallas_call x2, Pallas kernels, far_call(): pl.pallas_call(functools.partial(far_kernel, keys, padded, length, many),...  24.8 us
    pallas_call x1, Pallas kernels, per_device(): pl.pallas_call(functools.partial(own_kernel, keys, padded, texts_here), g...  15.8 us
    all_to_all x1, blocking collectives, exchange(): lax.all_to_all(x, 'dp', split_axis=0, concat_axis=0, axis_index_groups=gr...  15.5 us
    unnamed x7, local copies, waits for them, and re-layouts  10.2 us
    ppermute x6, starting transfers between devices, swap(): lax.ppermute(block, 'mp', [(i, (i + r) % members) for i in range(members)])  8.93 us
    pallas_call x1, Pallas kernels, per_device(): pl.pallas_call(functools.partial(pack_first_kernel, early, images_here),...  5.94 us
  transfers between devices with their start and end apart: 14, of which 8 were waited for; matrix products, arithmetic and copies ran while one was open for 4% of the time, Pallas kernels for 24%

profile of v5, /device:TPU:1, one launch (start us, length us, event | category | flops | bytes accessed | tf_op | source)
XLA Modules:
  0.0 250.2 jit_solution(1375578636296611829)
XLA Ops:
  7.2 0.0 copy-start
  7.2 1.9 copy-done
  9.1 0.4 constant_dynamic-slice_fusion
  9.5 1.3 copy.15.grad_hbm.grad_ref
  10.8 5.9 %pack_first.1 = (bf16[64,144,128]{2,1,0:T(8,128)(2,1)}, f32[3,560,128]{2,1,0:T(8,128)}, s32[3,16]{1,0:T(4,128)}) custom-call(s32[1]{0:T(128)} %bitcast.2.odd_ref, s32[3,16]{1,0:T(4,128)} %bitcast.28, bf16[560,768]{1,0:T(8,128)(2,1)} %bitcast.25, bf16[192,768]{1,0:T(8,128)(2,1)} %weight_ref.1, bf16[16,4,35,256]{3,2,1,0:T(8,128)(2,1)} %copy.15.grad_hbm.grad_ref), custom_call_target="tpu_custom_call" | custom-call | flops 2875000064 | bytes 18000000 | tf_op jit(solution)/shard_map/pack_first/pallas_call | solution.py:589
  16.8 13.3 %all-to-all-start = ((bf16[64,144,128]{2,1,0:T(8,128)(2,1)}), bf16[64,144,128]{2,1,0:T(8,128)(2,1)}, u32[]{:S(2)}, u32[]{:S(2)}) async-start(bf16[64,144,128]{2,1,0:T(8,128)(2,1)} %get-tuple-element.26), calls=%async_computation | async-start | bytes 4718592 | tf_op jit(solution)/shard_map/all_to_all | solution.py:562
  30.1 3.0 %copy.13.kv_ref = bf16[4,3,577,128]{3,2,1,0:T(8,128)(2,1)} copy(bf16[4,3,577,128]{3,0,2,1:T(4,128)(2,1)} %param.7) | data formatting | bytes 3545088 | tf_op args[2]
  33.1 15.8 %own.1 = (f32[4,3,592,128]{3,2,1,0:T(8,128)}, f32[4,3,256,128]{3,2,1,0:T(8,128)}, bf16[4,3,1184,128]{3,2,1,0:T(8,128)(2,1)}, bf16[4,3,128,592]{3,2,1,0:T(8,128)(2,1)}) custom-call(s32[1]{0:T(128)} %bitcast.2.odd_ref, f32[3,560,128]{2,1,0:T(8,128)} %get-tuple-element.24.query_ref, bf16[16,4,35,256]{3,2,1,0:T(8,128)(2,1)} %copy.15.grad_hbm.grad_ref, ...), custom_call_target="tpu_custom_call" | custom-call | flops 7474999808 | bytes 46800000 | tf_op jit(solution)/shard_map/own/pallas_call | solution.py:612
  48.9 3.5 %pack_later.1 = bf16[64,72,128]{2,1,0:T(8,128)(2,1)} custom-call(s32[1]{0:T(128)} %bitcast.2.odd_ref, s32[3,16]{1,0:T(4,128)} %bitcast.29, s32[3,16]{1,0:T(4,128)} %get-tuple-element.23.rank_ref, f32[3,560,128]{2,1,0:T(8,128)} %get-tuple-element.24.query_ref, bf16[16,4,35,256]{3,2,1,0:T(8,128)(2,1)} %copy.15.grad_hbm.grad_ref, ...), custom_call_target="tpu_custom_call" | custom-call | flops 2300000000 | bytes 14400000 | tf_op jit(solution)/shard_map/pack_later/pallas_call | solution.py:639
  52.5 32.7 %all-to-all-done.wire_hbm.wire_ref = bf16[64,144,128]{2,1,0:T(8,128)(2,1)} async-done(((bf16[64,144,128]{2,1,0:T(8,128)(2,1)}), bf16[64,144,128]{2,1,0:T(8,128)(2,1)}, u32[]{:S(2)}, u32[]{:S(2)}) %all-to-all-start) | async-done | bytes 2359328 | tf_op jit(solution)/shard_map/all_to_all | solution.py:562
  85.2 7.3 %all-to-all-start.1 = ((bf16[64,72,128]{2,1,0:T(8,128)(2,1)}), bf16[64,72,128]{2,1,0:T(8,128)(2,1)}, u32[]{:S(2)}, u32[]{:S(2)}) async-start(bf16[64,72,128]{2,1,0:T(8,128)(2,1)} %pack_later.1), calls=%async_computation.1 | async-start | bytes 2359296 | tf_op jit(solution)/shard_map/all_to_all | solution.py:562
  92.6 1.9 plan.1.plan_ref
  94.4 15.2 %far0.1 = (bf16[4,3,577,128]{3,2,1,0:T(8,128)(2,1)}, bf16[64,72,128]{2,1,0:T(8,128)(2,1)}) custom-call(s32[72,128]{1,0:T(8,128)} %plan.1.plan_ref, bf16[64,144,128]{2,1,0:T(8,128)(2,1)} %all-to-all-done.wire_hbm.wire_ref, bf16[4,3,1184,128]{3,2,1,0:T(8,128)(2,1)} %get-tuple-element.28.both_ref, bf16[4,3,128,592]{3,2,1,0:T(8,128)(2,1)} %get-tuple-element.29.kkt_ref, ...), custom_call_target="tpu_custom_call" | custom-call | flops 12650000384 | bytes 79200000 | tf_op jit(solution)/shard_map/far0/pallas_call | solution.py:530
  109.6 13.5 %all-to-all-done.1.wire_ref = bf16[64,72,128]{2,1,0:T(8,128)(2,1)} async-done(((bf16[64,72,128]{2,1,0:T(8,128)(2,1)}), bf16[64,72,128]{2,1,0:T(8,128)(2,1)}, u32[]{:S(2)}, u32[]{:S(2)}) %all-to-all-start.1) | async-done | bytes 1179680 | tf_op jit(solution)/shard_map/all_to_all | solution.py:562
  123.1 8.7 %all-to-all-start.3 = ((bf16[64,72,128]{2,1,0:T(8,128)(2,1)}), bf16[64,72,128]{2,1,0:T(8,128)(2,1)}, u32[]{:S(2)}, u32[]{:S(2)}) async-start(bf16[64,72,128]{2,1,0:T(8,128)(2,1)} %get-tuple-element.32), calls=%async_computation.3 | async-start | bytes 2359296 | tf_op jit(solution)/shard_map/all_to_all | solution.py:562
  131.8 9.6 %far2.1 = (bf16[4,3,577,128]{3,2,1,0:T(8,128)(2,1)}, bf16[64,40,128]{2,1,0:T(8,128)(2,1)}) custom-call(s32[72,128]{1,0:T(8,128)} %plan.1.plan_ref, bf16[64,72,128]{2,1,0:T(8,128)(2,1)} %all-to-all-done.1.wire_ref, bf16[4,3,1184,128]{3,2,1,0:T(8,128)(2,1)} %get-tuple-element.28.both_ref, ...), custom_call_target="tpu_custom_call", output_to_operand_aliasing={{0}: (5, {})} | custom-call | flops 6899999744 | bytes 43200000 | tf_op jit(solution)/shard_map/far2/pallas_call | solution.py:530
  141.4 20.9 %all-to-all-done.3.back_ref = bf16[64,72,128]{2,1,0:T(8,128)(2,1)} async-done(((bf16[64,72,128]{2,1,0:T(8,128)(2,1)}), bf16[64,72,128]{2,1,0:T(8,128)(2,1)}, u32[]{:S(2)}, u32[]{:S(2)}) %all-to-all-start.3) | async-done | bytes 1179680 | tf_op jit(solution)/shard_map/all_to_all | solution.py:562
  162.3 6.8 %all-to-all-start.2 = ((bf16[64,40,128]{2,1,0:T(8,128)(2,1)}), bf16[64,40,128]{2,1,0:T(8,128)(2,1)}, u32[]{:S(2)}, u32[]{:S(2)}) async-start(bf16[64,40,128]{2,1,0:T(8,128)(2,1)} %get-tuple-element.31), calls=%async_computation.2 | async-start | bytes 1310720 | tf_op jit(solution)/shard_map/all_to_all | solution.py:562
  169.1 0.0 all-gather.2.cloned.1.call-start
  169.2 0.7 all-gather.2.cloned.1.call-update
  169.9 4.2 %gather_two.1 = (bf16[4,140,128]{2,1,0:T(8,128)(2,1)}, f32[128,768]{1,0:T(8,128)}) custom-call(s32[3,16]{1,0:T(4,128)} %bitcast.30, s32[3,16]{1,0:T(4,128)} %get-tuple-element.23.rank_ref, bf16[560,768]{1,0:T(8,128)(2,1)} %bitcast.26, f32[4,3,256,128]{3,2,1,0:T(8,128)} %get-tuple-element.25.own_ref, bf16[64,72,128]{2,1,0:T(8,128)(2,1)} %all-to-all-done.3.back_ref), custom_call_target="tpu_custom_call" | custom-call | flops 2300000000 | bytes 14400000 | tf_op jit(solution)/shard_map/gather_two/pallas_call | solution.py:680
  174.1 1.4 dynamic-slice_bitcast_fusion.4
  175.5 2.5 collective-permute-start
  178.0 11.4 %all-to-all-done.2.back_ref = bf16[64,40,128]{2,1,0:T(8,128)(2,1)} async-done(((bf16[64,40,128]{2,1,0:T(8,128)(2,1)}), bf16[64,40,128]{2,1,0:T(8,128)(2,1)}, u32[]{:S(2)}, u32[]{:S(2)}) %all-to-all-start.2) | async-done | bytes 655392 | tf_op jit(solution)/shard_map/all_to_all | solution.py:562
  189.4 0.0 collective-permute-done.after_ref.refs_3_
  189.4 3.7 %gather_last.1 = (bf16[4,140,128]{2,1,0:T(8,128)(2,1)}, f32[24,8,384]{2,1,0:T(8,128)}, bf16[24,8,384]{2,1,0:T(8,128)(2,1)}) custom-call(s32[1]{0:T(128)} %bitcast.core_ref, s32[3,16]{1,0:T(4,128)} %bitcast.31, s32[3,16]{1,0:T(4,128)} %get-tuple-element.23.rank_ref, bf16[560,768]{1,0:T(8,128)(2,1)} %bitcast.27, f32[4,3,256,128]{3,2,1,0:T(8,128)} %get-tuple-element.25.own_ref, ...), custom_call_target="tpu_custom_call" | custom-call | flops 1724999936 | bytes 10800000 | tf_op jit(solution)/shard_map/gather_last/pallas_call | solution.py:710
  193.1 0.5 collective-permute-start.1
  193.7 1.2 collective-permute-done.1.got_ref
  194.9 0.7 copy-done.1
  195.5 1.7 pair.1
  197.2 15.5 %all_to_all.30.parts_ref = bf16[32,8,384]{2,1,0:T(8,128)(2,1)} all-to-all(bf16[32,8,384]{2,1,0:T(8,128)(2,1)} %get-tuple-element.38), channel_id=1, replica_groups={{0,8,16,24,32,40,48,56,64,72,80,88,96,104,112,120,128,136,144,152,160,1..., dimensions={0} | all-to-all | bytes 393216 | tf_op jit(solution)/shard_map/all_to_all | solution.py:562
  212.8 1.7 total.1
  214.4 4.6 %all-to-all-start.5 = ((bf16[32,8,384]{2,1,0:T(8,128)(2,1)}), bf16[32,8,384]{2,1,0:T(8,128)(2,1)}, u32[]{:S(2)}, u32[]{:S(2)}) async-start(bf16[32,8,384]{2,1,0:T(8,128)(2,1)} %total.1), calls=%async_computation.5 | async-start | bytes 393216 | tf_op jit(solution)/shard_map/all_to_all | solution.py:562
  219.0 1.3 collective-permute-start.2
  220.3 2.5 collective-permute-start.3
  222.8 1.5 dynamic-slice_bitcast_fusion
  224.3 2.3 collective-permute-start.5
  226.6 0.4 collective-permute-start.6
  226.9 0.0 collective-permute-done.2.refs_1_
  226.9 0.0 collective-permute-done.3.refs_2_
  227.0 1.9 collective-permute-done.4.refs_5_
  228.9 0.3 collective-permute-done.5.refs_6_
  229.2 0.7 collective-permute-done.6.refs_7_
  229.9 2.7 %text.1.refs_1_ = bf16[140,768]{1,0:T(8,128)(2,1)} custom-call(s32[1]{0:T(128)} %bitcast.7.member_ref, bf16[768,768]{1,0:T(8,128)(2,1)} %all-gather.2.cloned.1.call-done.weight_ref, bf16[140,128]{1,0:T(8,128)(2,1)} %get-tuple-element.52.refs_0_, bf16[140,128]{1,0:T(8,128)(2,1)} %collective-permute-done.2.refs_1_, ...), custom_call_target="tpu_custom_call" | custom-call | flops 1724999936 | bytes 10800000 | tf_op jit(solution)/shard_map/text/pallas_call | solution.py:761
  232.5 3.8 %collective-permute-start.7 = (bf16[32,8,384]{2,1,0:T(8,128)(2,1)}, bf16[32,8,384]{2,1,0:T(8,128)(2,1)}, u32[]{:S(2)}, u32[]{:S(2)}) collective-permute-start(bf16[32,8,384]{2,1,0:T(8,128)(2,1)} %get-tuple-element.41.mine_ref), channel_id=1, source_target_pairs={{0,4},{4,0},{8,12},{12,8},{16,20},{20,16},{24,28},{28,24},{32,36},... | collective-permute-start | bytes 589832 | tf_op jit(solution)/shard_map/ppermute | solution.py:791
  236.4 3.4 %copy.14 = bf16[4,3,577,128]{3,0,2,1:T(4,128)(2,1)} copy(bf16[4,3,577,128]{3,2,1,0:T(8,128)(2,1)} %get-tuple-element.45) | data formatting | bytes 3545088
  239.7 1.7 reshape.25
  241.4 1.9 unfold.1
  (6 shorter events, 0.0 us)
Async XLA Ops:
  7.2 2.0 copy-start
  16.8 68.4 %all-to-all-start = ((bf16[64,144,128]{2,1,0:T(8,128)(2,1)}), bf16[64,144,128]{2,1,0:T(8,128)(2,1)}, u32[]{:S(2)}, u32[]{:S(2)}) async-start(bf16[64,144,128]{2,1,0:T(8,128)(2,1)} %get-tuple-element.26), calls=%async_computation | async-start | bytes 4718592 | tf_op jit(solution)/shard_map/all_to_all | solution.py:562
  85.2 37.9 %all-to-all-start.1 = ((bf16[64,72,128]{2,1,0:T(8,128)(2,1)}), bf16[64,72,128]{2,1,0:T(8,128)(2,1)}, u32[]{:S(2)}, u32[]{:S(2)}) async-start(bf16[64,72,128]{2,1,0:T(8,128)(2,1)} %pack_later.1), calls=%async_computation.1 | async-start | bytes 2359296 | tf_op jit(solution)/shard_map/all_to_all | solution.py:562
  123.1 39.2 %all-to-all-start.3 = ((bf16[64,72,128]{2,1,0:T(8,128)(2,1)}), bf16[64,72,128]{2,1,0:T(8,128)(2,1)}, u32[]{:S(2)}, u32[]{:S(2)}) async-start(bf16[64,72,128]{2,1,0:T(8,128)(2,1)} %get-tuple-element.32), calls=%async_computation.3 | async-start | bytes 2359296 | tf_op jit(solution)/shard_map/all_to_all | solution.py:562
  162.3 27.1 %all-to-all-start.2 = ((bf16[64,40,128]{2,1,0:T(8,128)(2,1)}), bf16[64,40,128]{2,1,0:T(8,128)(2,1)}, u32[]{:S(2)}, u32[]{:S(2)}) async-start(bf16[64,40,128]{2,1,0:T(8,128)(2,1)} %get-tuple-element.31), calls=%async_computation.2 | async-start | bytes 1310720 | tf_op jit(solution)/shard_map/all_to_all | solution.py:562
  169.1 57.8 %all-gather.2.cloned.1.call-start = ((), (), s32[]{:S(2)}) async-start(), calls=%async_computation.6 | async-start | bytes 1474560 | tf_op jit(solution)/shard_map/all_gather | solution.py:584
  175.5 13.9 %collective-permute-start = (bf16[140,128]{1,0:T(8,128)(2,1)S(1)}, bf16[140,128]{1,0:T(8,128)(2,1)}, u32[]{:S(2)}, u32[]{:S(2)}) collective-permute-start(bf16[140,128]{1,0:T(8,128)(2,1)S(1)} %get-tuple-element.53), channel_id=1, source_target_pairs={{0,3},{1,0},{2,1},{3,2},{4,7},{5,4},{6,5},{7,6},{8,11},{9,8},{10,9... | collective-permute-start | bytes 107528 | tf_op jit(solution)/shard_map/ppermute | solution.py:705
  193.1 1.7 collective-permute-start.1
  194.9 0.7 copy-start.1
  214.4 18.1 %all-to-all-start.5 = ((bf16[32,8,384]{2,1,0:T(8,128)(2,1)}), bf16[32,8,384]{2,1,0:T(8,128)(2,1)}, u32[]{:S(2)}, u32[]{:S(2)}) async-start(bf16[32,8,384]{2,1,0:T(8,128)(2,1)} %total.1), calls=%async_computation.5 | async-start | bytes 393216 | tf_op jit(solution)/shard_map/all_to_all | solution.py:562
  219.0 7.9 %collective-permute-start.2 = (bf16[140,128]{1,0:T(8,128)(2,1)S(1)}, bf16[140,128]{1,0:T(8,128)(2,1)}, u32[]{:S(2)}, u32[]{:S(2)}) collective-permute-start(bf16[140,128]{1,0:T(8,128)(2,1)S(1)} %get-tuple-element.51), channel_id=1, source_target_pairs={{0,1},{1,2},{2,3},{3,0},{4,5},{5,6},{6,7},{7,4},{8,9},{9,10},{10,1... | collective-permute-start | bytes 107528 | tf_op jit(solution)/shard_map/ppermute | solution.py:705
  220.3 6.6 %collective-permute-start.3 = (bf16[140,128]{1,0:T(8,128)(2,1)S(1)}, bf16[140,128]{1,0:T(8,128)(2,1)}, u32[]{:S(2)}, u32[]{:S(2)}) collective-permute-start(bf16[140,128]{1,0:T(8,128)(2,1)S(1)} %get-tuple-element.50), channel_id=1, source_target_pairs={{0,2},{1,3},{2,0},{3,1},{4,6},{5,7},{6,4},{7,5},{8,10},{9,11},{10,... | collective-permute-start | bytes 107528 | tf_op jit(solution)/shard_map/ppermute | solution.py:705
  224.3 4.6 %collective-permute-start.4 = (bf16[140,128]{1,0:T(8,128)(2,1)}, bf16[140,128]{1,0:T(8,128)(2,1)}, u32[]{:S(2)}, u32[]{:S(2)}) collective-permute-start(bf16[140,128]{1,0:T(8,128)(2,1)} %get-tuple-element.48), channel_id=1, source_target_pairs={{0,1},{1,2},{2,3},{3,0},{4,5},{5,6},{6,7},{7,4},{8,9},{9,10},{10,1... | collective-permute-start | bytes 107528 | tf_op jit(solution)/shard_map/ppermute | solution.py:705
  224.3 4.9 %collective-permute-start.5 = (bf16[140,128]{1,0:T(8,128)(2,1)}, bf16[140,128]{1,0:T(8,128)(2,1)}, u32[]{:S(2)}, u32[]{:S(2)}) collective-permute-start(bf16[140,128]{1,0:T(8,128)(2,1)} %get-tuple-element.47), channel_id=1, source_target_pairs={{0,2},{1,3},{2,0},{3,1},{4,6},{5,7},{6,4},{7,5},{8,10},{9,11},{10,... | collective-permute-start | bytes 107528 | tf_op jit(solution)/shard_map/ppermute | solution.py:705
  226.6 3.3 %collective-permute-start.6 = (bf16[140,128]{1,0:T(8,128)(2,1)S(1)}, bf16[140,128]{1,0:T(8,128)(2,1)}, u32[]{:S(2)}, u32[]{:S(2)}) collective-permute-start(bf16[140,128]{1,0:T(8,128)(2,1)S(1)} %get-tuple-element.46), channel_id=1, source_target_pairs={{0,3},{1,0},{2,1},{3,2},{4,7},{5,4},{6,5},{7,6},{8,11},{9,8},{10,9... | collective-permute-start | bytes 107528 | tf_op jit(solution)/shard_map/ppermute | solution.py:705
  232.5 8.9 %collective-permute-start.7 = (bf16[32,8,384]{2,1,0:T(8,128)(2,1)}, bf16[32,8,384]{2,1,0:T(8,128)(2,1)}, u32[]{:S(2)}, u32[]{:S(2)}) collective-permute-start(bf16[32,8,384]{2,1,0:T(8,128)(2,1)} %get-tuple-element.41.mine_ref), channel_id=1, source_target_pairs={{0,4},{4,0},{8,12},{12,8},{16,20},{20,16},{24,28},{28,24},{32,36},... | collective-permute-start | bytes 589832 | tf_op jit(solution)/shard_map/ppermute | solution.py:791
Sparse Core Ops, SparseCore 0:
  171.7 26.8 all-gather.1

commit v6 on v5

--- a/solution.py
+++ b/solution.py
@@ -426,14 +426,9 @@
     own_ref,
     back_ref,
     head_ref,
-    after_ref,
-    dq_ref,
-    keep_ref,
-    give_ref,
-    sum_scr,
-    text_scr,
-    cut_scr,
+    *rest,
 ):
+    dq_ref, keep_ref, give_ref, _, sum_scr, text_scr, cut_scr = rest[-7:]
     per = dq_ref.shape[1] // length
     sum_requests(
         1, length, images_here, neg_ref, rank_ref, own_ref, back_ref, sum_scr, text_scr, per
@@ -463,7 +458,8 @@
     out_ref[:pieces] = (keep_ref[...] + got_ref[...].astype(jnp.float32)).astype(jnp.bfloat16)
 
 
-def total_kernel(parts_ref, out_ref):
+def total_kernel(parts_ref, *rest):
+    out_ref = rest[-1]
     total = parts_ref[0].astype(jnp.float32)
     for d in range(1, parts_ref.shape[0]):
         total = total + parts_ref[d].astype(jnp.float32)
@@ -707,7 +703,8 @@
         return rows
 
     rows_first = swap(dq_first)
-    dq_later, keep, give = pl.pallas_call(
+    dkv = dkv.transpose(1, 2, 0, 3)
+    dq_later, keep, give, dkv = pl.pallas_call(
         functools.partial(gather_last_kernel, length, images_here),
         grid=(1,),
         in_specs=[
@@ -718,20 +715,23 @@
             pl.BlockSpec((images_here, 1, TILE, LANES), lambda n: (0, early, 0, 0)),
             VMEM,
             VMEM,
-            ANY,
-        ],
-        out_specs=[VMEM, VMEM, VMEM],
+        ]
+        + [ANY] * members,
+        out_specs=[VMEM, VMEM, VMEM, ANY],
         out_shape=[
             jax.ShapeDtypeStruct((members, count // members, LANES), bf16),
             jax.ShapeDtypeStruct((cut, 8, half), f32),
             jax.ShapeDtypeStruct((cut, 8, half), bf16),
-        ],
+            jax.ShapeDtypeStruct(dkv.shape, bf16),
+        ],
+        input_output_aliases={6 + members: 3},
         scratch_shapes=[pltpu.VMEM((1, count, LANES), f32)] * 2
         + [pltpu.VMEM((2, cut, 8, half), f32)],
         compiler_params=params(),
         cost_estimate=cost(3),
         name="gather_last",
-    )(core, neg, rank, flat_text, own_dq, home_later, weight_first, rows_first[-1])
+    )(core, neg, rank, flat_text, own_dq, home_later, weight_first, *rows_first[1:], dkv)
+    dkv = dkv.transpose(2, 0, 1, 3)
 
     got = lax.ppermute(give, "dp", partner)
     later = [dq_later]
@@ -747,16 +747,16 @@
         name="pair",
     )(keep, got, *later)
     parts = exchange(summed, chips)
+    rows_later = swap(dq_later)
     piece = pl.pallas_call(
         total_kernel,
-        in_specs=[VMEM],
+        in_specs=[VMEM] + [ANY] * (members - 1),
         out_specs=VMEM,
         out_shape=jax.ShapeDtypeStruct(parts.shape, bf16),
         compiler_params=params(),
         cost_estimate=cost(2),
         name="total",
-    )(parts)
-    rows_later = swap(dq_later)
+    )(parts, *rows_later[1:])
     mine = texts_here // members
     text_grad = pl.pallas_call(
         functools.partial(text_kernel, width, (early * HEAD_SIZE, (heads - early) * HEAD_SIZE)),
@@ -767,6 +767,7 @@
         cost_estimate=cost(3),
         name="text",
     )(member.reshape(1).astype(i32), all_weight, *rows_first, *rows_later)
+    text_grad = text_grad.reshape(length, mine, depth)
     pieces, text_grad = pl.pallas_call(
         lambda *refs: None,
         in_specs=[ANY, ANY],
@@ -779,7 +780,7 @@
         cost_estimate=cost(1),
         name="order",
     )(exchange(piece, chips), text_grad)
-    text_grad = text_grad.reshape(length, mine, depth).transpose(1, 0, 2)
+    text_grad = text_grad.transpose(1, 0, 2)
     weight_grad = pl.pallas_call(
         unfold_kernel,
         in_specs=[SMEM, VMEM, VMEM],

time: 252 us -> 247 us (0.980)
  blocking collectives: 15.5 us -> 0 us
  Pallas kernels: 67.8 us -> 81.3 us
  waiting for transfers between devices: 83.4 us -> 72.4 us
  starting transfers between devices: 54 us -> 61.6 us
    all_to_all x1 -> x0, blocking collectives: 15.5 us -> none  [exchange(): lax.all_to_all(x, 'dp', split_axis=0, concat_axis=0, axis_index_groups=gr...]
    pallas_call x2, Pallas kernels: 24.8 us -> 38.2 us  [far_call(): pl.pallas_call(functools.partial(far_kernel, keys, padded, length, many),...]
    all_to_all x5 -> x6, waiting for transfers between devices: 78.6 us -> 67.1 us  [exchange(): lax.all_to_all(x, 'dp', split_axis=0, concat_axis=0, axis_index_groups=gr...]
    all_to_all x5 -> x6, starting transfers between devices: 40.7 us -> 47.7 us  [exchange(): lax.all_to_all(x, 'dp', split_axis=0, concat_axis=0, axis_index_groups=gr...]
    pallas_call x0 -> x1, local copies, waits for them, and re-layouts: none -> 3.38 us  [far_call(): pl.pallas_call(functools.partial(far_kernel, keys, padded, length, many),...]
    unnamed x7 -> x14, local copies, waits for them, and re-layouts: 10.2 us -> 7.49 us
  transfers between devices with their start and end apart: 14 -> 15, of which waited for: 8 -> 10; matrix products, arithmetic and copies ran while one was open for 4% -> 4% of each run, Pallas kernels for 24% -> 30%
where the time goes in v6:
time: 247 us; the launch traced here: 245 us
  Pallas kernels  81.3 us (33%)
  waiting for transfers between devices  72.4 us (29%)
  starting transfers between devices  61.6 us (25%)
  local copies, waits for them, and re-layouts  15.8 us (6%)
  between operations  14.2 us (6%)
    all_to_all x6, waiting for transfers between devices, exchange(): lax.all_to_all(x, 'dp', split_axis=0, concat_axis=0, axis_index_groups=gr...  67.1 us
    all_to_all x6, starting transfers between devices, exchange(): lax.all_to_all(x, 'dp', split_axis=0, concat_axis=0, axis_index_groups=gr...  47.7 us
    pallas_call x2, Pallas kernels, far_call(): pl.pallas_call(functools.partial(far_kernel, keys, padded, length, many),...  38.2 us
    pallas_call x1, Pallas kernels, per_device(): pl.pallas_call(functools.partial(own_kernel, keys, padded, texts_here), g...  15.8 us
    ppermute x6, starting transfers between devices, swap(): lax.ppermute(block, 'mp', [(i, (i + r) % members) for i in range(members)])  9.64 us
    unnamed x14, local copies, waits for them, and re-layouts  7.49 us
    pallas_call x1, Pallas kernels, per_device(): pl.pallas_call(functools.partial(pack_first_kernel, early, images_here),...  5.92 us
  transfers between devices with their start and end apart: 15, of which 10 were waited for; matrix products, arithmetic and copies ran while one was open for 4% of the time, Pallas kernels for 30%

profile of v6, /device:TPU:1, one launch (start us, length us, event | category | flops | bytes accessed | tf_op | source)
XLA Modules:
  0.0 245.3 jit_solution(17150894248966655047)
XLA Ops:
  7.2 1.9 copy-done
  9.1 0.4 constant_dynamic-slice_fusion
  9.5 1.3 copy.16.grad_hbm.grad_ref
  10.8 5.9 %pack_first.1 = (bf16[64,144,128]{2,1,0:T(8,128)(2,1)}, f32[3,560,128]{2,1,0:T(8,128)}, s32[3,16]{1,0:T(4,128)}) custom-call(s32[1]{0:T(128)} %bitcast.2.odd_ref, s32[3,16]{1,0:T(4,128)} %bitcast.34, bf16[560,768]{1,0:T(8,128)(2,1)} %bitcast.31, bf16[192,768]{1,0:T(8,128)(2,1)} %weight_ref.1, bf16[16,4,35,256]{3,2,1,0:T(8,128)(2,1)} %copy.16.grad_hbm.grad_ref), custom_call_target="tpu_custom_call" | custom-call | flops 2875000064 | bytes 18000000 | tf_op jit(solution)/shard_map/pack_first/pallas_call | solution.py:585
  16.8 13.3 %all-to-all-start = ((bf16[64,144,128]{2,1,0:T(8,128)(2,1)}), bf16[64,144,128]{2,1,0:T(8,128)(2,1)}, u32[]{:S(2)}, u32[]{:S(2)}) async-start(bf16[64,144,128]{2,1,0:T(8,128)(2,1)} %get-tuple-element.27), calls=%async_computation | async-start | bytes 4718592 | tf_op jit(solution)/shard_map/all_to_all | solution.py:558
  30.1 2.9 %copy.14.kv_ref = bf16[4,3,577,128]{3,2,1,0:T(8,128)(2,1)} copy(bf16[4,3,577,128]{3,0,2,1:T(4,128)(2,1)} %param.7) | data formatting | bytes 3545088 | tf_op args[2]
  33.0 15.8 %own.1 = (f32[4,3,592,128]{3,2,1,0:T(8,128)}, f32[4,3,256,128]{3,2,1,0:T(8,128)}, bf16[4,3,1184,128]{3,2,1,0:T(8,128)(2,1)}, bf16[4,3,128,592]{3,2,1,0:T(8,128)(2,1)}) custom-call(s32[1]{0:T(128)} %bitcast.2.odd_ref, f32[3,560,128]{2,1,0:T(8,128)} %get-tuple-element.25.query_ref, bf16[16,4,35,256]{3,2,1,0:T(8,128)(2,1)} %copy.16.grad_hbm.grad_ref, ...), custom_call_target="tpu_custom_call" | custom-call | flops 7474999808 | bytes 46800000 | tf_op jit(solution)/shard_map/own/pallas_call | solution.py:608
  48.9 3.6 %pack_later.1 = bf16[64,72,128]{2,1,0:T(8,128)(2,1)} custom-call(s32[1]{0:T(128)} %bitcast.2.odd_ref, s32[3,16]{1,0:T(4,128)} %bitcast.35, s32[3,16]{1,0:T(4,128)} %get-tuple-element.24.rank_ref, f32[3,560,128]{2,1,0:T(8,128)} %get-tuple-element.25.query_ref, bf16[16,4,35,256]{3,2,1,0:T(8,128)(2,1)} %copy.16.grad_hbm.grad_ref, ...), custom_call_target="tpu_custom_call" | custom-call | flops 2300000000 | bytes 14400000 | tf_op jit(solution)/shard_map/pack_later/pallas_call | solution.py:635
  52.5 32.7 %all-to-all-done.wire_hbm.wire_ref = bf16[64,144,128]{2,1,0:T(8,128)(2,1)} async-done(((bf16[64,144,128]{2,1,0:T(8,128)(2,1)}), bf16[64,144,128]{2,1,0:T(8,128)(2,1)}, u32[]{:S(2)}, u32[]{:S(2)}) %all-to-all-start) | async-done | bytes 2359328 | tf_op jit(solution)/shard_map/all_to_all | solution.py:558
  85.2 7.3 %all-to-all-start.1 = ((bf16[64,72,128]{2,1,0:T(8,128)(2,1)}), bf16[64,72,128]{2,1,0:T(8,128)(2,1)}, u32[]{:S(2)}, u32[]{:S(2)}) async-start(bf16[64,72,128]{2,1,0:T(8,128)(2,1)} %pack_later.1), calls=%async_computation.1 | async-start | bytes 2359296 | tf_op jit(solution)/shard_map/all_to_all | solution.py:558
  92.5 1.9 plan.1.plan_ref
  94.4 24.2 %far0.1 = (bf16[4,3,577,128]{3,2,1,0:T(8,128)(2,1)}, bf16[64,72,128]{2,1,0:T(8,128)(2,1)}) custom-call(s32[72,128]{1,0:T(8,128)} %plan.1.plan_ref, bf16[64,144,128]{2,1,0:T(8,128)(2,1)} %all-to-all-done.wire_hbm.wire_ref, bf16[4,3,1184,128]{3,2,1,0:T(8,128)(2,1)} %get-tuple-element.29.both_ref, bf16[4,3,128,592]{3,2,1,0:T(8,128)(2,1)} %get-tuple-element.30.kkt_ref, ...), custom_call_target="tpu_custom_call" | custom-call | flops 12650000384 | bytes 79200000 | tf_op jit(solution)/shard_map/far0/pallas_call | solution.py:526
  118.6 4.4 %all-to-all-done.1.wire_ref = bf16[64,72,128]{2,1,0:T(8,128)(2,1)} async-done(((bf16[64,72,128]{2,1,0:T(8,128)(2,1)}), bf16[64,72,128]{2,1,0:T(8,128)(2,1)}, u32[]{:S(2)}, u32[]{:S(2)}) %all-to-all-start.1) | async-done | bytes 1179680 | tf_op jit(solution)/shard_map/all_to_all | solution.py:558
  123.1 7.5 %all-to-all-start.3 = ((bf16[64,72,128]{2,1,0:T(8,128)(2,1)}), bf16[64,72,128]{2,1,0:T(8,128)(2,1)}, u32[]{:S(2)}, u32[]{:S(2)}) async-start(bf16[64,72,128]{2,1,0:T(8,128)(2,1)} %get-tuple-element.33), calls=%async_computation.3 | async-start | bytes 2359296 | tf_op jit(solution)/shard_map/all_to_all | solution.py:558
  130.6 14.0 %far2.1 = (bf16[4,3,577,128]{3,2,1,0:T(8,128)(2,1)}, bf16[64,40,128]{2,1,0:T(8,128)(2,1)}) custom-call(s32[72,128]{1,0:T(8,128)} %plan.1.plan_ref, bf16[64,72,128]{2,1,0:T(8,128)(2,1)} %all-to-all-done.1.wire_ref, bf16[4,3,1184,128]{3,2,1,0:T(8,128)(2,1)} %get-tuple-element.29.both_ref, ...), custom_call_target="tpu_custom_call", output_to_operand_aliasing={{0}: (5, {})} | custom-call | flops 6899999744 | bytes 43200000 | tf_op jit(solution)/shard_map/far2/pallas_call | solution.py:526
  144.6 16.5 %all-to-all-done.3.back_ref = bf16[64,72,128]{2,1,0:T(8,128)(2,1)} async-done(((bf16[64,72,128]{2,1,0:T(8,128)(2,1)}), bf16[64,72,128]{2,1,0:T(8,128)(2,1)}, u32[]{:S(2)}, u32[]{:S(2)}) %all-to-all-start.3) | async-done | bytes 1179680 | tf_op jit(solution)/shard_map/all_to_all | solution.py:558
  161.1 6.8 %all-to-all-start.2 = ((bf16[64,40,128]{2,1,0:T(8,128)(2,1)}), bf16[64,40,128]{2,1,0:T(8,128)(2,1)}, u32[]{:S(2)}, u32[]{:S(2)}) async-start(bf16[64,40,128]{2,1,0:T(8,128)(2,1)} %get-tuple-element.32), calls=%async_computation.2 | async-start | bytes 1310720 | tf_op jit(solution)/shard_map/all_to_all | solution.py:558
  167.9 0.0 all-gather.2.cloned.1.call-start
  168.0 0.7 all-gather.2.cloned.1.call-update
  168.7 4.2 %gather_two.1 = (bf16[4,140,128]{2,1,0:T(8,128)(2,1)}, f32[128,768]{1,0:T(8,128)}) custom-call(s32[3,16]{1,0:T(4,128)} %bitcast.36, s32[3,16]{1,0:T(4,128)} %get-tuple-element.24.rank_ref, bf16[560,768]{1,0:T(8,128)(2,1)} %bitcast.32, f32[4,3,256,128]{3,2,1,0:T(8,128)} %get-tuple-element.26.own_ref, bf16[64,72,128]{2,1,0:T(8,128)(2,1)} %all-to-all-done.3.back_ref), custom_call_target="tpu_custom_call" | custom-call | flops 2300000000 | bytes 14400000 | tf_op jit(solution)/shard_map/gather_two/pallas_call | solution.py:676
  172.9 1.4 dynamic-slice_bitcast_fusion.1
  174.3 1.2 collective-permute-start
  175.5 2.5 %collective-permute-start.1 = (bf16[140,128]{1,0:T(8,128)(2,1)S(1)}, bf16[140,128]{1,0:T(8,128)(2,1)}, u32[]{:S(2)}, u32[]{:S(2)}) collective-permute-start(bf16[140,128]{1,0:T(8,128)(2,1)S(1)} %get-tuple-element.51), channel_id=1, source_target_pairs={{0,2},{1,3},{2,0},{3,1},{4,6},{5,7},{6,4},{7,5},{8,10},{9,11},{10,... | collective-permute-start | bytes 107528 | tf_op jit(solution)/shard_map/ppermute | solution.py:701
  178.0 1.1 collective-permute-start.2
  179.1 3.4 %copy.18 = bf16[4,3,577,128]{3,0,2,1:T(4,128)(2,1)} copy(bf16[4,3,577,128]{3,2,1,0:T(8,128)(2,1)} %get-tuple-element.36) | data formatting | bytes 3545088 | tf_op jit(solution)/shard_map/far2/pallas_call | solution.py:526
  182.5 5.7 %all-to-all-done.2.back_ref = bf16[64,40,128]{2,1,0:T(8,128)(2,1)} async-done(((bf16[64,40,128]{2,1,0:T(8,128)(2,1)}), bf16[64,40,128]{2,1,0:T(8,128)(2,1)}, u32[]{:S(2)}, u32[]{:S(2)}) %all-to-all-start.2) | async-done | bytes 655392 | tf_op jit(solution)/shard_map/all_to_all | solution.py:558
  188.3 3.7 %gather_last.1 = (bf16[4,140,128]{2,1,0:T(8,128)(2,1)}, f32[24,8,384]{2,1,0:T(8,128)}, bf16[24,8,384]{2,1,0:T(8,128)(2,1)}, bf16[3,577,4,128]{3,2,1,0:T(4,128)(2,1)}) custom-call(s32[1]{0:T(128)} %bitcast.core_ref, s32[3,16]{1,0:T(4,128)} %bitcast.37, s32[3,16]{1,0:T(4,128)} %get-tuple-element.24.rank_ref, ...), custom_call_target="tpu_custom_call", output_to_operand_aliasing={{3}: (10, {})} | custom-call | flops 1724999936 | bytes 10800000 | tf_op jit(solution)/shard_map/gather_last/pallas_call | solution.py:707
  192.0 0.5 collective-permute-start.3
  192.5 1.2 collective-permute-done.3.got_ref
  193.7 0.7 copy-done.2
  194.4 1.7 pair.1
  196.1 5.0 %all-to-all-start.4 = ((bf16[32,8,384]{2,1,0:T(8,128)(2,1)}), bf16[32,8,384]{2,1,0:T(8,128)(2,1)}, u32[]{:S(2)}, u32[]{:S(2)}) async-start(bf16[32,8,384]{2,1,0:T(8,128)(2,1)} %get-tuple-element.40), calls=%async_computation.4 | async-start | bytes 393216 | tf_op jit(solution)/shard_map/all_to_all | solution.py:558
  201.1 1.5 dynamic-slice_bitcast_fusion
  202.5 1.2 collective-permute-start.4
  203.8 2.5 %collective-permute-start.5 = (bf16[140,128]{1,0:T(8,128)(2,1)S(1)}, bf16[140,128]{1,0:T(8,128)(2,1)S(1)}, u32[]{:S(2)}, u32[]{:S(2)}) collective-permute-start(bf16[140,128]{1,0:T(8,128)(2,1)S(1)} %get-tuple-element.47), channel_id=1, source_target_pairs={{0,2},{1,3},{2,0},{3,1},{4,6},{5,7},{6,4},{7,5},{8,10},{9,11},{10,... | collective-permute-start | bytes 107528 | tf_op jit(solution)/shard_map/ppermute | solution.py:701
  206.2 1.1 collective-permute-start.6
  207.4 1.1 collective-permute-done.5.rest_1_.refs_6_
  208.5 1.0 collective-permute-done.6.rest_2_.refs_7_
  209.4 2.2 all-to-all-done.4.parts_ref
  211.7 1.7 total.1
  213.3 7.7 %all-to-all-start.5 = ((bf16[32,8,384]{2,1,0:T(8,128)(2,1)}), bf16[32,8,384]{2,1,0:T(8,128)(2,1)}, u32[]{:S(2)}, u32[]{:S(2)}) async-start(bf16[32,8,384]{2,1,0:T(8,128)(2,1)} %total.1), calls=%async_computation.5 | async-start | bytes 393216 | tf_op jit(solution)/shard_map/all_to_all | solution.py:558
  221.1 2.7 %text.1 = bf16[140,768]{1,0:T(8,128)(2,1)} custom-call(s32[1]{0:T(128)} %bitcast.13.member_ref, bf16[768,768]{1,0:T(8,128)(2,1)} %all-gather.2.cloned.1.call-done.weight_ref, bf16[140,128]{1,0:T(8,128)(2,1)} %get-tuple-element.49.refs_0_, bf16[140,128]{1,0:T(8,128)(2,1)} %collective-permute-done.rest_0_.refs_1_, ...), custom_call_target="tpu_custom_call" | custom-call | flops 1724999936 | bytes 10800000 | tf_op jit(solution)/shard_map/text/pallas_call | solution.py:761
  223.7 1.7 reshape.25.refs_1_
  225.4 5.5 %all-to-all-done.5.refs_0_ = bf16[32,8,384]{2,1,0:T(8,128)(2,1)} async-done(((bf16[32,8,384]{2,1,0:T(8,128)(2,1)}), bf16[32,8,384]{2,1,0:T(8,128)(2,1)}, u32[]{:S(2)}, u32[]{:S(2)}) %all-to-all-start.5) | async-done | bytes 196640 | tf_op jit(solution)/shard_map/all_to_all | solution.py:558
  230.9 3.7 %collective-permute-start.7 = (bf16[32,8,384]{2,1,0:T(8,128)(2,1)}, bf16[32,8,384]{2,1,0:T(8,128)(2,1)S(1)}, u32[]{:S(2)}, u32[]{:S(2)}) collective-permute-start(bf16[32,8,384]{2,1,0:T(8,128)(2,1)} %get-tuple-element.43.mine_ref), channel_id=1, source_target_pairs={{0,4},{4,0},{8,12},{12,8},{16,20},{20,16},{24,28},{28,24},{32,36},... | collective-permute-start | bytes 589832 | tf_op jit(solution)/shard_map/ppermute | solution.py:792
  234.6 1.3 collective-permute-done.7.other_ref
  235.9 0.7 copy-done.1
  236.5 1.9 unfold.1
  (15 shorter events, 0.1 us)
Async XLA Ops:
  7.2 2.0 copy-start
  16.8 68.4 %all-to-all-start = ((bf16[64,144,128]{2,1,0:T(8,128)(2,1)}), bf16[64,144,128]{2,1,0:T(8,128)(2,1)}, u32[]{:S(2)}, u32[]{:S(2)}) async-start(bf16[64,144,128]{2,1,0:T(8,128)(2,1)} %get-tuple-element.27), calls=%async_computation | async-start | bytes 4718592 | tf_op jit(solution)/shard_map/all_to_all | solution.py:558
  85.2 37.9 %all-to-all-start.1 = ((bf16[64,72,128]{2,1,0:T(8,128)(2,1)}), bf16[64,72,128]{2,1,0:T(8,128)(2,1)}, u32[]{:S(2)}, u32[]{:S(2)}) async-start(bf16[64,72,128]{2,1,0:T(8,128)(2,1)} %pack_later.1), calls=%async_computation.1 | async-start | bytes 2359296 | tf_op jit(solution)/shard_map/all_to_all | solution.py:558
  123.1 38.1 %all-to-all-start.3 = ((bf16[64,72,128]{2,1,0:T(8,128)(2,1)}), bf16[64,72,128]{2,1,0:T(8,128)(2,1)}, u32[]{:S(2)}, u32[]{:S(2)}) async-start(bf16[64,72,128]{2,1,0:T(8,128)(2,1)} %get-tuple-element.33), calls=%async_computation.3 | async-start | bytes 2359296 | tf_op jit(solution)/shard_map/all_to_all | solution.py:558
  161.1 27.1 %all-to-all-start.2 = ((bf16[64,40,128]{2,1,0:T(8,128)(2,1)}), bf16[64,40,128]{2,1,0:T(8,128)(2,1)}, u32[]{:S(2)}, u32[]{:S(2)}) async-start(bf16[64,40,128]{2,1,0:T(8,128)(2,1)} %get-tuple-element.32), calls=%async_computation.2 | async-start | bytes 1310720 | tf_op jit(solution)/shard_map/all_to_all | solution.py:558
  167.9 53.1 %all-gather.2.cloned.1.call-start = ((), (), s32[]{:S(2)}) async-start(), calls=%async_computation.6 | async-start | bytes 1474560 | tf_op jit(solution)/shard_map/all_gather | solution.py:580
  174.3 13.9 %collective-permute-start = (bf16[140,128]{1,0:T(8,128)(2,1)S(1)}, bf16[140,128]{1,0:T(8,128)(2,1)}, u32[]{:S(2)}, u32[]{:S(2)}) collective-permute-start(bf16[140,128]{1,0:T(8,128)(2,1)S(1)} %get-tuple-element.52), channel_id=1, source_target_pairs={{0,1},{1,2},{2,3},{3,0},{4,5},{5,6},{6,7},{7,4},{8,9},{9,10},{10,1... | collective-permute-start | bytes 107528 | tf_op jit(solution)/shard_map/ppermute | solution.py:701
  175.5 12.7 %collective-permute-start.1 = (bf16[140,128]{1,0:T(8,128)(2,1)S(1)}, bf16[140,128]{1,0:T(8,128)(2,1)}, u32[]{:S(2)}, u32[]{:S(2)}) collective-permute-start(bf16[140,128]{1,0:T(8,128)(2,1)S(1)} %get-tuple-element.51), channel_id=1, source_target_pairs={{0,2},{1,3},{2,0},{3,1},{4,6},{5,7},{6,4},{7,5},{8,10},{9,11},{10,... | collective-permute-start | bytes 107528 | tf_op jit(solution)/shard_map/ppermute | solution.py:701
  178.0 10.3 %collective-permute-start.2 = (bf16[140,128]{1,0:T(8,128)(2,1)S(1)}, bf16[140,128]{1,0:T(8,128)(2,1)}, u32[]{:S(2)}, u32[]{:S(2)}) collective-permute-start(bf16[140,128]{1,0:T(8,128)(2,1)S(1)} %get-tuple-element.50), channel_id=1, source_target_pairs={{0,3},{1,0},{2,1},{3,2},{4,7},{5,4},{6,5},{7,6},{8,11},{9,8},{10,9... | collective-permute-start | bytes 107528 | tf_op jit(solution)/shard_map/ppermute | solution.py:701
  192.0 1.7 collective-permute-start.3
  193.7 0.7 copy-start.2
  196.1 15.5 %all-to-all-start.4 = ((bf16[32,8,384]{2,1,0:T(8,128)(2,1)}), bf16[32,8,384]{2,1,0:T(8,128)(2,1)}, u32[]{:S(2)}, u32[]{:S(2)}) async-start(bf16[32,8,384]{2,1,0:T(8,128)(2,1)} %get-tuple-element.40), calls=%async_computation.4 | async-start | bytes 393216 | tf_op jit(solution)/shard_map/all_to_all | solution.py:558
  202.5 4.8 %collective-permute-start.4 = (bf16[140,128]{1,0:T(8,128)(2,1)S(1)}, bf16[140,128]{1,0:T(8,128)(2,1)S(1)}, u32[]{:S(2)}, u32[]{:S(2)}) collective-permute-start(bf16[140,128]{1,0:T(8,128)(2,1)S(1)} %get-tuple-element.48), channel_id=1, source_target_pairs={{0,1},{1,2},{2,3},{3,0},{4,5},{5,6},{6,7},{7,4},{8,9},{9,10},{10,1... | collective-permute-start | bytes 107528 | tf_op jit(solution)/shard_map/ppermute | solution.py:701
  203.8 4.7 %collective-permute-start.5 = (bf16[140,128]{1,0:T(8,128)(2,1)S(1)}, bf16[140,128]{1,0:T(8,128)(2,1)S(1)}, u32[]{:S(2)}, u32[]{:S(2)}) collective-permute-start(bf16[140,128]{1,0:T(8,128)(2,1)S(1)} %get-tuple-element.47), channel_id=1, source_target_pairs={{0,2},{1,3},{2,0},{3,1},{4,6},{5,7},{6,4},{7,5},{8,10},{9,11},{10,... | collective-permute-start | bytes 107528 | tf_op jit(solution)/shard_map/ppermute | solution.py:701
  206.2 3.2 %collective-permute-start.6 = (bf16[140,128]{1,0:T(8,128)(2,1)S(1)}, bf16[140,128]{1,0:T(8,128)(2,1)S(1)}, u32[]{:S(2)}, u32[]{:S(2)}) collective-permute-start(bf16[140,128]{1,0:T(8,128)(2,1)S(1)} %get-tuple-element.46), channel_id=1, source_target_pairs={{0,3},{1,0},{2,1},{3,2},{4,7},{5,4},{6,5},{7,6},{8,11},{9,8},{10,9... | collective-permute-start | bytes 107528 | tf_op jit(solution)/shard_map/ppermute | solution.py:701
  207.4 4.3 %copy-start.3 = (bf16[140,128]{1,0:T(8,128)(2,1)}, bf16[140,128]{1,0:T(8,128)(2,1)S(1)}, u32[]{:S(2)}) copy-start(bf16[140,128]{1,0:T(8,128)(2,1)S(1)} %collective-permute-done.4.rest_0_.refs_5_) | copy-start | bytes 107524
  208.5 3.2 %copy-start.4 = (bf16[140,128]{1,0:T(8,128)(2,1)}, bf16[140,128]{1,0:T(8,128)(2,1)S(1)}, u32[]{:S(2)}) copy-start(bf16[140,128]{1,0:T(8,128)(2,1)S(1)} %collective-permute-done.5.rest_1_.refs_6_) | copy-start | bytes 107524
  209.4 2.2 copy-start.5
  213.3 17.6 %all-to-all-start.5 = ((bf16[32,8,384]{2,1,0:T(8,128)(2,1)}), bf16[32,8,384]{2,1,0:T(8,128)(2,1)}, u32[]{:S(2)}, u32[]{:S(2)}) async-start(bf16[32,8,384]{2,1,0:T(8,128)(2,1)} %total.1), calls=%async_computation.5 | async-start | bytes 393216 | tf_op jit(solution)/shard_map/all_to_all | solution.py:558
  230.9 5.0 %collective-permute-start.7 = (bf16[32,8,384]{2,1,0:T(8,128)(2,1)}, bf16[32,8,384]{2,1,0:T(8,128)(2,1)S(1)}, u32[]{:S(2)}, u32[]{:S(2)}) collective-permute-start(bf16[32,8,384]{2,1,0:T(8,128)(2,1)} %get-tuple-element.43.mine_ref), channel_id=1, source_target_pairs={{0,4},{4,0},{8,12},{12,8},{16,20},{20,16},{24,28},{28,24},{32,36},... | collective-permute-start | bytes 589832 | tf_op jit(solution)/shard_map/ppermute | solution.py:792
  235.9 0.7 copy-start.1
Sparse Core Ops, SparseCore 0:
  170.6 26.8 all-gather.1

commit v7 on v6

--- a/solution.py
+++ b/solution.py
@@ -15,6 +15,7 @@
 PARTS = 4
 
 VMEM_LIMIT = 60 * 1024 * 1024
+SMALL_LIMIT = 16 * 1024 * 1024
 
 
 def cdiv(a, b):
@@ -394,22 +395,26 @@
     lax.fori_loop(0, texts_here, one, 0, unroll=2)
 
 
+def by_distance(member, members, mine, r):
+    return pl.ds(lax.rem(member + r, members) * mine, mine)
+
+
+def paired(x0, x1):
+    x = jnp.where(lower_half(x0.shape), x0, pltpu.roll(x1, HEAD_SIZE, 1))
+    return x.astype(jnp.bfloat16)
+
+
 def gather_two_kernel(
-    length, images_here, neg_ref, rank_ref, text_ref, own_ref, back_ref, dq_ref, weight_ref, sum_scr, text_scr
+    length, images_here, member_ref, neg_ref, rank_ref, text_ref, own_ref, back_ref, *rest
 ):
-    per = dq_ref.shape[1] // length
+    dq_refs, (weight_ref, sum_scr, text_scr) = rest[:-3], rest[-3:]
+    mine = dq_refs[0].shape[0]
     sum_requests(
-        2, length, images_here, neg_ref, rank_ref, own_ref, back_ref, sum_scr, text_scr, per
-    )
-    members, mine, _ = dq_ref.shape
-
-    def paired(x0, x1):
-        x = jnp.where(lower_half(x0.shape), x0, pltpu.roll(x1, HEAD_SIZE, 1))
-        return x.astype(jnp.bfloat16)
-
-    for m in range(members):
-        at = slice(m * mine, (m + 1) * mine)
-        dq_ref[m] = paired(text_scr[0, at, :], text_scr[1, at, :])
+        2, length, images_here, neg_ref, rank_ref, own_ref, back_ref, sum_scr, text_scr, mine // length
+    )
+    for r, dq_ref in enumerate(dq_refs):
+        at = by_distance(member_ref[0], len(dq_refs), mine, r)
+        dq_ref[...] = paired(text_scr[0, at, :], text_scr[1, at, :])
     dq = paired(sum_scr[0], sum_scr[1])
     weight_ref[...] = lax.dot_general(
         dq, text_ref[...], (((0,), (0,)), ((), ())), preferred_element_type=jnp.float32
@@ -419,7 +424,7 @@
 def gather_last_kernel(
     length,
     images_here,
-    core_ref,
+    place_ref,
     neg_ref,
     rank_ref,
     text_ref,
@@ -428,14 +433,16 @@
     head_ref,
     *rest,
 ):
-    dq_ref, keep_ref, give_ref, _, sum_scr, text_scr, cut_scr = rest[-7:]
-    per = dq_ref.shape[1] // length
+    keep_ref, give_ref, _, sum_scr, text_scr, cut_scr = rest[-6:]
+    members = len(rest) // 2 - 3
+    dq_refs = rest[-6 - members : -6]
+    mine = dq_refs[0].shape[0]
     sum_requests(
-        1, length, images_here, neg_ref, rank_ref, own_ref, back_ref, sum_scr, text_scr, per
-    )
-    members, mine, _ = dq_ref.shape
-    for m in range(members):
-        dq_ref[m] = text_scr[0, m * mine : (m + 1) * mine, :].astype(jnp.bfloat16)
+        1, length, images_here, neg_ref, rank_ref, own_ref, back_ref, sum_scr, text_scr, mine // length
+    )
+    for r, dq_ref in enumerate(dq_refs):
+        at = by_distance(place_ref[0], members, mine, r)
+        dq_ref[...] = text_scr[0, at, :].astype(jnp.bfloat16)
     dq = sum_scr[0].astype(jnp.bfloat16)
     last = lax.dot_general(
         dq, text_ref[...], (((0,), (0,)), ((), ())), preferred_element_type=jnp.float32
@@ -447,7 +454,7 @@
         rows = head_ref[b * 8 : b * 8 + 8, :] if b < before else last[(b - before) * 8 : (b - before) * 8 + 8]
         for side in range(2):
             cut_scr[2 * b // blocks, 2 * b % blocks + side] = rows[:, side * half : (side + 1) * half]
-    core = core_ref[0]
+    core = place_ref[1]
     keep_ref[...] = cut_scr[core]
     give_ref[...] = cut_scr[1 - core].astype(jnp.bfloat16)
 
@@ -496,8 +503,8 @@
     out_ref[...] = total.astype(jnp.bfloat16)
 
 
-def params():
-    return pltpu.CompilerParams(vmem_limit_bytes=VMEM_LIMIT)
+def params(limit=VMEM_LIMIT):
+    return pltpu.CompilerParams(vmem_limit_bytes=limit)
 
 
 def cost(us):
@@ -671,40 +678,40 @@
     half = depth // 2
     cut = width // 8
     core = lax.rem(lax.axis_index("dp"), 2).reshape(1).astype(i32)
+    place = jnp.concatenate([member.reshape(1).astype(i32), core])
     chips = [list(range(c, owners, 2)) for c in range(2)]
     partner = [(d, d ^ 1) for d in range(owners)]
-    dq_first, weight_first = pl.pallas_call(
+    mine = texts_here // members
+    block = jax.ShapeDtypeStruct((mine * length, LANES), bf16)
+    *dq_first, weight_first = pl.pallas_call(
         functools.partial(gather_two_kernel, length, images_here),
         grid=(1,),
         in_specs=[
             SMEM,
             SMEM,
+            SMEM,
             VMEM,
             pl.BlockSpec((images_here, early, TILE, LANES), lambda n: (0, 0, 0, 0)),
             VMEM,
         ],
-        out_specs=[VMEM, VMEM],
-        out_shape=[
-            jax.ShapeDtypeStruct((members, count // members, LANES), bf16),
-            jax.ShapeDtypeStruct((early * HEAD_SIZE, depth), f32),
-        ],
+        out_specs=[VMEM] * (members + 1),
+        out_shape=[block] * members
+        + [jax.ShapeDtypeStruct((early * HEAD_SIZE, depth), f32)],
         scratch_shapes=[pltpu.VMEM((early, count, LANES), f32)] * 2,
         compiler_params=params(),
         cost_estimate=cost(4),
         name="gather_two",
-    )(neg, rank, flat_text, own_dq, home_first)
+    )(place, neg, rank, flat_text, own_dq, home_first)
     def swap(dq):
-        rows = []
-        for r in range(members):
-            block = lax.dynamic_index_in_dim(dq, lax.rem(member + r, members), 0, False)
-            if r:
-                block = lax.ppermute(block, "mp", [(i, (i + r) % members) for i in range(members)])
-            rows.append(block)
+        rows = [dq[0]]
+        for r in range(1, members):
+            pairs = [(i, (i + r) % members) for i in range(members)]
+            rows.append(lax.ppermute(dq[r], "mp", pairs))
         return rows
 
     rows_first = swap(dq_first)
     dkv = dkv.transpose(1, 2, 0, 3)
-    dq_later, keep, give, dkv = pl.pallas_call(
+    *dq_later, keep, give, dkv = pl.pallas_call(
         functools.partial(gather_last_kernel, length, images_here),
         grid=(1,),
         in_specs=[
@@ -717,35 +724,34 @@
             VMEM,
         ]
         + [ANY] * members,
-        out_specs=[VMEM, VMEM, VMEM, ANY],
-        out_shape=[
-            jax.ShapeDtypeStruct((members, count // members, LANES), bf16),
+        out_specs=[VMEM] * (members + 2) + [ANY],
+        out_shape=[block] * members
+        + [
             jax.ShapeDtypeStruct((cut, 8, half), f32),
             jax.ShapeDtypeStruct((cut, 8, half), bf16),
             jax.ShapeDtypeStruct(dkv.shape, bf16),
         ],
-        input_output_aliases={6 + members: 3},
+        input_output_aliases={6 + members: members + 2},
         scratch_shapes=[pltpu.VMEM((1, count, LANES), f32)] * 2
         + [pltpu.VMEM((2, cut, 8, half), f32)],
         compiler_params=params(),
         cost_estimate=cost(3),
         name="gather_last",
-    )(core, neg, rank, flat_text, own_dq, home_later, weight_first, *rows_first[1:], dkv)
+    )(place, neg, rank, flat_text, own_dq, home_later, weight_first, *rows_first[1:], dkv)
     dkv = dkv.transpose(2, 0, 1, 3)
 
     got = lax.ppermute(give, "dp", partner)
-    later = [dq_later]
-    summed, dq_later = pl.pallas_call(
+    summed, *dq_later = pl.pallas_call(
         pair_kernel,
-        in_specs=[VMEM, VMEM] + [ANY] * len(later),
-        out_specs=[VMEM] + [ANY] * len(later),
+        in_specs=[VMEM, VMEM] + [ANY] * members,
+        out_specs=[VMEM] + [ANY] * members,
         out_shape=[jax.ShapeDtypeStruct((owners // 2, 8, half), bf16)]
-        + [jax.ShapeDtypeStruct(x.shape, x.dtype) for x in later],
-        input_output_aliases={2 + n: 1 + n for n in range(len(later))},
-        compiler_params=params(),
+        + [block] * members,
+        input_output_aliases={2 + n: 1 + n for n in range(members)},
+        compiler_params=params(SMALL_LIMIT),
         cost_estimate=cost(2),
         name="pair",
-    )(keep, got, *later)
+    )(keep, got, *dq_later)
     parts = exchange(summed, chips)
     rows_later = swap(dq_later)
     piece = pl.pallas_call(
@@ -757,7 +763,6 @@
         cost_estimate=cost(2),
         name="total",
     )(parts, *rows_later[1:])
-    mine = texts_here // members
     text_grad = pl.pallas_call(
         functools.partial(text_kernel, width, (early * HEAD_SIZE, (heads - early) * HEAD_SIZE)),
         in_specs=[SMEM] + [VMEM] * (1 + 2 * members),
@@ -786,7 +791,7 @@
         in_specs=[SMEM, VMEM, VMEM],
         out_specs=VMEM,
         out_shape=jax.ShapeDtypeStruct((width, depth), f32),
-        compiler_params=params(),
+        compiler_params=params(SMALL_LIMIT),
         cost_estimate=cost(2),
         name="unfold",
     )(core, pieces, lax.ppermute(pieces, "dp", partner))

time: 247 us -> 252 us (1.020)
  waiting for transfers between devices: 72.4 us -> 81.5 us
  Pallas kernels: 81.3 us -> 72.6 us
  local copies, waits for them, and re-layouts: 15.8 us -> 19.4 us
    all_to_all x6, waiting for transfers between devices: 67.1 us -> 76 us  [exchange(): lax.all_to_all(x, 'dp', split_axis=0, concat_axis=0, axis_index_groups=gr...]
    pallas_call x2, Pallas kernels: 38.2 us -> 31.4 us  [far_call(): pl.pallas_call(functools.partial(far_kernel, keys, padded, length, many),...]
    unnamed x14 -> x36, local copies, waits for them, and re-layouts: 7.49 us -> 13.9 us
    squeeze x2 -> x0, local copies, waits for them, and re-layouts: 2.89 us -> none  [swap(): block = lax.dynamic_index_in_dim(dq, lax.rem(member + r, members), 0, False)]
  transfers between devices with their start and end apart: 15 -> 15, of which waited for: 10 -> 10; matrix products, arithmetic and copies ran while one was open for 4% -> 3% of each run, Pallas kernels for 30% -> 26%
where the time goes in v7:
time: 252 us; the launch traced here: 251 us
  waiting for transfers between devices  81.5 us (32%)
  Pallas kernels  72.6 us (29%)
  starting transfers between devices  62.8 us (25%)
  local copies, waits for them, and re-layouts  19.4 us (8%)
  between operations  14.2 us (6%)
    all_to_all x6, waiting for transfers between devices, exchange(): lax.all_to_all(x, 'dp', split_axis=0, concat_axis=0, axis_index_groups=gr...  76 us
    all_to_all x6, starting transfers between devices, exchange(): lax.all_to_all(x, 'dp', split_axis=0, concat_axis=0, axis_index_groups=gr...  48.7 us
    pallas_call x2, Pallas kernels, far_call(): pl.pallas_call(functools.partial(far_kernel, keys, padded, length, many),...  31.4 us
    pallas_call x1, Pallas kernels, per_device(): pl.pallas_call(functools.partial(own_kernel, keys, padded, texts_here), g...  15.8 us
    unnamed x36, local copies, waits for them, and re-layouts  13.9 us
    ppermute x6, starting transfers between devices, swap(): rows.append(lax.ppermute(dq[r], 'mp', pairs))  9.74 us
    pallas_call x1, Pallas kernels, per_device(): pl.pallas_call(functools.partial(pack_first_kernel, early, images_here),...  5.94 us
  transfers between devices with their start and end apart: 15, of which 10 were waited for; matrix products, arithmetic and copies ran while one was open for 3% of the time, Pallas kernels for 26%

profile of v7, /device:TPU:1, one launch (start us, length us, event | category | flops | bytes accessed | tf_op | source)
XLA Modules:
  0.0 251.1 jit_solution(14403345809395474893)
XLA Ops:
  7.2 1.9 copy-done
  9.5 1.3 copy.19.grad_hbm.grad_ref
  10.8 5.9 %pack_first.1 = (bf16[64,144,128]{2,1,0:T(8,128)(2,1)}, f32[3,560,128]{2,1,0:T(8,128)}, s32[3,16]{1,0:T(4,128)}) custom-call(s32[1]{0:T(128)} %bitcast.3.odd_ref, s32[3,16]{1,0:T(4,128)} %bitcast.18, bf16[560,768]{1,0:T(8,128)(2,1)} %bitcast.15, bf16[192,768]{1,0:T(8,128)(2,1)} %weight_ref.1, bf16[16,4,35,256]{3,2,1,0:T(8,128)(2,1)} %copy.19.grad_hbm.grad_ref), custom_call_target="tpu_custom_call" | custom-call | flops 2875000064 | bytes 18000000 | tf_op jit(solution)/shard_map/pack_first/pallas_call | solution.py:592
  16.8 13.3 %all-to-all-start = ((bf16[64,144,128]{2,1,0:T(8,128)(2,1)}), bf16[64,144,128]{2,1,0:T(8,128)(2,1)}, u32[]{:S(2)}, u32[]{:S(2)}) async-start(bf16[64,144,128]{2,1,0:T(8,128)(2,1)} %get-tuple-element.36), calls=%async_computation | async-start | bytes 4718592 | tf_op jit(solution)/shard_map/all_to_all | solution.py:565
  30.1 3.0 %copy.17.kv_ref = bf16[4,3,577,128]{3,2,1,0:T(8,128)(2,1)} copy(bf16[4,3,577,128]{3,0,2,1:T(4,128)(2,1)} %param.7) | data formatting | bytes 3545088 | tf_op args[2]
  33.1 15.8 %own.1 = (f32[4,3,592,128]{3,2,1,0:T(8,128)}, f32[4,3,256,128]{3,2,1,0:T(8,128)}, bf16[4,3,1184,128]{3,2,1,0:T(8,128)(2,1)}, bf16[4,3,128,592]{3,2,1,0:T(8,128)(2,1)}) custom-call(s32[1]{0:T(128)} %bitcast.3.odd_ref, f32[3,560,128]{2,1,0:T(8,128)} %get-tuple-element.34.query_ref, bf16[16,4,35,256]{3,2,1,0:T(8,128)(2,1)} %copy.19.grad_hbm.grad_ref, ...), custom_call_target="tpu_custom_call" | custom-call | flops 7474999808 | bytes 46800000 | tf_op jit(solution)/shard_map/own/pallas_call | solution.py:615
  48.9 3.5 %pack_later.1 = bf16[64,72,128]{2,1,0:T(8,128)(2,1)} custom-call(s32[1]{0:T(128)} %bitcast.3.odd_ref, s32[3,16]{1,0:T(4,128)} %bitcast.19, s32[3,16]{1,0:T(4,128)} %get-tuple-element.33.rank_ref, f32[3,560,128]{2,1,0:T(8,128)} %get-tuple-element.34.query_ref, bf16[16,4,35,256]{3,2,1,0:T(8,128)(2,1)} %copy.19.grad_hbm.grad_ref, ...), custom_call_target="tpu_custom_call" | custom-call | flops 2300000000 | bytes 14400000 | tf_op jit(solution)/shard_map/pack_later/pallas_call | solution.py:642
  52.4 32.8 %all-to-all-done.wire_hbm.wire_ref = bf16[64,144,128]{2,1,0:T(8,128)(2,1)} async-done(((bf16[64,144,128]{2,1,0:T(8,128)(2,1)}), bf16[64,144,128]{2,1,0:T(8,128)(2,1)}, u32[]{:S(2)}, u32[]{:S(2)}) %all-to-all-start) | async-done | bytes 2359328 | tf_op jit(solution)/shard_map/all_to_all | solution.py:565
  85.2 7.3 %all-to-all-start.1 = ((bf16[64,72,128]{2,1,0:T(8,128)(2,1)}), bf16[64,72,128]{2,1,0:T(8,128)(2,1)}, u32[]{:S(2)}, u32[]{:S(2)}) async-start(bf16[64,72,128]{2,1,0:T(8,128)(2,1)} %pack_later.1), calls=%async_computation.1 | async-start | bytes 2359296 | tf_op jit(solution)/shard_map/all_to_all | solution.py:565
  92.5 1.9 plan.1.plan_ref
  94.4 19.6 %far0.1 = (bf16[4,3,577,128]{3,2,1,0:T(8,128)(2,1)}, bf16[64,72,128]{2,1,0:T(8,128)(2,1)}) custom-call(s32[72,128]{1,0:T(8,128)} %plan.1.plan_ref, bf16[64,144,128]{2,1,0:T(8,128)(2,1)} %all-to-all-done.wire_hbm.wire_ref, bf16[4,3,1184,128]{3,2,1,0:T(8,128)(2,1)} %get-tuple-element.38.both_ref, bf16[4,3,128,592]{3,2,1,0:T(8,128)(2,1)} %get-tuple-element.39.kkt_ref, ...), custom_call_target="tpu_custom_call" | custom-call | flops 12650000384 | bytes 79200000 | tf_op jit(solution)/shard_map/far0/pallas_call | solution.py:533
  114.1 9.0 %all-to-all-done.1.wire_ref = bf16[64,72,128]{2,1,0:T(8,128)(2,1)} async-done(((bf16[64,72,128]{2,1,0:T(8,128)(2,1)}), bf16[64,72,128]{2,1,0:T(8,128)(2,1)}, u32[]{:S(2)}, u32[]{:S(2)}) %all-to-all-start.1) | async-done | bytes 1179680 | tf_op jit(solution)/shard_map/all_to_all | solution.py:565
  123.1 9.7 %all-to-all-start.3 = ((bf16[64,72,128]{2,1,0:T(8,128)(2,1)}), bf16[64,72,128]{2,1,0:T(8,128)(2,1)}, u32[]{:S(2)}, u32[]{:S(2)}) async-start(bf16[64,72,128]{2,1,0:T(8,128)(2,1)} %get-tuple-element.42), calls=%async_computation.3 | async-start | bytes 2359296 | tf_op jit(solution)/shard_map/all_to_all | solution.py:565
  132.8 11.8 %far2.1 = (bf16[4,3,577,128]{3,2,1,0:T(8,128)(2,1)}, bf16[64,40,128]{2,1,0:T(8,128)(2,1)}) custom-call(s32[72,128]{1,0:T(8,128)} %plan.1.plan_ref, bf16[64,72,128]{2,1,0:T(8,128)(2,1)} %all-to-all-done.1.wire_ref, bf16[4,3,1184,128]{3,2,1,0:T(8,128)(2,1)} %get-tuple-element.38.both_ref, ...), custom_call_target="tpu_custom_call", output_to_operand_aliasing={{0}: (5, {})} | custom-call | flops 6899999744 | bytes 43200000 | tf_op jit(solution)/shard_map/far2/pallas_call | solution.py:533
  144.6 18.7 %all-to-all-done.3.back_ref = bf16[64,72,128]{2,1,0:T(8,128)(2,1)} async-done(((bf16[64,72,128]{2,1,0:T(8,128)(2,1)}), bf16[64,72,128]{2,1,0:T(8,128)(2,1)}, u32[]{:S(2)}, u32[]{:S(2)}) %all-to-all-start.3) | async-done | bytes 1179680 | tf_op jit(solution)/shard_map/all_to_all | solution.py:565
  163.3 6.8 %all-to-all-start.2 = ((bf16[64,40,128]{2,1,0:T(8,128)(2,1)}), bf16[64,40,128]{2,1,0:T(8,128)(2,1)}, u32[]{:S(2)}, u32[]{:S(2)}) async-start(bf16[64,40,128]{2,1,0:T(8,128)(2,1)} %get-tuple-element.41), calls=%async_computation.2 | async-start | bytes 1310720 | tf_op jit(solution)/shard_map/all_to_all | solution.py:565
  170.2 0.7 all-gather.2.cloned.1.call-update
  171.5 4.2 %gather_two.1 = (bf16[140,128]{1,0:T(8,128)(2,1)}, bf16[140,128]{1,0:T(8,128)(2,1)}, bf16[140,128]{1,0:T(8,128)(2,1)}, bf16[140,128]{1,0:T(8,128)(2,1)}, f32[128,768]{1,0:T(8,128)}) custom-call(s32[2]{0:T(128)} %pad_add_fusion.member_ref.place_ref, s32[3,16]{1,0:T(4,128)} %bitcast.20, s32[3,16]{1,0:T(4,128)} %get-tuple-element.33.rank_ref, ...), custom_call_target="tpu_custom_call" | custom-call | flops 2300000000 | bytes 14400000 | tf_op jit(solution)/shard_map/gather_two/pallas_call | solution.py:686
  175.7 1.2 collective-permute-start
  176.9 2.5 collective-permute-start.1
  179.3 1.2 collective-permute-start.2
  180.5 3.4 %copy.21 = bf16[4,3,577,128]{3,0,2,1:T(4,128)(2,1)} copy(bf16[4,3,577,128]{3,2,1,0:T(8,128)(2,1)} %get-tuple-element.47) | data formatting | bytes 3545088 | tf_op jit(solution)/shard_map/far2/pallas_call | solution.py:533
  183.9 6.6 %all-to-all-done.2.back_ref = bf16[64,40,128]{2,1,0:T(8,128)(2,1)} async-done(((bf16[64,40,128]{2,1,0:T(8,128)(2,1)}), bf16[64,40,128]{2,1,0:T(8,128)(2,1)}, u32[]{:S(2)}, u32[]{:S(2)}) %all-to-all-start.2) | async-done | bytes 655392 | tf_op jit(solution)/shard_map/all_to_all | solution.py:565
  191.1 3.7 %gather_last.1 = (bf16[140,128]{1,0:T(8,128)(2,1)}, bf16[140,128]{1,0:T(8,128)(2,1)}, bf16[140,128]{1,0:T(8,128)(2,1)}, bf16[140,128]{1,0:T(8,128)(2,1)}, f32[24...) custom-call(s32[2]{0:T(128)} %pad_add_fusion.member_ref.place_ref, ...), custom_call_target="tpu_custom_call", output_to_operand_aliasing={{6}: (10, {})} | custom-call | flops 1724999936 | bytes 10800000 | tf_op jit(solution)/shard_map/gather_last/pallas_call | solution.py:714
  195.4 1.2 collective-permute-done.3.got_ref
  196.6 0.8 copy-done.2
  197.4 0.8 copy-done.4
  198.1 0.8 copy-done.6
  198.9 1.0 copy-done.8
  199.9 0.8 copy-done.9
  200.7 0.7 copy-done.1
  201.3 0.6 copy-done.3
  202.6 0.6 copy-done.7
  203.8 4.9 %all-to-all-start.4 = ((bf16[32,8,384]{2,1,0:T(8,128)(2,1)}), bf16[32,8,384]{2,1,0:T(8,128)(2,1)}, u32[]{:S(2)}, u32[]{:S(2)}) async-start(bf16[32,8,384]{2,1,0:T(8,128)(2,1)} %copy-done.1), calls=%async_computation.4 | async-start | bytes 393216 | tf_op jit(solution)/shard_map/all_to_all | solution.py:565
  208.8 1.3 collective-permute-start.4
  210.1 2.5 collective-permute-start.5
  212.5 1.2 collective-permute-start.6
  213.7 1.1 collective-permute-done.5.rest_1_.refs_6_
  214.8 1.1 collective-permute-done.6.rest_2_.refs_7_
  215.9 3.4 %all-to-all-done.4.parts_ref = bf16[32,8,384]{2,1,0:T(8,128)(2,1)} async-done(((bf16[32,8,384]{2,1,0:T(8,128)(2,1)}), bf16[32,8,384]{2,1,0:T(8,128)(2,1)}, u32[]{:S(2)}, u32[]{:S(2)}) %all-to-all-start.4) | async-done | bytes 196640 | tf_op jit(solution)/shard_map/all_to_all | solution.py:565
  219.3 1.7 total.1
  221.0 6.5 %all-to-all-start.5 = ((bf16[32,8,384]{2,1,0:T(8,128)(2,1)}), bf16[32,8,384]{2,1,0:T(8,128)(2,1)}, u32[]{:S(2)}, u32[]{:S(2)}) async-start(bf16[32,8,384]{2,1,0:T(8,128)(2,1)} %total.1), calls=%async_computation.5 | async-start | bytes 393216 | tf_op jit(solution)/shard_map/all_to_all | solution.py:565
  227.6 2.7 %text.1 = bf16[140,768]{1,0:T(8,128)(2,1)} custom-call(s32[1]{0:T(128)} %bitcast.member_ref, bf16[768,768]{1,0:T(8,128)(2,1)} %all-gather.2.cloned.1.call-done.weight_ref, bf16[140,128]{1,0:T(8,128)(2,1)} %get-tuple-element.58.refs_0_, bf16[140,128]{1,0:T(8,128)(2,1)} %copy-done.11, bf16[140,128]{1,0:T(8,128)(2,1)} %copy-done.12, ...), custom_call_target="tpu_custom_call" | custom-call | flops 1724999936 | bytes 10800000 | tf_op jit(solution)/shard_map/text/pallas_call | solution.py:766
  230.2 1.7 reshape.26.refs_1_
  231.9 5.5 %all-to-all-done.5.refs_0_ = bf16[32,8,384]{2,1,0:T(8,128)(2,1)} async-done(((bf16[32,8,384]{2,1,0:T(8,128)(2,1)}), bf16[32,8,384]{2,1,0:T(8,128)(2,1)}, u32[]{:S(2)}, u32[]{:S(2)}) %all-to-all-start.5) | async-done | bytes 196640 | tf_op jit(solution)/shard_map/all_to_all | solution.py:565
  237.4 3.8 %collective-permute-start.7 = (bf16[32,8,384]{2,1,0:T(8,128)(2,1)}, bf16[32,8,384]{2,1,0:T(8,128)(2,1)S(1)}, u32[]{:S(2)}, u32[]{:S(2)}) collective-permute-start(bf16[32,8,384]{2,1,0:T(8,128)(2,1)} %get-tuple-element.61.mine_ref), channel_id=1, source_target_pairs={{0,4},{4,0},{8,12},{12,8},{16,20},{20,16},{24,28},{28,24},{32,36},... | collective-permute-start | bytes 589832 | tf_op jit(solution)/shard_map/ppermute | solution.py:797
  241.2 1.3 collective-permute-done.7.other_ref
  242.5 1.8 unfold.1
  (36 shorter events, 3.5 us)
Async XLA Ops:
  7.2 2.0 copy-start
  16.8 68.4 %all-to-all-start = ((bf16[64,144,128]{2,1,0:T(8,128)(2,1)}), bf16[64,144,128]{2,1,0:T(8,128)(2,1)}, u32[]{:S(2)}, u32[]{:S(2)}) async-start(bf16[64,144,128]{2,1,0:T(8,128)(2,1)} %get-tuple-element.36), calls=%async_computation | async-start | bytes 4718592 | tf_op jit(solution)/shard_map/all_to_all | solution.py:565
  85.2 37.9 %all-to-all-start.1 = ((bf16[64,72,128]{2,1,0:T(8,128)(2,1)}), bf16[64,72,128]{2,1,0:T(8,128)(2,1)}, u32[]{:S(2)}, u32[]{:S(2)}) async-start(bf16[64,72,128]{2,1,0:T(8,128)(2,1)} %pack_later.1), calls=%async_computation.1 | async-start | bytes 2359296 | tf_op jit(solution)/shard_map/all_to_all | solution.py:565
  123.1 40.3 %all-to-all-start.3 = ((bf16[64,72,128]{2,1,0:T(8,128)(2,1)}), bf16[64,72,128]{2,1,0:T(8,128)(2,1)}, u32[]{:S(2)}, u32[]{:S(2)}) async-start(bf16[64,72,128]{2,1,0:T(8,128)(2,1)} %get-tuple-element.42), calls=%async_computation.3 | async-start | bytes 2359296 | tf_op jit(solution)/shard_map/all_to_all | solution.py:565
  163.3 27.1 %all-to-all-start.2 = ((bf16[64,40,128]{2,1,0:T(8,128)(2,1)}), bf16[64,40,128]{2,1,0:T(8,128)(2,1)}, u32[]{:S(2)}, u32[]{:S(2)}) async-start(bf16[64,40,128]{2,1,0:T(8,128)(2,1)} %get-tuple-element.41), calls=%async_computation.2 | async-start | bytes 1310720 | tf_op jit(solution)/shard_map/all_to_all | solution.py:565
  170.1 57.4 %all-gather.2.cloned.1.call-start = ((), (), s32[]{:S(2)}) async-start(), calls=%async_computation.6 | async-start | bytes 1474560 | tf_op jit(solution)/shard_map/all_gather | solution.py:587
  175.7 14.8 %collective-permute-start = (bf16[140,128]{1,0:T(8,128)(2,1)}, bf16[140,128]{1,0:T(8,128)(2,1)S(1)}, u32[]{:S(2)}, u32[]{:S(2)}) collective-permute-start(bf16[140,128]{1,0:T(8,128)(2,1)} %get-tuple-element.44), channel_id=1, source_target_pairs={{0,1},{1,2},{2,3},{3,0},{4,5},{5,6},{6,7},{7,4},{8,9},{9,10},{10,1... | collective-permute-start | bytes 107528 | tf_op jit(solution)/shard_map/ppermute | solution.py:709
  176.9 13.6 %collective-permute-start.1 = (bf16[140,128]{1,0:T(8,128)(2,1)}, bf16[140,128]{1,0:T(8,128)(2,1)S(1)}, u32[]{:S(2)}, u32[]{:S(2)}) collective-permute-start(bf16[140,128]{1,0:T(8,128)(2,1)} %get-tuple-element.45), channel_id=1, source_target_pairs={{0,2},{1,3},{2,0},{3,1},{4,6},{5,7},{6,4},{7,5},{8,10},{9,11},{10,... | collective-permute-start | bytes 107528 | tf_op jit(solution)/shard_map/ppermute | solution.py:709
  179.3 11.1 %collective-permute-start.2 = (bf16[140,128]{1,0:T(8,128)(2,1)}, bf16[140,128]{1,0:T(8,128)(2,1)S(1)}, u32[]{:S(2)}, u32[]{:S(2)}) collective-permute-start(bf16[140,128]{1,0:T(8,128)(2,1)} %get-tuple-element.46), channel_id=1, source_target_pairs={{0,3},{1,0},{2,1},{3,2},{4,7},{5,4},{6,5},{7,6},{8,11},{9,8},{10,9... | collective-permute-start | bytes 107528 | tf_op jit(solution)/shard_map/ppermute | solution.py:709
  190.4 0.6 copy-start.11
  190.5 0.6 copy-start.12
  190.5 0.6 copy-start.13
  194.8 1.8 collective-permute-start.3
  196.6 0.8 copy-start.2
  197.4 0.8 copy-start.4
  198.1 0.8 copy-start.6
  198.9 1.0 copy-start.8
  199.9 0.8 copy-start.9
  200.7 0.7 copy-start.1
  201.3 0.6 copy-start.3
  202.0 0.6 copy-start.5
  202.6 0.6 copy-start.7
  203.2 0.6 copy-start.10
  203.8 15.5 %all-to-all-start.4 = ((bf16[32,8,384]{2,1,0:T(8,128)(2,1)}), bf16[32,8,384]{2,1,0:T(8,128)(2,1)}, u32[]{:S(2)}, u32[]{:S(2)}) async-start(bf16[32,8,384]{2,1,0:T(8,128)(2,1)} %copy-done.1), calls=%async_computation.4 | async-start | bytes 393216 | tf_op jit(solution)/shard_map/all_to_all | solution.py:565
  208.8 4.9 %collective-permute-start.4 = (bf16[140,128]{1,0:T(8,128)(2,1)}, bf16[140,128]{1,0:T(8,128)(2,1)S(1)}, u32[]{:S(2)}, u32[]{:S(2)}) collective-permute-start(bf16[140,128]{1,0:T(8,128)(2,1)} %copy-done.3), channel_id=1, source_target_pairs={{0,1},{1,2},{2,3},{3,0},{4,5},{5,6},{6,7},{7,4},{8,9},{9,10},{10,1... | collective-permute-start | bytes 107528 | tf_op jit(solution)/shard_map/ppermute | solution.py:709
  210.1 4.7 %collective-permute-start.5 = (bf16[140,128]{1,0:T(8,128)(2,1)}, bf16[140,128]{1,0:T(8,128)(2,1)S(1)}, u32[]{:S(2)}, u32[]{:S(2)}) collective-permute-start(bf16[140,128]{1,0:T(8,128)(2,1)} %copy-done.5), channel_id=1, source_target_pairs={{0,2},{1,3},{2,0},{3,1},{4,6},{5,7},{6,4},{7,5},{8,10},{9,11},{10,... | collective-permute-start | bytes 107528 | tf_op jit(solution)/shard_map/ppermute | solution.py:709
  212.5 3.4 %collective-permute-start.6 = (bf16[140,128]{1,0:T(8,128)(2,1)}, bf16[140,128]{1,0:T(8,128)(2,1)S(1)}, u32[]{:S(2)}, u32[]{:S(2)}) collective-permute-start(bf16[140,128]{1,0:T(8,128)(2,1)} %copy-done.7), channel_id=1, source_target_pairs={{0,3},{1,0},{2,1},{3,2},{4,7},{5,4},{6,5},{7,6},{8,11},{9,8},{10,9... | collective-permute-start | bytes 107528 | tf_op jit(solution)/shard_map/ppermute | solution.py:709
  213.7 5.6 %copy-start.14 = (bf16[140,128]{1,0:T(8,128)(2,1)}, bf16[140,128]{1,0:T(8,128)(2,1)S(1)}, u32[]{:S(2)}) copy-start(bf16[140,128]{1,0:T(8,128)(2,1)S(1)} %collective-permute-done.4.rest_0_.refs_5_) | copy-start | bytes 107524
  214.8 4.5 %copy-start.15 = (bf16[140,128]{1,0:T(8,128)(2,1)}, bf16[140,128]{1,0:T(8,128)(2,1)S(1)}, u32[]{:S(2)}) copy-start(bf16[140,128]{1,0:T(8,128)(2,1)S(1)} %collective-permute-done.5.rest_1_.refs_6_) | copy-start | bytes 107524
  215.9 3.4 %copy-start.16 = (bf16[140,128]{1,0:T(8,128)(2,1)}, bf16[140,128]{1,0:T(8,128)(2,1)S(1)}, u32[]{:S(2)}) copy-start(bf16[140,128]{1,0:T(8,128)(2,1)S(1)} %collective-permute-done.6.rest_2_.refs_7_) | copy-start | bytes 107524
  221.0 16.4 %all-to-all-start.5 = ((bf16[32,8,384]{2,1,0:T(8,128)(2,1)}), bf16[32,8,384]{2,1,0:T(8,128)(2,1)}, u32[]{:S(2)}, u32[]{:S(2)}) async-start(bf16[32,8,384]{2,1,0:T(8,128)(2,1)} %total.1), calls=%async_computation.5 | async-start | bytes 393216 | tf_op jit(solution)/shard_map/all_to_all | solution.py:565
  237.4 5.1 %collective-permute-start.7 = (bf16[32,8,384]{2,1,0:T(8,128)(2,1)}, bf16[32,8,384]{2,1,0:T(8,128)(2,1)S(1)}, u32[]{:S(2)}, u32[]{:S(2)}) collective-permute-start(bf16[32,8,384]{2,1,0:T(8,128)(2,1)} %get-tuple-element.61.mine_ref), channel_id=1, source_target_pairs={{0,4},{4,0},{8,12},{12,8},{16,20},{20,16},{24,28},{28,24},{32,36},... | collective-permute-start | bytes 589832 | tf_op jit(solution)/shard_map/ppermute | solution.py:797
Sparse Core Ops, SparseCore 0:
  172.8 26.8 all-gather.1

commit v8 on v7

--- a/solution.py
+++ b/solution.py
@@ -748,7 +748,7 @@
         out_shape=[jax.ShapeDtypeStruct((owners // 2, 8, half), bf16)]
         + [block] * members,
         input_output_aliases={2 + n: 1 + n for n in range(members)},
-        compiler_params=params(SMALL_LIMIT),
+        compiler_params=params(),
         cost_estimate=cost(2),
         name="pair",
     )(keep, got, *dq_later)

time: 252 us -> 246 us (0.976)
  waiting for transfers between devices: 81.5 us -> 88.1 us
  local copies, waits for them, and re-layouts: 19.4 us -> 12.9 us
  Pallas kernels: 72.6 us -> 67.6 us
  starting transfers between devices: 62.8 us -> 59.7 us
    pallas_call x2, Pallas kernels: 31.4 us -> 24.7 us  [far_call(): pl.pallas_call(functools.partial(far_kernel, keys, padded, length, many),...]
    all_to_all x6, waiting for transfers between devices: 76 us -> 82.7 us  [exchange(): lax.all_to_all(x, 'dp', split_axis=0, concat_axis=0, axis_index_groups=gr...]
    unnamed x36 -> x18, local copies, waits for them, and re-layouts: 13.9 us -> 7.45 us
    all_to_all x6, starting transfers between devices: 48.7 us -> 45.7 us  [exchange(): lax.all_to_all(x, 'dp', split_axis=0, concat_axis=0, axis_index_groups=gr...]
  transfers between devices with their start and end apart: 15 -> 15, of which waited for: 10 -> 10; matrix products, arithmetic and copies ran while one was open for 3% -> 4% of each run, Pallas kernels for 26% -> 25%
where the time goes in v8:
time: 246 us; the launch traced here: 243 us
  waiting for transfers between devices  88.1 us (36%)
  Pallas kernels  67.6 us (27%)
  starting transfers between devices  59.7 us (24%)
  between operations  14.2 us (6%)
  local copies, waits for them, and re-layouts  12.9 us (5%)
    all_to_all x6, waiting for transfers between devices, exchange(): lax.all_to_all(x, 'dp', split_axis=0, concat_axis=0, axis_index_groups=gr...  82.7 us
    all_to_all x6, starting transfers between devices, exchange(): lax.all_to_all(x, 'dp', split_axis=0, concat_axis=0, axis_index_groups=gr...  45.7 us
    pallas_call x2, Pallas kernels, far_call(): pl.pallas_call(functools.partial(far_kernel, keys, padded, length, many),...  24.7 us
    pallas_call x1, Pallas kernels, per_device(): pl.pallas_call(functools.partial(own_kernel, keys, padded, texts_here), g...  15.8 us
    ppermute x6, starting transfers between devices, swap(): rows.append(lax.ppermute(dq[r], 'mp', pairs))  9.73 us
    unnamed x18, local copies, waits for them, and re-layouts  7.45 us
    pallas_call x1, Pallas kernels, per_device(): pl.pallas_call(functools.partial(pack_first_kernel, early, images_here),...  5.91 us
  transfers between devices with their start and end apart: 15, of which 10 were waited for; matrix products, arithmetic and copies ran while one was open for 4% of the time, Pallas kernels for 25%

profile of v8, /device:TPU:1, one launch (start us, length us, event | category | flops | bytes accessed | tf_op | source)
XLA Modules:
  0.0 243.2 jit_solution(9596577041318540435)
XLA Ops:
  7.2 1.9 copy-done
  9.1 0.4 constant_dynamic-slice_fusion
  9.5 1.3 copy.19.grad_hbm.grad_ref
  10.8 5.9 %pack_first.1 = (bf16[64,144,128]{2,1,0:T(8,128)(2,1)}, f32[3,560,128]{2,1,0:T(8,128)}, s32[3,16]{1,0:T(4,128)}) custom-call(s32[1]{0:T(128)} %bitcast.3.odd_ref, s32[3,16]{1,0:T(4,128)} %bitcast.18, bf16[560,768]{1,0:T(8,128)(2,1)} %bitcast.15, bf16[192,768]{1,0:T(8,128)(2,1)} %weight_ref.1, bf16[16,4,35,256]{3,2,1,0:T(8,128)(2,1)} %copy.19.grad_hbm.grad_ref), custom_call_target="tpu_custom_call" | custom-call | flops 2875000064 | bytes 18000000 | tf_op jit(solution)/shard_map/pack_first/pallas_call | solution.py:592
  16.7 13.3 %all-to-all-start = ((bf16[64,144,128]{2,1,0:T(8,128)(2,1)}), bf16[64,144,128]{2,1,0:T(8,128)(2,1)}, u32[]{:S(2)}, u32[]{:S(2)}) async-start(bf16[64,144,128]{2,1,0:T(8,128)(2,1)} %get-tuple-element.36), calls=%async_computation | async-start | bytes 4718592 | tf_op jit(solution)/shard_map/all_to_all | solution.py:565
  30.1 2.9 %copy.17.kv_ref = bf16[4,3,577,128]{3,2,1,0:T(8,128)(2,1)} copy(bf16[4,3,577,128]{3,0,2,1:T(4,128)(2,1)} %param.7) | data formatting | bytes 3545088 | tf_op args[2]
  33.0 15.8 %own.1 = (f32[4,3,592,128]{3,2,1,0:T(8,128)}, f32[4,3,256,128]{3,2,1,0:T(8,128)}, bf16[4,3,1184,128]{3,2,1,0:T(8,128)(2,1)}, bf16[4,3,128,592]{3,2,1,0:T(8,128)(2,1)}) custom-call(s32[1]{0:T(128)} %bitcast.3.odd_ref, f32[3,560,128]{2,1,0:T(8,128)} %get-tuple-element.34.query_ref, bf16[16,4,35,256]{3,2,1,0:T(8,128)(2,1)} %copy.19.grad_hbm.grad_ref, ...), custom_call_target="tpu_custom_call" | custom-call | flops 7474999808 | bytes 46800000 | tf_op jit(solution)/shard_map/own/pallas_call | solution.py:615
  48.9 3.5 %pack_later.1 = bf16[64,72,128]{2,1,0:T(8,128)(2,1)} custom-call(s32[1]{0:T(128)} %bitcast.3.odd_ref, s32[3,16]{1,0:T(4,128)} %bitcast.19, s32[3,16]{1,0:T(4,128)} %get-tuple-element.33.rank_ref, f32[3,560,128]{2,1,0:T(8,128)} %get-tuple-element.34.query_ref, bf16[16,4,35,256]{3,2,1,0:T(8,128)(2,1)} %copy.19.grad_hbm.grad_ref, ...), custom_call_target="tpu_custom_call" | custom-call | flops 2300000000 | bytes 14400000 | tf_op jit(solution)/shard_map/pack_later/pallas_call | solution.py:642
  52.4 32.8 %all-to-all-done.wire_hbm.wire_ref = bf16[64,144,128]{2,1,0:T(8,128)(2,1)} async-done(((bf16[64,144,128]{2,1,0:T(8,128)(2,1)}), bf16[64,144,128]{2,1,0:T(8,128)(2,1)}, u32[]{:S(2)}, u32[]{:S(2)}) %all-to-all-start) | async-done | bytes 2359328 | tf_op jit(solution)/shard_map/all_to_all | solution.py:565
  85.2 7.3 %all-to-all-start.1 = ((bf16[64,72,128]{2,1,0:T(8,128)(2,1)}), bf16[64,72,128]{2,1,0:T(8,128)(2,1)}, u32[]{:S(2)}, u32[]{:S(2)}) async-start(bf16[64,72,128]{2,1,0:T(8,128)(2,1)} %pack_later.1), calls=%async_computation.1 | async-start | bytes 2359296 | tf_op jit(solution)/shard_map/all_to_all | solution.py:565
  92.5 1.9 plan.1.plan_ref
  94.4 15.1 %far0.1 = (bf16[4,3,577,128]{3,2,1,0:T(8,128)(2,1)}, bf16[64,72,128]{2,1,0:T(8,128)(2,1)}) custom-call(s32[72,128]{1,0:T(8,128)} %plan.1.plan_ref, bf16[64,144,128]{2,1,0:T(8,128)(2,1)} %all-to-all-done.wire_hbm.wire_ref, bf16[4,3,1184,128]{3,2,1,0:T(8,128)(2,1)} %get-tuple-element.38.both_ref, bf16[4,3,128,592]{3,2,1,0:T(8,128)(2,1)} %get-tuple-element.39.kkt_ref, ...), custom_call_target="tpu_custom_call" | custom-call | flops 12650000384 | bytes 79200000 | tf_op jit(solution)/shard_map/far0/pallas_call | solution.py:533
  109.5 13.5 %all-to-all-done.1.wire_ref = bf16[64,72,128]{2,1,0:T(8,128)(2,1)} async-done(((bf16[64,72,128]{2,1,0:T(8,128)(2,1)}), bf16[64,72,128]{2,1,0:T(8,128)(2,1)}, u32[]{:S(2)}, u32[]{:S(2)}) %all-to-all-start.1) | async-done | bytes 1179680 | tf_op jit(solution)/shard_map/all_to_all | solution.py:565
  123.0 6.8 %all-to-all-start.3 = ((bf16[64,72,128]{2,1,0:T(8,128)(2,1)}), bf16[64,72,128]{2,1,0:T(8,128)(2,1)}, u32[]{:S(2)}, u32[]{:S(2)}) async-start(bf16[64,72,128]{2,1,0:T(8,128)(2,1)} %get-tuple-element.42), calls=%async_computation.3 | async-start | bytes 2359296 | tf_op jit(solution)/shard_map/all_to_all | solution.py:565
  129.8 9.6 %far2.1 = (bf16[4,3,577,128]{3,2,1,0:T(8,128)(2,1)}, bf16[64,40,128]{2,1,0:T(8,128)(2,1)}) custom-call(s32[72,128]{1,0:T(8,128)} %plan.1.plan_ref, bf16[64,72,128]{2,1,0:T(8,128)(2,1)} %all-to-all-done.1.wire_ref, bf16[4,3,1184,128]{3,2,1,0:T(8,128)(2,1)} %get-tuple-element.38.both_ref, ...), custom_call_target="tpu_custom_call", output_to_operand_aliasing={{0}: (5, {})} | custom-call | flops 6899999744 | bytes 43200000 | tf_op jit(solution)/shard_map/far2/pallas_call | solution.py:533
  139.4 20.9 %all-to-all-done.3.back_ref = bf16[64,72,128]{2,1,0:T(8,128)(2,1)} async-done(((bf16[64,72,128]{2,1,0:T(8,128)(2,1)}), bf16[64,72,128]{2,1,0:T(8,128)(2,1)}, u32[]{:S(2)}, u32[]{:S(2)}) %all-to-all-start.3) | async-done | bytes 1179680 | tf_op jit(solution)/shard_map/all_to_all | solution.py:565
  160.4 6.8 %all-to-all-start.2 = ((bf16[64,40,128]{2,1,0:T(8,128)(2,1)}), bf16[64,40,128]{2,1,0:T(8,128)(2,1)}, u32[]{:S(2)}, u32[]{:S(2)}) async-start(bf16[64,40,128]{2,1,0:T(8,128)(2,1)} %get-tuple-element.41), calls=%async_computation.2 | async-start | bytes 1310720 | tf_op jit(solution)/shard_map/all_to_all | solution.py:565
  167.2 0.0 all-gather.2.cloned.1.call-start
  167.2 0.7 all-gather.2.cloned.1.call-update
  167.9 0.7 pad_add_fusion.member_ref.place_ref
  168.6 4.2 %gather_two.1 = (bf16[140,128]{1,0:T(8,128)(2,1)}, bf16[140,128]{1,0:T(8,128)(2,1)}, bf16[140,128]{1,0:T(8,128)(2,1)}, bf16[140,128]{1,0:T(8,128)(2,1)}, f32[128,768]{1,0:T(8,128)}) custom-call(s32[2]{0:T(128)} %pad_add_fusion.member_ref.place_ref, s32[3,16]{1,0:T(4,128)} %bitcast.20, s32[3,16]{1,0:T(4,128)} %get-tuple-element.33.rank_ref, ...), custom_call_target="tpu_custom_call" | custom-call | flops 2300000000 | bytes 14400000 | tf_op jit(solution)/shard_map/gather_two/pallas_call | solution.py:686
  172.8 1.2 collective-permute-start
  174.0 2.4 %collective-permute-start.1 = (bf16[140,128]{1,0:T(8,128)(2,1)}, bf16[140,128]{1,0:T(8,128)(2,1)S(1)}, u32[]{:S(2)}, u32[]{:S(2)}) collective-permute-start(bf16[140,128]{1,0:T(8,128)(2,1)} %get-tuple-element.45), channel_id=1, source_target_pairs={{0,2},{1,3},{2,0},{3,1},{4,6},{5,7},{6,4},{7,5},{8,10},{9,11},{10,... | collective-permute-start | bytes 107528 | tf_op jit(solution)/shard_map/ppermute | solution.py:709
  176.4 1.2 collective-permute-start.2
  177.6 3.4 %copy.21 = bf16[4,3,577,128]{3,0,2,1:T(4,128)(2,1)} copy(bf16[4,3,577,128]{3,2,1,0:T(8,128)(2,1)} %get-tuple-element.47) | data formatting | bytes 3545088 | tf_op jit(solution)/shard_map/far2/pallas_call | solution.py:533
  181.0 6.5 %all-to-all-done.2.back_ref = bf16[64,40,128]{2,1,0:T(8,128)(2,1)} async-done(((bf16[64,40,128]{2,1,0:T(8,128)(2,1)}), bf16[64,40,128]{2,1,0:T(8,128)(2,1)}, u32[]{:S(2)}, u32[]{:S(2)}) %all-to-all-start.2) | async-done | bytes 655392 | tf_op jit(solution)/shard_map/all_to_all | solution.py:565
  187.5 0.6 copy-done.2
  188.1 0.0 copy-done.4
  188.2 3.7 %gather_last.1 = (bf16[140,128]{1,0:T(8,128)(2,1)}, bf16[140,128]{1,0:T(8,128)(2,1)}, bf16[140,128]{1,0:T(8,128)(2,1)}, bf16[140,128]{1,0:T(8,128)(2,1)}, f32[24...) custom-call(s32[2]{0:T(128)} %pad_add_fusion.member_ref.place_ref, ...), custom_call_target="tpu_custom_call", output_to_operand_aliasing={{6}: (10, {})} | custom-call | flops 1724999936 | bytes 10800000 | tf_op jit(solution)/shard_map/gather_last/pallas_call | solution.py:714
  191.9 0.6 collective-permute-start.3
  192.4 1.2 collective-permute-done.3.got_ref
  193.7 0.7 copy-done.1
  194.3 1.7 pair.1
  196.0 4.9 %all-to-all-start.4 = ((bf16[32,8,384]{2,1,0:T(8,128)(2,1)}), bf16[32,8,384]{2,1,0:T(8,128)(2,1)}, u32[]{:S(2)}, u32[]{:S(2)}) async-start(bf16[32,8,384]{2,1,0:T(8,128)(2,1)} %get-tuple-element.54), calls=%async_computation.4 | async-start | bytes 393216 | tf_op jit(solution)/shard_map/all_to_all | solution.py:565
  201.0 1.3 collective-permute-start.4
  202.3 2.4 %collective-permute-start.5 = (bf16[140,128]{1,0:T(8,128)(2,1)}, bf16[140,128]{1,0:T(8,128)(2,1)S(1)}, u32[]{:S(2)}, u32[]{:S(2)}) collective-permute-start(bf16[140,128]{1,0:T(8,128)(2,1)} %get-tuple-element.56), channel_id=1, source_target_pairs={{0,2},{1,3},{2,0},{3,1},{4,6},{5,7},{6,4},{7,5},{8,10},{9,11},{10,... | collective-permute-start | bytes 107528 | tf_op jit(solution)/shard_map/ppermute | solution.py:709
  204.7 1.1 collective-permute-start.6
  205.9 1.1 collective-permute-done.5.rest_1_.refs_6_
  207.0 1.1 collective-permute-done.6.rest_2_.refs_7_
  208.2 3.4 %all-to-all-done.4.parts_ref = bf16[32,8,384]{2,1,0:T(8,128)(2,1)} async-done(((bf16[32,8,384]{2,1,0:T(8,128)(2,1)}), bf16[32,8,384]{2,1,0:T(8,128)(2,1)}, u32[]{:S(2)}, u32[]{:S(2)}) %all-to-all-start.4) | async-done | bytes 196640 | tf_op jit(solution)/shard_map/all_to_all | solution.py:565
  211.6 1.7 total.1
  213.2 6.5 %all-to-all-start.5 = ((bf16[32,8,384]{2,1,0:T(8,128)(2,1)}), bf16[32,8,384]{2,1,0:T(8,128)(2,1)}, u32[]{:S(2)}, u32[]{:S(2)}) async-start(bf16[32,8,384]{2,1,0:T(8,128)(2,1)} %total.1), calls=%async_computation.5 | async-start | bytes 393216 | tf_op jit(solution)/shard_map/all_to_all | solution.py:565
  219.8 2.7 %text.1 = bf16[140,768]{1,0:T(8,128)(2,1)} custom-call(s32[1]{0:T(128)} %bitcast.member_ref, bf16[768,768]{1,0:T(8,128)(2,1)} %all-gather.2.cloned.1.call-done.weight_ref, bf16[140,128]{1,0:T(8,128)(2,1)} %get-tuple-element.58.refs_0_, bf16[140,128]{1,0:T(8,128)(2,1)} %copy-done.2, bf16[140,128]{1,0:T(8,128)(2,1)} %copy-done.3, bf16[140,128]{1,0:T(8,128)(2,1)} %copy-done.4, ...), custom_call_target="tpu_custom_call" | custom-call | flops 1724999936 | bytes 10800000 | tf_op jit(solution)/shard_map/text/pallas_call | solution.py:766
  222.5 1.7 reshape.26.refs_1_
  224.1 5.5 %all-to-all-done.5.refs_0_ = bf16[32,8,384]{2,1,0:T(8,128)(2,1)} async-done(((bf16[32,8,384]{2,1,0:T(8,128)(2,1)}), bf16[32,8,384]{2,1,0:T(8,128)(2,1)}, u32[]{:S(2)}, u32[]{:S(2)}) %all-to-all-start.5) | async-done | bytes 196640 | tf_op jit(solution)/shard_map/all_to_all | solution.py:565
  229.6 3.7 %collective-permute-start.7 = (bf16[32,8,384]{2,1,0:T(8,128)(2,1)}, bf16[32,8,384]{2,1,0:T(8,128)(2,1)S(1)}, u32[]{:S(2)}, u32[]{:S(2)}) collective-permute-start(bf16[32,8,384]{2,1,0:T(8,128)(2,1)} %get-tuple-element.61.mine_ref), channel_id=1, source_target_pairs={{0,4},{4,0},{8,12},{12,8},{16,20},{20,16},{24,28},{28,24},{32,36},... | collective-permute-start | bytes 589832 | tf_op jit(solution)/shard_map/ppermute | solution.py:797
  233.3 1.3 collective-permute-done.7.other_ref
  234.6 1.8 unfold.1
  (18 shorter events, 0.1 us)
Async XLA Ops:
  7.2 2.0 copy-start
  16.7 68.4 %all-to-all-start = ((bf16[64,144,128]{2,1,0:T(8,128)(2,1)}), bf16[64,144,128]{2,1,0:T(8,128)(2,1)}, u32[]{:S(2)}, u32[]{:S(2)}) async-start(bf16[64,144,128]{2,1,0:T(8,128)(2,1)} %get-tuple-element.36), calls=%async_computation | async-start | bytes 4718592 | tf_op jit(solution)/shard_map/all_to_all | solution.py:565
  85.2 37.9 %all-to-all-start.1 = ((bf16[64,72,128]{2,1,0:T(8,128)(2,1)}), bf16[64,72,128]{2,1,0:T(8,128)(2,1)}, u32[]{:S(2)}, u32[]{:S(2)}) async-start(bf16[64,72,128]{2,1,0:T(8,128)(2,1)} %pack_later.1), calls=%async_computation.1 | async-start | bytes 2359296 | tf_op jit(solution)/shard_map/all_to_all | solution.py:565
  123.0 37.3 %all-to-all-start.3 = ((bf16[64,72,128]{2,1,0:T(8,128)(2,1)}), bf16[64,72,128]{2,1,0:T(8,128)(2,1)}, u32[]{:S(2)}, u32[]{:S(2)}) async-start(bf16[64,72,128]{2,1,0:T(8,128)(2,1)} %get-tuple-element.42), calls=%async_computation.3 | async-start | bytes 2359296 | tf_op jit(solution)/shard_map/all_to_all | solution.py:565
  160.4 27.1 %all-to-all-start.2 = ((bf16[64,40,128]{2,1,0:T(8,128)(2,1)}), bf16[64,40,128]{2,1,0:T(8,128)(2,1)}, u32[]{:S(2)}, u32[]{:S(2)}) async-start(bf16[64,40,128]{2,1,0:T(8,128)(2,1)} %get-tuple-element.41), calls=%async_computation.2 | async-start | bytes 1310720 | tf_op jit(solution)/shard_map/all_to_all | solution.py:565
  167.2 52.6 %all-gather.2.cloned.1.call-start = ((), (), s32[]{:S(2)}) async-start(), calls=%async_computation.6 | async-start | bytes 1474560 | tf_op jit(solution)/shard_map/all_gather | solution.py:587
  172.8 14.7 %collective-permute-start = (bf16[140,128]{1,0:T(8,128)(2,1)}, bf16[140,128]{1,0:T(8,128)(2,1)S(1)}, u32[]{:S(2)}, u32[]{:S(2)}) collective-permute-start(bf16[140,128]{1,0:T(8,128)(2,1)} %get-tuple-element.44), channel_id=1, source_target_pairs={{0,1},{1,2},{2,3},{3,0},{4,5},{5,6},{6,7},{7,4},{8,9},{9,10},{10,1... | collective-permute-start | bytes 107528 | tf_op jit(solution)/shard_map/ppermute | solution.py:709
  174.0 13.5 %collective-permute-start.1 = (bf16[140,128]{1,0:T(8,128)(2,1)}, bf16[140,128]{1,0:T(8,128)(2,1)S(1)}, u32[]{:S(2)}, u32[]{:S(2)}) collective-permute-start(bf16[140,128]{1,0:T(8,128)(2,1)} %get-tuple-element.45), channel_id=1, source_target_pairs={{0,2},{1,3},{2,0},{3,1},{4,6},{5,7},{6,4},{7,5},{8,10},{9,11},{10,... | collective-permute-start | bytes 107528 | tf_op jit(solution)/shard_map/ppermute | solution.py:709
  176.4 11.1 %collective-permute-start.2 = (bf16[140,128]{1,0:T(8,128)(2,1)}, bf16[140,128]{1,0:T(8,128)(2,1)S(1)}, u32[]{:S(2)}, u32[]{:S(2)}) collective-permute-start(bf16[140,128]{1,0:T(8,128)(2,1)} %get-tuple-element.46), channel_id=1, source_target_pairs={{0,3},{1,0},{2,1},{3,2},{4,7},{5,4},{6,5},{7,6},{8,11},{9,8},{10,9... | collective-permute-start | bytes 107528 | tf_op jit(solution)/shard_map/ppermute | solution.py:709
  187.5 0.6 copy-start.2
  187.5 0.6 copy-start.3
  187.5 0.6 copy-start.4
  191.9 1.8 collective-permute-start.3
  193.6 0.7 copy-start.1
  196.0 15.5 %all-to-all-start.4 = ((bf16[32,8,384]{2,1,0:T(8,128)(2,1)}), bf16[32,8,384]{2,1,0:T(8,128)(2,1)}, u32[]{:S(2)}, u32[]{:S(2)}) async-start(bf16[32,8,384]{2,1,0:T(8,128)(2,1)} %get-tuple-element.54), calls=%async_computation.4 | async-start | bytes 393216 | tf_op jit(solution)/shard_map/all_to_all | solution.py:565
  201.0 4.9 %collective-permute-start.4 = (bf16[140,128]{1,0:T(8,128)(2,1)}, bf16[140,128]{1,0:T(8,128)(2,1)S(1)}, u32[]{:S(2)}, u32[]{:S(2)}) collective-permute-start(bf16[140,128]{1,0:T(8,128)(2,1)} %get-tuple-element.55), channel_id=1, source_target_pairs={{0,1},{1,2},{2,3},{3,0},{4,5},{5,6},{6,7},{7,4},{8,9},{9,10},{10,1... | collective-permute-start | bytes 107528 | tf_op jit(solution)/shard_map/ppermute | solution.py:709
  202.3 4.7 %collective-permute-start.5 = (bf16[140,128]{1,0:T(8,128)(2,1)}, bf16[140,128]{1,0:T(8,128)(2,1)S(1)}, u32[]{:S(2)}, u32[]{:S(2)}) collective-permute-start(bf16[140,128]{1,0:T(8,128)(2,1)} %get-tuple-element.56), channel_id=1, source_target_pairs={{0,2},{1,3},{2,0},{3,1},{4,6},{5,7},{6,4},{7,5},{8,10},{9,11},{10,... | collective-permute-start | bytes 107528 | tf_op jit(solution)/shard_map/ppermute | solution.py:709
  204.7 3.4 %collective-permute-start.6 = (bf16[140,128]{1,0:T(8,128)(2,1)}, bf16[140,128]{1,0:T(8,128)(2,1)S(1)}, u32[]{:S(2)}, u32[]{:S(2)}) collective-permute-start(bf16[140,128]{1,0:T(8,128)(2,1)} %get-tuple-element.57), channel_id=1, source_target_pairs={{0,3},{1,0},{2,1},{3,2},{4,7},{5,4},{6,5},{7,6},{8,11},{9,8},{10,9... | collective-permute-start | bytes 107528 | tf_op jit(solution)/shard_map/ppermute | solution.py:709
  205.9 5.7 %copy-start.5 = (bf16[140,128]{1,0:T(8,128)(2,1)}, bf16[140,128]{1,0:T(8,128)(2,1)S(1)}, u32[]{:S(2)}) copy-start(bf16[140,128]{1,0:T(8,128)(2,1)S(1)} %collective-permute-done.4.rest_0_.refs_5_) | copy-start | bytes 107524
  207.0 4.5 %copy-start.6 = (bf16[140,128]{1,0:T(8,128)(2,1)}, bf16[140,128]{1,0:T(8,128)(2,1)S(1)}, u32[]{:S(2)}) copy-start(bf16[140,128]{1,0:T(8,128)(2,1)S(1)} %collective-permute-done.5.rest_1_.refs_6_) | copy-start | bytes 107524
  208.2 3.4 %copy-start.7 = (bf16[140,128]{1,0:T(8,128)(2,1)}, bf16[140,128]{1,0:T(8,128)(2,1)S(1)}, u32[]{:S(2)}) copy-start(bf16[140,128]{1,0:T(8,128)(2,1)S(1)} %collective-permute-done.6.rest_2_.refs_7_) | copy-start | bytes 107524
  213.2 16.4 %all-to-all-start.5 = ((bf16[32,8,384]{2,1,0:T(8,128)(2,1)}), bf16[32,8,384]{2,1,0:T(8,128)(2,1)}, u32[]{:S(2)}, u32[]{:S(2)}) async-start(bf16[32,8,384]{2,1,0:T(8,128)(2,1)} %total.1), calls=%async_computation.5 | async-start | bytes 393216 | tf_op jit(solution)/shard_map/all_to_all | solution.py:565
  229.6 5.0 %collective-permute-start.7 = (bf16[32,8,384]{2,1,0:T(8,128)(2,1)}, bf16[32,8,384]{2,1,0:T(8,128)(2,1)S(1)}, u32[]{:S(2)}, u32[]{:S(2)}) collective-permute-start(bf16[32,8,384]{2,1,0:T(8,128)(2,1)} %get-tuple-element.61.mine_ref), channel_id=1, source_target_pairs={{0,4},{4,0},{8,12},{12,8},{16,20},{20,16},{24,28},{28,24},{32,36},... | collective-permute-start | bytes 589832 | tf_op jit(solution)/shard_map/ppermute | solution.py:797
Sparse Core Ops, SparseCore 0:
  169.8 26.8 all-gather.1
